TPU v7x, 32 devices: a whole 2x2x4 slice. The times are simulated.
32 devices in a mesh: dp: 4 (over z), mp: 8 (over y, x, core).
Axes of the slice: x: 2, y: 2, z: 4, core: 2. Of those that a mesh axis runs over, the one named last changes fastest.
Arguments:
- hidden_in: bfloat16 [8, 2048, 2048], P('dp', 'mp'), may hold values from -6 to 6
- doc_ids: int32 [8, 2048], P('dp'), may hold values from 0 to 2, never falling along the last dimension, each value on 1 to 1920 neighbouring positions
- tile_slot: int32 [44], replicated, may hold values from 0 to 47, as said below
- attention_gain: float32 [2048], replicated, may hold values from 0.1 to 1.9
- query_gain: float32 [64], replicated, may hold values from 0.1 to 1.9
- key_gain: float32 [64], replicated, may hold values from 0.1 to 1.9
- attend_weight: bfloat16 [2048, 1920], P('mp'), may hold values from -0.125 to 0.125
- output_weight: bfloat16 [1280, 2048], P('mp'), may hold values from -1 to 1
- feed_gain: float32 [2048], replicated, may hold values from 0.1 to 1.9
- gate_up_slots: bfloat16 [48, 2048, 256], P('mp'), may hold values from -0.125 to 0.125
- down_slots: bfloat16 [48, 128, 2048], P('mp'), may hold values from -0.15625 to 0.15625
- out_grad: float32 [8, 2048, 2048], P('dp', 'mp'), may hold values from -6 to 6
Outputs:
- layer_out: float32 [8, 2048, 2048], P('dp', 'mp')
- input_grad: float32 [8, 2048, 2048], P('dp', 'mp')
- grad_attend: float32 [2048, 1920], P('mp')
- grad_output: float32 [1280, 2048], P('mp')
- grad_gate_up: float32 [48, 2048, 256], P('mp')
- grad_down: float32 [48, 128, 2048], P('mp')
- grad_attention_gain: float32 [2048], replicated
- grad_query_gain: float32 [64], replicated
- grad_key_gain: float32 [64], replicated
- grad_feed_gain: float32 [2048], replicated
Inputs may be any that keep to these rules, and one draw needn't show every extreme that they name: tile_slot holds 44 distinct slots; slot c * 6 + k lies on mp device c; the 4 unused slots are each the last slot of a different device, never of the last device.
All inputs are finite; a program needn't handle non-finite values.
Results may differ from a plain program's by a relative error of at most 0.022.
Values may be sent and summed in bfloat16 or wider, within the bound.
A program may use at most 512 MiB of HBM per device.

v0:
```python
import jax
import jax.numpy as jnp
from jax import lax
from jax.sharding import PartitionSpec as P

H = 20
KVH = 5
HD = 64
TILE = 128


EPSILON = 1e-06


def doc_positions(docs):
    index = jnp.arange(docs.shape[-1], dtype=jnp.int32)
    change = jnp.concatenate(
        [jnp.ones(docs.shape[:-1] + (1,), dtype=jnp.bool_), docs[..., 1:] != docs[..., :-1]],
        axis=-1,
    )
    starts = lax.cummax(jnp.where(change, index, 0), axis=docs.ndim - 1)
    return index - starts


def rotary_tables(positions, head_dim):
    half_dim = head_dim // 2
    freqs = 1.0 / 10000.0 ** (jnp.arange(half_dim, dtype=jnp.float32) * 2.0 / head_dim)
    angles = positions.astype(jnp.float32)[..., None] * freqs
    cosine = jnp.cos(angles)
    sine = jnp.sin(angles)
    return (jnp.concatenate([cosine, cosine], -1), jnp.concatenate([sine, sine], -1))


def rotate(values, cosine, sine):
    half_dim = values.shape[-1] // 2
    turned = jnp.concatenate([-values[..., half_dim:], values[..., :half_dim]], -1)
    return values * cosine + turned * sine


def unrotate(grads, cosine, sine):
    half_dim = grads.shape[-1] // 2
    scaled = grads * sine
    turned = jnp.concatenate([scaled[..., half_dim:], -scaled[..., :half_dim]], -1)
    return grads * cosine + turned


def rms_forward(values, gain):
    scale = lax.rsqrt(jnp.mean(values * values, axis=-1, keepdims=True) + EPSILON)
    return (values * scale * gain, scale)


def rms_backward(values, scale, gain, grads):
    weighted = grads * gain
    inner = jnp.mean(weighted * values, axis=-1, keepdims=True)
    backed = scale * (weighted - values * scale * scale * inner)
    return (backed, grads * values * scale)


def shards(
    hidden_in,
    doc_ids,
    tile_slot,
    attention_gain,
    query_gain,
    key_gain,
    attend_weight,
    output_weight,
    feed_gain,
    gate_up_slots,
    down_slots,
    out_grad,
):
    row_count, local_len, model_width = hidden_in.shape
    sequence_len = doc_ids.shape[1]
    slot_count = gate_up_slots.shape[0]
    groups = H // KVH
    query_width = H * HD
    key_width = KVH * HD
    scale_dot = HD ** (-0.5)
    tokens = row_count * local_len
    everything = row_count * sequence_len
    mp_rank = lax.axis_index("mp")
    offset = mp_rank * local_len
    local_pos = lax.dynamic_slice_in_dim(doc_positions(doc_ids), offset, local_len, 1)
    query_docs = lax.dynamic_slice_in_dim(doc_ids, offset, local_len, 1)
    query_index = offset + jnp.arange(local_len, dtype=jnp.int32)
    key_index = jnp.arange(sequence_len, dtype=jnp.int32)
    allowed = (key_index[None, None, :] <= query_index[None, :, None]) & (
        query_docs[:, :, None] == doc_ids[:, None, :]
    )
    allowed = allowed[:, None, None, :, :]
    cosine, sine = rotary_tables(local_pos, HD)
    cosine = cosine[:, :, None, :]
    sine = sine[:, :, None, :]
    x_value = hidden_in.astype(jnp.float32)
    normed_a, scale_a = rms_forward(x_value, attention_gain)
    normed_ab = normed_a.astype(jnp.bfloat16).reshape(tokens, model_width)
    attend_full, output_full = (
        lax.all_gather(attend_weight, "mp", axis=0, tiled=True),
        lax.all_gather(output_weight, "mp", axis=0, tiled=True),
    )
    joined = jnp.dot(normed_ab, attend_full, preferred_element_type=jnp.float32).reshape(
        row_count, local_len, -1
    )
    query_raw = joined[..., :query_width].reshape(row_count, local_len, H, HD)
    key_raw = joined[..., query_width : query_width + key_width].reshape(
        row_count, local_len, KVH, HD
    )
    value_raw = joined[..., query_width + key_width :]
    query_norm, query_scale = rms_forward(query_raw, query_gain)
    key_norm, key_scale = rms_forward(key_raw, key_gain)
    queries = (
        rotate(query_norm, cosine, sine)
        .astype(jnp.bfloat16)
        .reshape(row_count, local_len, KVH, groups, HD)
    )
    keys_local = (
        rotate(key_norm, cosine, sine).astype(jnp.bfloat16).reshape(row_count, local_len, key_width)
    )
    values_local = value_raw.astype(jnp.bfloat16)
    keys_all, values_all = (
        lax.all_gather(keys_local, "mp", axis=1, tiled=True),
        lax.all_gather(values_local, "mp", axis=1, tiled=True),
    )
    keys_all = keys_all.reshape(row_count, sequence_len, KVH, HD)
    values_all = values_all.reshape(row_count, sequence_len, KVH, HD)

    def masked_scores():
        product = (
            jnp.einsum("rqkgd,rskd->rkgqs", queries, keys_all, preferred_element_type=jnp.float32)
            * scale_dot
        )
        return jnp.where(allowed, product, -1e30)

    scores = masked_scores()
    highest_score = jnp.max(scores, axis=-1, keepdims=True)
    exponent = jnp.exp(scores - highest_score)
    row_total = jnp.sum(exponent, axis=-1, keepdims=True)
    log_total = highest_score + jnp.log(row_total)
    probs_b = (exponent / row_total).astype(jnp.bfloat16)
    context = jnp.einsum(
        "rkgqs,rskd->rqkgd", probs_b, values_all, preferred_element_type=jnp.float32
    )
    context_b = context.astype(jnp.bfloat16).reshape(tokens, query_width)
    attention_out = jnp.dot(context_b, output_full, preferred_element_type=jnp.float32).reshape(
        row_count, local_len, model_width
    )
    middle = x_value + attention_out
    normed_f, scale_f = rms_forward(middle, feed_gain)
    normed_fb = normed_f.astype(jnp.bfloat16)
    slot_index = mp_rank * slot_count + jnp.arange(slot_count, dtype=jnp.int32)
    live_slot = jnp.any(tile_slot[None, :] == slot_index[:, None], axis=1).astype(jnp.float32)[
        :, None, None
    ]

    def feed_forward(gathered):
        flat_rows = gathered.reshape(everything, model_width)
        combined = jnp.einsum(
            "nd,cdf->cnf", flat_rows, gate_up_slots, preferred_element_type=jnp.float32
        )
        gate_part = combined[..., :TILE]
        upper_part = combined[..., TILE:]
        return (flat_rows, gate_part, upper_part, jax.nn.sigmoid(gate_part))

    gathered_f = lax.all_gather(normed_fb, "mp", axis=1, tiled=True)
    flat_f, gate_f, upper_f, sigmoid_f = feed_forward(gathered_f)
    hidden_b = (gate_f * sigmoid_f * upper_f * live_slot).astype(jnp.bfloat16)
    partial_out = jnp.einsum(
        "cnf,cfd->nd", hidden_b, down_slots, preferred_element_type=jnp.float32
    )
    ffn_out = lax.psum_scatter(
        partial_out.reshape(row_count, sequence_len, model_width).astype(jnp.bfloat16),
        "mp",
        scatter_dimension=1,
        tiled=True,
    ).astype(jnp.float32)
    layer_out = middle + ffn_out
    grad_branch = out_grad.astype(jnp.bfloat16)
    grad_full = lax.all_gather(grad_branch, "mp", axis=1, tiled=True).reshape(
        everything, model_width
    )
    again_f = lax.all_gather(normed_fb, "mp", axis=1, tiled=True)
    attend_back, output_back = (
        lax.all_gather(attend_weight, "mp", axis=0, tiled=True),
        lax.all_gather(output_weight, "mp", axis=0, tiled=True),
    )
    flat_b, gate_b, upper_b, sigmoid_b = feed_forward(again_f)
    silu_b = gate_b * sigmoid_b
    hidden_again = (silu_b * upper_b * live_slot).astype(jnp.bfloat16)
    grad_down = jnp.einsum(
        "cnf,nd->cfd", hidden_again, grad_full, preferred_element_type=jnp.float32
    )
    grad_hidden = (
        jnp.einsum("nd,cfd->cnf", grad_full, down_slots, preferred_element_type=jnp.float32)
        * live_slot
    )
    grad_gate = grad_hidden * upper_b * sigmoid_b * (1.0 + gate_b * (1.0 - sigmoid_b))
    grad_upper = grad_hidden * silu_b
    grad_both = jnp.concatenate([grad_gate, grad_upper], axis=-1).astype(jnp.bfloat16)
    grad_gate_up = jnp.einsum("nd,cnf->cdf", flat_b, grad_both, preferred_element_type=jnp.float32)
    grad_flat = jnp.einsum(
        "cnf,cdf->nd", grad_both, gate_up_slots, preferred_element_type=jnp.float32
    )
    grad_normed_f = lax.psum_scatter(
        grad_flat.reshape(row_count, sequence_len, model_width),
        "mp",
        scatter_dimension=1,
        tiled=True,
    )
    back_f, gain_part_f = rms_backward(middle, scale_f, feed_gain, grad_normed_f)
    grad_middle = out_grad + back_f
    grad_attn_b = grad_middle.astype(jnp.bfloat16).reshape(tokens, model_width)
    grad_output = jnp.einsum(
        "nh,nd->hd", context_b, grad_attn_b, preferred_element_type=jnp.float32
    )
    grad_context = jnp.einsum(
        "nd,hd->nh", grad_attn_b, output_back, preferred_element_type=jnp.float32
    )
    grad_context_b = grad_context.astype(jnp.bfloat16).reshape(
        row_count, local_len, KVH, groups, HD
    )
    probs_again = jnp.exp(masked_scores() - log_total)
    grad_probs = jnp.einsum(
        "rqkgd,rskd->rkgqs", grad_context_b, values_all, preferred_element_type=jnp.float32
    )
    inner_sum = jnp.sum(grad_probs * probs_again, axis=-1, keepdims=True)
    grad_scores_b = (probs_again * (grad_probs - inner_sum)).astype(jnp.bfloat16)
    grad_queries = (
        jnp.einsum("rkgqs,rskd->rqkgd", grad_scores_b, keys_all, preferred_element_type=jnp.float32)
        * scale_dot
    )
    grad_keys = (
        jnp.einsum("rkgqs,rqkgd->rskd", grad_scores_b, queries, preferred_element_type=jnp.float32)
        * scale_dot
    )
    grad_values = jnp.einsum(
        "rkgqs,rqkgd->rskd",
        probs_again.astype(jnp.bfloat16),
        grad_context_b,
        preferred_element_type=jnp.float32,
    )
    grad_keys_local, grad_values_local = (
        lax.psum_scatter(
            grad_keys.reshape(row_count, sequence_len, key_width).astype(jnp.bfloat16),
            "mp",
            scatter_dimension=1,
            tiled=True,
        ).astype(jnp.float32),
        lax.psum_scatter(
            grad_values.reshape(row_count, sequence_len, key_width).astype(jnp.bfloat16),
            "mp",
            scatter_dimension=1,
            tiled=True,
        ).astype(jnp.float32),
    )
    grad_query_norm = unrotate(grad_queries.reshape(row_count, local_len, H, HD), cosine, sine)
    back_q, gain_part_q = rms_backward(query_raw, query_scale, query_gain, grad_query_norm)
    grad_key_norm = unrotate(grad_keys_local.reshape(row_count, local_len, KVH, HD), cosine, sine)
    back_k, gain_part_k = rms_backward(key_raw, key_scale, key_gain, grad_key_norm)
    grad_joined = jnp.concatenate(
        [
            back_q.reshape(row_count, local_len, query_width),
            back_k.reshape(row_count, local_len, key_width),
            grad_values_local,
        ],
        axis=-1,
    )
    grad_joined_b = grad_joined.astype(jnp.bfloat16).reshape(tokens, -1)
    grad_attend = jnp.einsum(
        "nd,nf->df", normed_ab, grad_joined_b, preferred_element_type=jnp.float32
    )
    grad_normed_a = jnp.einsum(
        "nf,df->nd", grad_joined_b, attend_back, preferred_element_type=jnp.float32
    )
    back_a, gain_part_a = rms_backward(
        x_value, scale_a, attention_gain, grad_normed_a.reshape(row_count, local_len, model_width)
    )
    input_grad = grad_middle + back_a
    attend_share, output_share = (
        lax.psum_scatter(
            grad_attend.astype(jnp.bfloat16), "mp", scatter_dimension=0, tiled=True
        ).astype(jnp.float32),
        lax.psum_scatter(
            grad_output.astype(jnp.bfloat16), "mp", scatter_dimension=0, tiled=True
        ).astype(jnp.float32),
    )
    attend_total, output_total, gate_up_total, down_total = (
        lax.psum(attend_share.astype(jnp.bfloat16), "dp").astype(jnp.float32),
        lax.psum(output_share.astype(jnp.bfloat16), "dp").astype(jnp.float32),
        lax.psum(grad_gate_up.astype(jnp.bfloat16), "dp").astype(jnp.float32),
        lax.psum(grad_down.astype(jnp.bfloat16), "dp").astype(jnp.float32),
    )
    gain_attention, gain_query, gain_key, gain_feed = lax.psum(
        (
            jnp.sum(gain_part_a, axis=(0, 1)),
            jnp.sum(gain_part_q, axis=(0, 1, 2)),
            jnp.sum(gain_part_k, axis=(0, 1, 2)),
            jnp.sum(gain_part_f, axis=(0, 1)),
        ),
        ("dp", "mp"),
    )
    return (
        layer_out,
        input_grad,
        attend_total,
        output_total,
        gate_up_total,
        down_total,
        gain_attention,
        gain_query,
        gain_key,
        gain_feed,
    )


def solution(mesh):
    placed = (
        P("dp", "mp", None),
        P("dp", None),
        P(),
        P(),
        P(),
        P(),
        P("mp", None),
        P("mp", None),
        P(),
        P("mp", None, None),
        P("mp", None, None),
        P("dp", "mp", None),
    )
    return jax.shard_map(
        shards,
        mesh=mesh,
        in_specs=placed,
        out_specs=(
            P("dp", "mp", None),
            P("dp", "mp", None),
            P("mp", None),
            P("mp", None),
            P("mp", None, None),
            P("mp", None, None),
            P(),
            P(),
            P(),
            P(),
        ),
        check_vma=False,
    )
```

profile of v0, /device:TPU:0, one launch (start us, length us, event | category | flops | bytes accessed | tf_op | source)
XLA Modules:
  0.0 1593.2 jit_solution(8462800758156782099)
XLA Ops:
  13.5 51.3 %all-gather.7.cloned.1.call-done = bf16[2048,1920]{1,0:T(8,128)(2,1)} async-done(((bf16[256,1920]{1,0:T(8,128)(2,1)}), bf16[2048,1920]{1,0:T(8,128)(2,1)}) %all-gather.7.cloned.1.call-update) | async-done | bytes 7864336 | tf_op jit(solution)/shard_map/all_gather | solution.py:99
  64.8 7.7 fusion.18
  98.7 13.1 all-gather.11.cloned.1.call-done
  111.8 32.4 %fusion.61 = (f32[2,5,4,256]{3,2,1,0:T(4,128)S(1)}, f32[2,5,4,256,2048]{3,4,2,1,0:T(8,128)}) fusion(bf16[2,2048,5,64,1]{1,3,4,2,0:T(8,128)(2,1)} %bitcast.187, bf16[2,256,5,4,64]{1,4,3,2,0:T(8,128)(2,1)} %fusion.43, pred[2,256,2048]{1,2,0:T(8,128)(4,1)} %compare_and_fusion), kind=kOutput, calls=%fused_computation.138 | convolution fusion | flops 2747258880 | bytes 88907776 | tf_op jit(solution)/shard_map/rqkgd,rskd->rkgqs/dot_general | solution.py:130
  144.2 26.5 %fusion.3 = f32[2,5,4,256]{3,2,1,0:T(4,128)S(1)} fusion(f32[2,5,4,256,2048]{3,4,2,1,0:T(8,128)} %get-tuple-element.99, f32[2,5,4,256]{3,2,1,0:T(4,128)S(1)} %get-tuple-element.98), kind=kLoop, calls=%fused_computation.9 | loop fusion | flops 41932800 | bytes 83968000 | tf_op jit(solution)/shard_map/reduce_sum | solution.py:138
  175.6 31.4 %fusion.44 = bf16[2,5,64,4,256]{4,2,3,1,0:T(8,128)(2,1)} fusion(bf16[2,2048,5,64,1]{1,3,4,2,0:T(8,128)(2,1)} %bitcast.194, f32[2,5,4,256,2048]{3,4,2,1,0:T(8,128)} %get-tuple-element.99, f32[2,5,4,256]{3,2,1,0:T(4,128)S(1)} %fusion.3, f32[2,5,4,256]{3,2,1,0:T(4,128)S(1)} %get-tuple-element.98), kind=kOutput, calls=%fused_computation.81 | convolution fusion | flops 2747924480 | bytes 87900160 | tf_op jit(solution)/shard_map/rkgqs,rskd->rqkgd/dot_general | solution.py:141
  207.0 6.8 multiply_reduce_fusion.2
  221.7 85.8 %all-gather.15.cloned.1.call-done = bf16[2,2048,2048]{2,1,0:T(8,128)(2,1)} async-done(((bf16[2,256,2048]{2,1,0:T(8,128)(2,1)}), bf16[2,2048,2048]{2,1,0:T(8,128)(2,1)}) %all-gather.15.cloned.1.call-update) | async-done | bytes 16777232 | tf_op jit(solution)/shard_map/all_gather | solution.py:165
  307.6 33.9 %convolution_bitcast_fusion = f32[6,4096,256]{1,2,0:T(8,128)} fusion(bf16[4096,2048,1]{1,0,2:T(8,128)(2,1)} %bitcast.211, bf16[6,2048,256]{2,1,0:T(8,128)(2,1)} %param.21), kind=kOutput, calls=%fused_computation.26 | convolution fusion | flops 25769803776 | bytes 48234496 | tf_op jit(solution)/shard_map/nd,cdf->cnf/dot_general | solution.py:158
  341.4 58.4 %all-gather.17.cloned.1.call-done = bf16[2,2048,2048]{2,1,0:T(8,128)(2,1)} async-done(((bf16[2,256,2048]{2,1,0:T(8,128)(2,1)}), bf16[2,2048,2048]{2,1,0:T(8,128)(2,1)}) %all-gather.17.cloned.1.call-update) | async-done | bytes 16777232 | tf_op jit(solution)/shard_map/all_gather | solution.py:179
  399.8 29.9 %fusion.11 = (bf16[6,4096,128]{1,2,0:T(8,128)(2,1)}, bf16[6,4096,128]{1,2,0:T(8,128)(2,1)}, bf16[6,4096,128]{1,2,0:T(8,128)(2,1)}) fusion(f32[6,4096,256]{1,2,0:T(8,128)} %convolution_bitcast_fusion, f32[6]{0:T(128)S(1)} %convert_element_type.131, bf16[6,128,2048]{2,1,0:T(8,128)(2,1)S(1)} %copy-done, bf16[4096,2048,1]{1,0,2:T(8,128)(2,1)} %bitcast.213), kind=kOutput, calls=%fused_computation.21 | convolution fusion | flops 12938379264 | bytes 63964160 | tf_op jit(solution)/shard_map/nd,cfd->cnf/dot_general | solution.py:194
  429.7 34.0 %fusion.15 = f32[4096,2048,1]{1,0,2:T(8,128)} fusion(bf16[6,2048,256]{2,1,0:T(8,128)(2,1)} %param.21, bf16[6,4096,128]{1,2,0:T(8,128)(2,1)} %get-tuple-element.79, bf16[6,4096,128]{1,2,0:T(8,128)(2,1)} %get-tuple-element.78), kind=kOutput, calls=%fused_computation.33 | convolution fusion | flops 25794969600 | bytes 52428800 | tf_op jit(solution)/shard_map/cnf,cdf->nd/dot_general | solution.py:201
  463.8 19.0 %bitcast_convert_fusion = bf16[4096,2048]{1,0:T(8,128)(2,1)} fusion(bf16[6,4096,128]{1,2,0:T(8,128)(2,1)} %get-tuple-element.80, bf16[6,128,2048]{2,1,0:T(8,128)(2,1)S(1)} %copy-done), kind=kOutput, calls=%fused_computation.14 | convolution fusion | flops 12893290496 | bytes 26214400 | tf_op jit(solution)/shard_map/cnf,cfd->nd/dot_general | solution.py:168
  483.7 185.5 %reduce-scatter.9.cloned.1.call-done = f32[2,256,2048]{2,1,0:T(8,128)} async-done(((f32[2,2048,2048]{2,1,0:T(8,128)}), f32[2,256,2048]{2,1,0:T(8,128)}) %reduce-scatter.9.cloned.1.call-update) | async-done | bytes 4194320 | tf_op jit(solution)/shard_map/reduce_scatter | solution.py:204
  674.3 114.8 %reduce-scatter.7.cloned.1.call-done = bf16[2,256,2048]{2,1,0:T(8,128)(2,1)} async-done(((bf16[2,2048,2048]{2,1,0:T(8,128)(2,1)}), bf16[2,256,2048]{2,1,0:T(8,128)(2,1)}) %reduce-scatter.7.cloned.1.call-update) | async-done | bytes 2097168 | tf_op jit(solution)/shard_map/reduce_scatter | solution.py:171
  789.1 8.9 fusion.58
  798.0 7.3 convolution_convert_fusion.2
  814.0 56.3 %fusion = (f32[2,5,4,256]{3,2,1,0:T(4,128)S(1)}, f32[2,5,2048,256,4]{3,2,4,1,0:T(8,128)}) fusion(f32[2,5,4,256,2048]{3,4,2,1,0:T(8,128)} %get-tuple-element.99, f32[2,5,4,256]{3,2,1,0:T(4,128)S(1)} %log_add_fusion, bf16[2,2048,5,64,1]{1,3,4,2,0:T(8,128)(2,1)} %bitcast.195, bf16[2,256,5,4,64]{1,4,3,2,0:T(8,128)(2,1)S(1)} %copy.187), kind=kOutput, calls=%fused_computation.2 | convolution fusion | flops 2747258880 | bytes 171786240 | tf_op jit(solution)/shard_map/rqkgd,rskd->rkgqs/dot_general | solution.py:223
  870.3 65.5 %fusion.2 = bf16[2,5,4,256,2048]{3,4,2,1,0:T(8,128)(2,1)} fusion(f32[2,5,2048,256,4]{3,2,4,1,0:T(8,128)} %get-tuple-element.103, f32[2,5,4,256,2048]{3,4,2,1,0:T(8,128)} %get-tuple-element.99, f32[2,5,4,256]{3,2,1,0:T(4,128)S(1)} %get-tuple-element.102, f32[2,5,4,256]{3,2,1,0:T(4,128)S(1)} %log_add_fusion), kind=kLoop, calls=%fused_computation.4 | loop fusion | flops 83886080 | bytes 209797120 | tf_op jit(solution)/shard_map/convert_element_type | solution.py:227
  935.8 19.7 %fusion.20 = bf16[2,5,64,2048]{3,2,1,0:T(8,128)(2,1)} fusion(bf16[2,256,5,4,64]{1,4,3,2,0:T(8,128)(2,1)S(1)} %copy-done.10, bf16[2,5,4,256,2048]{3,4,2,1,0:T(8,128)(2,1)} %fusion.2), kind=kOutput, calls=%fused_computation.42 | convolution fusion | flops 2686976000 | bytes 45875200 | tf_op jit(solution)/shard_map/rkgqs,rqkgd->rskd/dot_general | solution.py:233
  955.6 31.1 %bitcast_convert_fusion.2 = bf16[2,5,64,2048]{3,2,1,0:T(8,128)(2,1)} fusion(bf16[2,256,5,4,64]{1,4,3,2,0:T(8,128)(2,1)S(1)} %copy.187, f32[2,5,4,256,2048]{3,4,2,1,0:T(8,128)} %get-tuple-element.99, f32[2,5,4,256]{3,2,1,0:T(4,128)S(1)} %log_add_fusion), kind=kOutput, calls=%fused_computation.40 | convolution fusion | flops 2727608320 | bytes 87859200 | tf_op jit(solution)/shard_map/rkgqs,rqkgd->rskd/dot_general | solution.py:236
  1008.1 19.7 %convolution_multiply_fusion = f32[2,5,64,4,256]{4,2,3,1,0:T(8,128)} fusion(bf16[2,2048,5,64,1]{1,3,4,2,0:T(8,128)(2,1)S(1)} %bitcast.188, bf16[2,5,4,256,2048]{3,4,2,1,0:T(8,128)(2,1)} %fusion.2), kind=kOutput, calls=%fused_computation.80 | convolution fusion | flops 2685009920 | bytes 47185920 | tf_op jit(solution)/shard_map/rkgqs,rskd->rqkgd/dot_general | solution.py:229
  1044.1 7.9 multiply_reduce_fusion.3
  1058.8 8.5 bitcast_convert_fusion.1
  1067.4 20.0 %convolution_convert_fusion.1 = bf16[6,128,2048]{2,1,0:T(8,128)(2,1)} fusion(bf16[6,4096,128]{1,2,0:T(8,128)(2,1)} %get-tuple-element.80, bf16[4096,2048,1]{1,0,2:T(8,128)(2,1)} %bitcast.214), kind=kOutput, calls=%fused_computation.64 | convolution fusion | flops 12886474752 | bytes 26214400 | tf_op jit(solution)/shard_map/cnf,nd->cfd/dot_general | solution.py:190
  1087.4 34.6 %convert_bitcast_fusion = bf16[6,2048,256]{1,2,0:T(8,128)(2,1)} fusion(bf16[4096,2048,1]{1,0,2:T(8,128)(2,1)} %bitcast.212, bf16[6,4096,128]{1,2,0:T(8,128)(2,1)} %get-tuple-element.79, bf16[6,4096,128]{1,2,0:T(8,128)(2,1)} %get-tuple-element.78), kind=kOutput, calls=%fused_computation.39 | convolution fusion | flops 25798115328 | bytes 35651584 | tf_op jit(solution)/shard_map/nd,cnf->cdf/dot_general | solution.py:200
  1121.9 61.0 %reduce-scatter.15.cloned.1.call-done = bf16[256,1920]{1,0:T(8,128)(2,1)} async-done(((bf16[2048,1920]{1,0:T(8,128)(2,1)}), bf16[256,1920]{1,0:T(8,128)(2,1)}) %reduce-scatter.15.cloned.1.call-update) | async-done | bytes 983056 | tf_op jit(solution)/shard_map/reduce_scatter | solution.py:280
  1184.5 10.7 fusion.33
  1195.2 43.4 %all-reduce.1 = (f32[2048]{0:T(1024)}, f32[64]{0:T(128)}, f32[64]{0:T(128)}, f32[2048]{0:T(1024)}) all-reduce(f32[2048]{0:T(1024)S(1)} %get-tuple-element.62, f32[64]{0:T(128)S(1)} %reduce_sum.153, f32[64]{0:T(128)S(1)} %reduce_sum.156, f32[2048]{0:T(1024)S(1)} %copy-done.31), channel_id=1, replica_groups=mesh['dp'=4,'mp'=8] {'dp','mp'}, use_global_device_ids=true, to_apply=%region_25.26 | all-reduce | flops 4224 | bytes 33792 | tf_op jit(solution)/shard_map/psum | solution.py:293
  1238.6 6.7 fusion.29
  1245.3 321.2 %all-reduce.5.cloned.1.call-done = (bf16[6,2048,256]{1,2,0:T(8,128)(2,1)}, bf16[256,1920]{1,0:T(8,128)(2,1)}, bf16[160,2048]{1,0:T(8,128)(2,1)}, bf16[6,128,2048]{2,1,0:T(8,128)(2,1)}) async-done(((bf16[6,2048,256]{1,2,0:T(8,128)(2,1)}, bf16[256,1920]{1,0:T(8,128)(2,1)}, bf16[160,2048]{1,0:T(8,128)(2,1)}, bf16[6,128,2048]{2,1,0:T(8,128)(2,1)}), (bf16[6,2048,256]{1,2,0:T(8,128)(2,1)}, ...) | async-done | bytes 11075600 | tf_op jit(solution)/shard_map/psum | solution.py:290
  1571.4 9.4 copy.204
  (205 shorter events, 115.8 us)
Async XLA Ops:
  7.2 392.6 %copy-start = (bf16[6,128,2048]{2,1,0:T(8,128)(2,1)S(1)}, bf16[6,128,2048]{2,1,0:T(8,128)(2,1)}, u32[]{:S(2)}) copy-start(bf16[6,128,2048]{2,1,0:T(8,128)(2,1)} %param.22) | copy-start | bytes 9437188
  7.2 57.6 %all-gather.7.cloned.1.call-start = ((), (), s32[]{:S(2)}) async-start(), calls=%async_computation.6 | async-start | bytes 8847360 | tf_op jit(solution)/shard_map/all_gather | solution.py:99
  7.9 103.9 %all-gather.11.cloned.1.call-start = ((), (), s32[]{:S(2)}) async-start(), calls=%async_computation.8 | async-start | bytes 2949120 | tf_op jit(solution)/shard_map/all_gather | solution.py:122
  8.9 71.4 %copy-start.34 = (f32[320]{0:T(512)}, f32[320]{0:T(512)S(1)}, u32[]{:S(2)}) copy-start(f32[320]{0:T(512)S(1)} %mul.487) | copy-start | bytes 3844
  11.3 85.5 %copy-start.13 = (f32[2,256,64]{1,2,0:T(8,128)}, f32[2,256,64]{1,2,0:T(8,128)S(1)}, u32[]{:S(2)}) copy-start(f32[2,256,64]{1,2,0:T(8,128)S(1)} %pad_maximum_fusion.7) | copy-start | bytes 393220
  11.3 85.5 %copy-start.16 = (f32[2,256,64]{1,2,0:T(8,128)}, f32[2,256,64]{1,2,0:T(8,128)S(1)}, u32[]{:S(2)}) copy-start(f32[2,256,64]{1,2,0:T(8,128)S(1)} %pad_maximum_fusion.8) | copy-start | bytes 393220
  13.5 59.1 %copy-start.39 = (f32[2,256]{1,0:T(2,128)}, f32[2,256]{1,0:T(2,128)S(1)}, u32[]{:S(2)}) copy-start(f32[2,256]{1,0:T(2,128)S(1)} %add_rsqrt_fusion.3) | copy-start | bytes 6148
  13.5 65.4 %copy-start.41 = (f32[64]{0:T(128)S(1)}, f32[64]{0:T(128)}, u32[]{:S(2)}) copy-start(f32[64]{0:T(128)} %param.17) | copy-start | bytes 772
  81.2 89.6 %all-gather.9.cloned.1.call-start = ((), (), s32[]{:S(2)}) async-start(), calls=%async_computation.7 | async-start | bytes 3538944 | tf_op jit(solution)/shard_map/all_gather | solution.py:123
  83.3 123.6 %all-gather.13.cloned.1.call-start = ((), (), s32[]{:S(2)}) async-start(), calls=%async_computation.9 | async-start | bytes 5898240 | tf_op jit(solution)/shard_map/all_gather | solution.py:100
  83.9 223.6 %all-gather.15.cloned.1.call-start = ((), (), s32[]{:S(2)}) async-start(), calls=%async_computation.10 | async-start | bytes 18874368 | tf_op jit(solution)/shard_map/all_gather | solution.py:165
  90.3 5.6 copy-start.37
  144.2 31.4 %copy-start.24 = (f32[2,5,4,256]{3,2,1,0:T(4,128)}, f32[2,5,4,256]{3,2,1,0:T(4,128)S(1)}, u32[]{:S(2)}) copy-start(f32[2,5,4,256]{3,2,1,0:T(4,128)S(1)} %get-tuple-element.98) | copy-start | bytes 122884
  170.7 36.2 %copy-start.26 = (f32[2,5,4,256]{3,2,1,0:T(4,128)}, f32[2,5,4,256]{3,2,1,0:T(4,128)S(1)}, u32[]{:S(2)}) copy-start(f32[2,5,4,256]{3,2,1,0:T(4,128)S(1)} %fusion.3) | copy-start | bytes 122884
  207.0 8.8 copy-start.29
  217.5 182.2 %all-gather.17.cloned.1.call-start = ((), (), s32[]{:S(2)}) async-start(), calls=%async_computation.12 | async-start | bytes 18874368 | tf_op jit(solution)/shard_map/all_gather | solution.py:179
  221.4 447.7 %reduce-scatter.9.cloned.1.call-start = ((), (), s32[]{:S(2)}) async-start(), calls=%async_computation.13 | async-start | bytes 37748736 | tf_op jit(solution)/shard_map/reduce_scatter | solution.py:204
  463.8 325.4 %reduce-scatter.7.cloned.1.call-start = ((), (), s32[]{:S(2)}) async-start(), calls=%async_computation.11 | async-start | bytes 18874368 | tf_op jit(solution)/shard_map/reduce_scatter | solution.py:171
  482.9 186.3 %copy-start.30 = (f32[2048]{0:T(1024)S(1)}, f32[2048]{0:T(1024)}, u32[]{:S(2)}) copy-start(f32[2048]{0:T(1024)} %param.20) | copy-start | bytes 24580
  482.9 186.3 %copy-start.33 = (f32[2,256]{1,0:T(2,128)S(1)}, f32[2,256]{1,0:T(2,128)}, u32[]{:S(2)}) copy-start(f32[2,256]{1,0:T(2,128)} %copy-done.32) | copy-start | bytes 6148
  482.9 569.1 %reduce-scatter.11.cloned.1.call-start = ((), (), s32[]{:S(2)}) async-start(), calls=%async_computation.14 | async-start | bytes 2949120 | tf_op jit(solution)/shard_map/reduce_scatter | solution.py:243
  798.0 7.3 copy-start.18
  870.3 65.5 %copy-start.10 = (bf16[2,256,5,4,64]{1,4,3,2,0:T(8,128)(2,1)S(1)}, bf16[2,256,5,4,64]{1,4,3,2,0:T(8,128)(2,1)}, u32[]{:S(2)}) copy-start(bf16[2,256,5,4,64]{1,4,3,2,0:T(8,128)(2,1)} %fusion.43) | copy-start | bytes 3932164
  955.6 99.3 %reduce-scatter.13.cloned.1.call-start = ((), (), s32[]{:S(2)}) async-start(), calls=%async_computation.15 | async-start | bytes 3538944 | tf_op jit(solution)/shard_map/reduce_scatter | solution.py:249
  991.5 130.4 %reduce-scatter.17.cloned.1.call-start = ((), (), s32[]{:S(2)}) async-start(), calls=%async_computation.17 | async-start | bytes 5898240 | tf_op jit(solution)/shard_map/reduce_scatter | solution.py:283
  999.5 183.5 %reduce-scatter.15.cloned.1.call-start = ((), (), s32[]{:S(2)}) async-start(), calls=%async_computation.16 | async-start | bytes 8847360 | tf_op jit(solution)/shard_map/reduce_scatter | solution.py:280
  1008.1 19.7 %copy-start.17 = (f32[2,256,64]{1,2,0:T(8,128)S(1)}, f32[2,256,64]{1,2,0:T(8,128)}, u32[]{:S(2)}) copy-start(f32[2,256,64]{1,2,0:T(8,128)} %copy-done.16) | copy-start | bytes 393220
  1044.1 9.1 copy-start.8
  1044.1 9.1 copy-start.42
  1067.3 499.2 %all-reduce.5.cloned.1.call-start = ((), (), s32[]{:S(2)}) async-start(), calls=%async_computation.18 | async-start | bytes 22151168 | tf_op jit(solution)/shard_map/psum | solution.py:290
  1184.5 10.7 copy-start.31
  1580.8 5.6 copy-start.1
  (25 other events, 70.5 us)
Sparse Core Ops, SparseCore 0:
  9.9 54.8 all-gather.6
  81.3 30.4 all-gather.10
  114.3 32.3 all-gather.8
  148.4 41.1 all-gather.12
  217.6 89.8 all-gather.14
  309.9 89.8 all-gather.16
  463.9 205.2 reduce-scatter.8
  673.2 115.9 reduce-scatter.6
  955.7 43.6 reduce-scatter.10
  1003.0 46.2 reduce-scatter.12
  1052.7 56.5 reduce-scatter.16
  1113.6 69.3 reduce-scatter.14
  1185.9 380.5 all-reduce.4
where the time goes:
time: 1600 us; the launch traced here: 1590 us
  waiting for transfers between devices  893 us (56%)
  matrix products  409 us (26%)
  other arithmetic  161 us (10%)
  local copies, waits for them, and re-layouts  71.4 us (4%)
  blocking collectives  43.4 us (3%)
    psum x1, waiting for transfers between devices, shards(): lax.psum(grad_gate_up.astype(jnp.bfloat16), 'dp').astype(jnp.float32)  321 us
    reduce_scatter x1, waiting for transfers between devices, shards(): lax.psum_scatter(grad_flat.reshape(row_count, sequence_len, model_width),...  185 us
    reduce_scatter x1, waiting for transfers between devices, shards(): lax.psum_scatter(partial_out.reshape(row_count, sequence_len, model_width...  115 us
    all_gather x1, waiting for transfers between devices, shards(): gathered_f = lax.all_gather(normed_fb, 'mp', axis=1, tiled=True)  85.8 us
    convert_element_type x1, other arithmetic, shards(): (probs_again * (grad_probs - inner_sum)).astype(jnp.bfloat16)  65.5 us
    reduce_scatter x1, waiting for transfers between devices, shards(): lax.psum_scatter(grad_attend.astype(jnp.bfloat16), 'mp', scatter_dimensio...  61 us
    all_gather x1, waiting for transfers between devices, shards(): lax.all_gather(grad_branch, 'mp', axis=1, tiled=True)  58.4 us
    dot_general x1, matrix products, shards(): jnp.einsum('rqkgd,rskd->rkgqs', grad_context_b, values_all, preferred_ele...  56.3 us
  transfers between devices with their start and end apart: 13, of which 8 were waited for; matrix products, arithmetic and copies ran while one was open for 23% of the time, Pallas kernels for 0%

commit v1 on v0

v1 whole, which is shorter than its diff:
```python
import functools

import jax
import jax.numpy as jnp
from jax import lax
from jax.experimental import pallas as pl
from jax.experimental.pallas import tpu as pltpu
from jax.sharding import PartitionSpec as P

H = 20
KVH = 5
HD = 64
TILE = 128
EPSILON = 1e-06
QW = H * HD
LANES = 128
GW = (H // KVH) * HD
LOG2E = 1.4426950408889634
LN2 = 0.6931471805599453
BF = jnp.bfloat16
F32 = jnp.float32
MIB = 1 << 20
NT = (((1,), (1,)), ((), ()))
TN = (((0,), (0,)), ((), ()))


def params(mib=56, axes=1, key=None):
    if key is None:
        return pltpu.CompilerParams(
            vmem_limit_bytes=mib * MIB, dimension_semantics=("arbitrary",) * axes
        )
    return pltpu.CompilerParams(
        vmem_limit_bytes=mib * MIB,
        dimension_semantics=("arbitrary",) * axes if axes else None,
        collective_id=key,
        has_side_effects=True,
    )


def mm(a, b):
    return jnp.dot(a, b, preferred_element_type=F32)


def dg(a, b, dims):
    return lax.dot_general(a, b, dims, preferred_element_type=F32)


def doc_starts(docs):
    index = jnp.arange(docs.shape[-1], dtype=jnp.int32)
    change = jnp.concatenate(
        [jnp.ones(docs.shape[:-1] + (1,), dtype=jnp.bool_), docs[..., 1:] != docs[..., :-1]],
        axis=-1,
    )
    return lax.cummax(jnp.where(change, index, 0), axis=docs.ndim - 1)


def rotary_tables(positions):
    half_dim = HD // 2
    freqs = 1.0 / 10000.0 ** (jnp.arange(half_dim, dtype=jnp.float32) * 2.0 / HD)
    angles = positions.astype(jnp.float32)[..., None] * freqs
    return jnp.tile(jnp.cos(angles), 4), jnp.tile(jnp.sin(angles), 4)


def rms_scale(values):
    return lax.rsqrt(jnp.mean(values * values, axis=-1, keepdims=True) + EPSILON)


MESH = pl.DeviceIdType.MESH


def flip(me, k):
    bit = 1
    while bit <= k:
        if k & bit:
            me = me + bit - 2 * bit * lax.rem(lax.div(me, bit), 2)
        bit *= 2
    return me


def link_bits(n):
    return [1 << i for i in range(1, n.bit_length() - 1)]


def greet(n, me):
    barrier = pltpu.get_barrier_semaphore()
    bits = [1] + link_bits(n)
    for bit in bits:
        pl.semaphore_signal(barrier, inc=1, device_id={"mp": flip(me, bit)}, device_id_type=MESH)
    pl.semaphore_wait(barrier, len(bits))


class Gather:
    def __init__(self, n, me, own, slot, send, recv):
        self.n, self.me, self.own, self.slot, self.send, self.recv = n, me, own, slot, send, recv
        bits = link_bits(n)
        self.order = (bits + [1], bits[::-1] + [1])
        even = [(k, h) for k in range(2, n, 2) for h in (0, 1)]
        even.sort(key=lambda kh: (bin(kh[0]).count("1"), max(self.place(*kh)), kh[1]))
        self.even = even

    def place(self, k, half):
        return [i for i, bit in enumerate(self.order[half]) if k & bit]

    def copy(self, k, half, bit):
        return pltpu.make_async_remote_copy(
            src_ref=self.own(half) if k == 0 else self.slot(k, half),
            dst_ref=self.slot(k, half),
            send_sem=self.send.at[k ^ bit, half],
            recv_sem=self.recv.at[k ^ bit, half],
            device_id={"mp": flip(self.me, bit)},
            device_id_type=MESH,
        )

    def onward(self, k, half):
        return self.order[half][(max(self.place(k, half)) + 1) if k else 0 :]

    def start(self):
        for i in range(len(self.order[0])):
            for half in (0, 1):
                self.copy(0, half, self.order[half][i]).start()

    def arrive(self, k, half):
        here = self.slot(k, half)
        pltpu.make_async_remote_copy(
            src_ref=here,
            dst_ref=here,
            send_sem=self.send.at[k, half],
            recv_sem=self.recv.at[k, half],
            device_id={"mp": flip(self.me, 1)},
            device_id_type=MESH,
        ).wait_recv()

    def forward(self, k, half):
        self.arrive(k, half)
        for bit in self.onward(k, half):
            self.copy(k, half, bit).start()

    def rest(self):
        for k, half in [(1, 0), (1, 1)] + [(k + 1, h) for k, h in self.even]:
            self.arrive(k, half)

    def drain(self):
        for k in range(0, self.n, 2):
            for half in (0, 1):
                for bit in self.onward(k, half):
                    self.copy(k, half, bit).wait_send()


class Scatter:
    def __init__(self, n, me, part, core, link, stage, sems):
        self.n, self.me, self.part = n, me, part
        self.core, self.link, self.stage = core, link, stage
        self.core_send, self.core_recv, self.link_send, self.link_recv = sems
        bits = link_bits(n)
        self.order = (bits[::-1], bits)

    def first(self, k, half):
        return next(i for i, bit in enumerate(self.order[half]) if k & bit)

    def core_copy(self, k, ref):
        return pltpu.make_async_remote_copy(
            src_ref=ref,
            dst_ref=self.core(k // 2),
            send_sem=self.core_send.at[k // 2],
            recv_sem=self.core_recv.at[k // 2],
            device_id={"mp": flip(self.me, 1)},
            device_id_type=MESH,
        )

    def link_copy(self, k, half):
        bit = self.order[half][self.first(k, half)]
        return pltpu.make_async_remote_copy(
            src_ref=self.part(self.stage(k // 2 - 1), half),
            dst_ref=self.link(half, k // 2 - 1),
            send_sem=self.link_send.at[half, k // 2 - 1],
            recv_sem=self.link_recv.at[half, k // 2 - 1],
            device_id={"mp": flip(self.me, bit)},
            device_id_type=MESH,
        )

    def addends(self, k, half):
        upto = self.first(k, half) if k else len(self.order[half])
        return [k | bit for bit in self.order[half][:upto]]

    def odd(self, k, ref):
        self.core_copy(k, ref).start()

    def even(self, k, ref):
        self.core_copy(k + 1, self.core(k // 2)).wait_recv()
        for half in (0, 1):
            joined = [self.part(ref, half), self.part(self.core(k // 2), half)]
            for j in self.addends(k, half):
                self.link_copy(j, half).wait_recv()
                joined.append(self.link(half, j // 2 - 1))
            add_up(self.part(self.stage(k // 2 - 1), half), joined)
            self.link_copy(k, half).start()

    def own(self, ref, out):
        self.core_copy(1, self.core(0)).wait_recv()
        for half in (0, 1):
            joined = [self.part(ref, half), self.part(self.core(0), half)]
            for j in self.addends(0, half):
                self.link_copy(j, half).wait_recv()
                joined.append(self.link(half, j // 2 - 1))
            add_up(self.part(out, half), joined)

    def drain(self, ref):
        for k in range(1, self.n, 2):
            self.core_copy(k, ref).wait_send()
        for k in range(2, self.n, 2):
            for half in (0, 1):
                self.link_copy(k, half).wait_send()


def add_up(out, terms):
    rows = out.shape[-2]
    step = 16
    lead = (slice(None),) * (len(out.shape) - 2)

    @pl.loop(0, rows // step)
    def _(i):
        at = lead + (pl.ds(pl.multiple_of(i * step, step), step), slice(None))
        total = terms[0][at].astype(F32)
        for t in terms[1:]:
            total = total + t[at].astype(F32)
        out[at] = total.astype(out.dtype)


def scatter_scratch(n, shape, half):
    return [
        pltpu.VMEM((n // 2,) + shape, BF),
        pltpu.VMEM((2, n // 2 - 1) + half, BF),
        pltpu.VMEM((n // 2 - 1,) + shape, BF),
        pltpu.SemaphoreType.DMA((n // 2,)),
        pltpu.SemaphoreType.DMA((n // 2,)),
        pltpu.SemaphoreType.DMA((2, n // 2 - 1)),
        pltpu.SemaphoreType.DMA((2, n // 2 - 1)),
    ]


def make_scatter(n, me, part, refs):
    core, link, stage = refs[:3]
    return Scatter(
        n,
        me,
        part,
        lambda i: core.at[i],
        lambda h, i: link.at[h, i],
        lambda i: stage.at[i],
        refs[3:7],
    )


def half_turn(x, lane):
    first = (lane % HD) < HD // 2
    return jnp.where(first, -pltpu.roll(x, LANES - HD // 2, 1), pltpu.roll(x, HD // 2, 1))


def half_turn_back(x, lane):
    first = (lane % HD) < HD // 2
    return jnp.where(first, pltpu.roll(x, LANES - HD // 2, 1), -pltpu.roll(x, HD // 2, 1))


def group_mean(x, ones):
    high = x.astype(BF)
    low = (x - high.astype(F32)).astype(BF)
    return (mm(high, ones) + mm(low, ones)) * (1.0 / HD)


def project_kernel(
    n, x_ref, gain_ref, w_ref, cos_ref, sin_ref, gq_ref, gk_ref, ones_ref,
    normed_ref, raw_ref, q_ref, w_out, kv_out,
    w_all, kv_own, w_send, w_recv, kv_send, kv_recv, local,
):
    me = lax.axis_index("mp")
    depth = w_ref.shape[0]
    tokens = x_ref.shape[0]
    rows = kv_out.shape[0]
    span = tokens // rows
    half = depth // 2
    own_w = pltpu.make_async_copy(w_ref, w_all.at[me], local.at[0])
    own_w.start()
    greet(n, me)
    weights = Gather(
        n,
        me,
        lambda h: w_ref.at[pl.ds(h * half, half)],
        lambda k, h: w_all.at[flip(me, k), pl.ds(h * half, half)],
        w_send,
        w_recv,
    )
    weights.start()
    step = min(64, tokens)

    @pl.loop(0, tokens // step)
    def _(i):
        at = pl.ds(pl.multiple_of(i * step, step), step)
        x = x_ref[at, :].astype(F32)
        scale = lax.rsqrt(jnp.mean(x * x, axis=-1, keepdims=True) + EPSILON)
        normed_ref[at, :] = (x * scale * gain_ref[...]).astype(BF)

    chunk = min(256, tokens)

    def accumulate(k, fresh):
        block = flip(me, k)
        columns = pl.ds(pl.multiple_of(block * depth, depth), depth)

        @pl.loop(0, tokens // chunk)
        def _(i):
            at = pl.ds(pl.multiple_of(i * chunk, chunk), chunk)
            term = mm(normed_ref[at, columns], w_all[block])
            raw_ref[at, :] = term if fresh else raw_ref[at, :] + term

    own_w.wait()
    accumulate(0, True)
    for h in (0, 1):
        weights.arrive(1, h)
    accumulate(1, False)
    for i, (k, h) in enumerate(weights.even):
        weights.forward(k, h)
        if any(k == other for other, _ in weights.even[:i]):
            accumulate(k, False)
    for k in range(3, n, 2):
        for h in (0, 1):
            weights.arrive(k, h)
        accumulate(k, False)
    out_w = pltpu.make_async_copy(w_all, w_out, local.at[0])
    out_w.start()

    chunk = min(128, tokens)
    lane = lax.broadcasted_iota(jnp.int32, (chunk, LANES), 1)

    def finish(i, tiles):
        at = pl.ds(pl.multiple_of(i * chunk, chunk), chunk)
        cos, sin = cos_ref[at, :], sin_ref[at, :]
        for tile in tiles:
            lanes = slice(tile * LANES, (tile + 1) * LANES)
            x = raw_ref[at, lanes]
            query = tile < QW // LANES
            scale = lax.rsqrt(group_mean(x * x, ones_ref[...]) + EPSILON)
            v = x * scale * (gq_ref[...] if query else gk_ref[...])
            y = v * cos + half_turn(v, lane) * sin
            if query:
                q_ref[at, lanes] = (y * (HD**-0.5 * LOG2E)).astype(BF)
            else:
                mine = slice(tile * LANES - QW, (tile + 1) * LANES - QW)
                kv_own[at, mine] = jnp.where(lane < HD, y, x).astype(BF)

    count = raw_ref.shape[1] // LANES

    @pl.loop(0, tokens // chunk)
    def _(i):
        finish(i, range(QW // LANES, count))

    both = rows // 2
    keep = [
        pltpu.make_async_copy(
            kv_own.at[pl.ds(r * span, span)], kv_out.at[r, me], local.at[1 + r]
        )
        for r in range(rows)
    ]
    for c in keep:
        c.start()
    kvs = Gather(
        n,
        me,
        lambda h: kv_own.at[pl.ds(h * span, span)],
        lambda k, h: kv_out.at[h, flip(me, k)],
        kv_send,
        kv_recv,
    )
    kvs.start()

    @pl.loop(0, tokens // chunk)
    def _(i):
        finish(i, range(QW // LANES))

    for k, h in kvs.even:
        kvs.forward(k, h)
    kvs.rest()
    for c in keep:
        c.wait()
    out_w.wait()
    weights.drain()
    kvs.drain()


def project(n, rows, x, gain, w, cos, sin, gq, gk, ones):
    tokens, width = x.shape
    depth, columns = w.shape
    vmem = pl.BlockSpec(memory_space=pltpu.VMEM)
    hbm = pl.BlockSpec(memory_space=pl.ANY)
    kvw = columns - QW
    return pl.pallas_call(
        functools.partial(project_kernel, n),
        in_specs=[vmem, vmem, hbm, vmem, vmem, vmem, vmem, vmem],
        out_specs=[vmem, vmem, vmem, hbm, hbm],
        out_shape=[
            jax.ShapeDtypeStruct((tokens, width), BF),
            jax.ShapeDtypeStruct((tokens, columns), F32),
            jax.ShapeDtypeStruct((tokens, QW), BF),
            jax.ShapeDtypeStruct((n, depth, columns), BF),
            jax.ShapeDtypeStruct((rows, n, tokens // rows, kvw), BF),
        ],
        scratch_shapes=[
            pltpu.VMEM((n, depth, columns), BF),
            pltpu.VMEM((tokens, kvw), BF),
            pltpu.SemaphoreType.DMA((n, 2)),
            pltpu.SemaphoreType.DMA((n, 2)),
            pltpu.SemaphoreType.DMA((n, 2)),
            pltpu.SemaphoreType.DMA((n, 2)),
            pltpu.SemaphoreType.DMA((1 + rows,)),
        ],
        compiler_params=params(axes=0, key=0),
        name="project",
    )(x, gain, w, cos, sin, gq, gk, ones)


def unproject_kernel(
    n, dq_ref, dkv_ref, raw_ref, cos_ref, sin_ref, gq_ref, gk_ref, ones_ref, normed_ref, gout_ref,
    gj_ref, sq_ref, sk_ref, attend_ref, output_ref,
    dkv_own, term, *scratch,
):
    me = lax.axis_index("mp")
    greet(n, me)
    tokens = dq_ref.shape[0]
    rows = dkv_ref.shape[0]
    span = tokens // rows
    columns = raw_ref.shape[1]
    depth = attend_ref.shape[0]

    keys = make_scatter(n, me, lambda ref, h: ref.at[h], scratch[:7])
    half_w = output_ref.shape[1] // 2
    outs = make_scatter(
        n, me, lambda ref, h: ref.at[:, pl.ds(h * half_w, half_w)], scratch[7:14]
    )
    half_d = depth // 2
    weights = make_scatter(
        n, me, lambda ref, h: ref.at[pl.ds(h * half_d, half_d)], scratch[14:21]
    )

    def dkv_term(k):
        return dkv_ref.at[:, flip(me, k)]

    def out_term(k):
        return gout_ref.at[flip(me, k)]

    for k in range(n - 1, 0, -2):
        keys.odd(k, dkv_term(k))
    for k in range(n - 2, 0, -2):
        keys.even(k, dkv_term(k))
    for k in range(n - 1, 0, -2):
        outs.odd(k, out_term(k))

    chunk = min(128, tokens)
    lane = lax.broadcasted_iota(jnp.int32, (chunk, LANES), 1)
    sq_ref[...] = jnp.zeros_like(sq_ref)
    sk_ref[...] = jnp.zeros_like(sk_ref)

    def back(i, tiles, query):
        at = pl.ds(pl.multiple_of(i * chunk, chunk), chunk)
        cos, sin = cos_ref[at, :], sin_ref[at, :]
        total = 0.0
        for tile in tiles:
            lanes = slice(tile * LANES, (tile + 1) * LANES)
            x = raw_ref[at, lanes]
            if query:
                e = dq_ref[at, lanes]
            else:
                per = span // chunk
                here = pl.ds(pl.multiple_of(lax.rem(i, per) * chunk, chunk), chunk)
                e = dkv_own[lax.div(i, per), here, slice(tile * LANES - QW, (tile + 1) * LANES - QW)]
            scale = lax.rsqrt(group_mean(x * x, ones_ref[...]) + EPSILON)
            v = x * scale
            turned = e * cos + half_turn_back(e * sin, lane)
            u = turned * (gq_ref[...] if query else gk_ref[...])
            grad = scale * (u - v * group_mean(u * v, ones_ref[...]))
            gj_ref[at, lanes] = (grad if query else jnp.where(lane < HD, grad, e)).astype(BF)
            total = total + jnp.sum(turned * v, axis=0, keepdims=True)
        sums = sq_ref if query else sk_ref
        sums[...] += jnp.broadcast_to(total, sums.shape)

    count = columns // LANES

    @pl.loop(0, tokens // chunk)
    def _(i):
        back(i, range(QW // LANES), True)

    for k in range(n - 2, 0, -2):
        outs.even(k, out_term(k))

    keys.own(dkv_term(0), dkv_own)

    @pl.loop(0, tokens // chunk)
    def _(i):
        back(i, range(QW // LANES, count), False)

    for k in range(n - 1, -1, -1):
        at = pl.ds(pl.multiple_of(flip(me, k) * depth, depth), depth)
        here = term.at[k]
        here[...] = dg(normed_ref[:, at], gj_ref[...], TN).astype(BF)
        if k % 2:
            weights.odd(k, here)
        elif k:
            weights.even(k, here)
    outs.own(out_term(0), output_ref)
    weights.own(term.at[0], attend_ref)
    keys.drain(dkv_term(0))
    outs.drain(out_term(0))
    weights.drain(term.at[0])


def unproject(n, dq, dkv, raw, cos, sin, gq, gk, ones, normed, gout):
    tokens, columns = raw.shape
    rows = dkv.shape[0]
    span = tokens // rows
    kvw = columns - QW
    width = normed.shape[1]
    depth = width // n
    vmem = pl.BlockSpec(memory_space=pltpu.VMEM)
    return pl.pallas_call(
        functools.partial(unproject_kernel, n),
        in_specs=[vmem] * 10,
        out_specs=[vmem] * 5,
        out_shape=[
            jax.ShapeDtypeStruct((tokens, columns), BF),
            jax.ShapeDtypeStruct((8, LANES), F32),
            jax.ShapeDtypeStruct((8, LANES), F32),
            jax.ShapeDtypeStruct((depth, columns), BF),
            jax.ShapeDtypeStruct((QW // n, width), BF),
        ],
        scratch_shapes=[pltpu.VMEM((rows, span, kvw), F32), pltpu.VMEM((n, depth, columns), BF)]
        + scatter_scratch(n, (rows, span, kvw), (span, kvw))
        + scatter_scratch(n, (QW // n, width), (QW // n, width // 2))
        + scatter_scratch(n, (depth, columns), (depth // 2, columns)),
        compiler_params=params(mib=60, axes=0, key=2),
        name="unproject",
    )(dq, dkv, raw, cos, sin, gq, gk, ones, normed, gout)


def key_positions(shape, axis, group, per, span):
    return group * per * span + lax.broadcasted_iota(jnp.int32, shape, axis)


def attend_kernel(keys, info, q_ref, kv_ref, start_ref, ctx_ref, rl_ref, acc):
    span = q_ref.shape[1]
    per = keys // span
    row = pl.program_id(0)
    me, first, last_start = info[row, 0], info[row, 1], info[row, 2]
    low_q = lax.broadcasted_iota(jnp.int32, (span, LANES), 1) < HD
    low_k = lax.broadcasted_iota(jnp.int32, (keys, LANES), 1) < HD
    one = jnp.ones((keys, LANES), BF)
    none = jnp.zeros((span, LANES), BF)
    queries = []
    for h in range(GW // HD):
        pair = q_ref[0, :, (h // 2) * LANES : (h // 2 + 1) * LANES]
        queries.append(jnp.where(low_q, pair, none) if h % 2 == 0 else jnp.where(low_q, none, pair))
    acc[...] = jnp.zeros_like(acc)

    def block(g, masked):
        group = g
        kv = kv_ref[0, pl.ds(pl.multiple_of(group * keys, keys), keys), :]
        vk = jnp.concatenate([kv[:, HD:], kv[:, :HD]], axis=1)
        key_sides = (kv, vk)
        value_sides = (jnp.where(low_k, vk, one), jnp.where(low_k, one, kv))
        if masked:
            position = key_positions((span, keys), 1, group, per, span)
            own = me * span + lax.broadcasted_iota(jnp.int32, (span, keys), 0)
            seen = (position <= own) & (position >= start_ref[0][:, :1])
        for h in range(GW // HD):
            p = jnp.exp2(dg(queries[h], key_sides[h % 2], NT))
            if masked:
                p = jnp.where(seen, p, 0.0)
            acc[h] += mm(p.astype(BF), value_sides[h % 2])

    def step(g, carry):
        edge = (g == me // per) | (g * keys < last_start)
        pl.when(edge)(lambda: block(g, True))
        pl.when(jnp.logical_not(edge))(lambda: block(g, False))
        return carry

    lax.fori_loop(first, me // per + 1, step, 0)
    for pair in range(GW // LANES):
        even, odd = acc[2 * pair], acc[2 * pair + 1]
        total = jnp.where(low_q, pltpu.roll(even, HD, 1), pltpu.roll(odd, HD, 1))
        inverse = 1.0 / total
        lanes = slice(pair * LANES, (pair + 1) * LANES)
        ctx_ref[0, :, lanes] = (jnp.where(low_q, even, odd) * inverse).astype(BF)
        rl_ref[0, :, lanes] = inverse


def attend(info, q, kv, start):
    rows, span, _ = q.shape
    length = kv.shape[1]
    keys = min(512, length)
    own = lambda r, h, info: (r, 0, h)
    spec = pltpu.PrefetchScalarGridSpec(
        num_scalar_prefetch=1,
        grid=(rows, KVH),
        in_specs=[
            pl.BlockSpec((1, span, GW), own),
            pl.BlockSpec((1, length, LANES), own),
            pl.BlockSpec((1, span, LANES), lambda r, h, info: (r, 0, 0)),
        ],
        out_specs=[pl.BlockSpec((1, span, GW), own), pl.BlockSpec((1, span, GW), own)],
        scratch_shapes=[pltpu.VMEM((GW // HD, span, LANES), F32)],
    )
    return pl.pallas_call(
        functools.partial(attend_kernel, keys),
        grid_spec=spec,
        out_shape=[jax.ShapeDtypeStruct(q.shape, BF), jax.ShapeDtypeStruct(q.shape, F32)],
        compiler_params=params(axes=2),
        cost_estimate=pl.CostEstimate(
            flops=16 * rows * H * span * length * HD,
            bytes_accessed=rows * (length * 1280 + span * QW * 8),
            transcendentals=rows * H * span * length,
        ),
        name="attend",
    )(info, q, kv, start)


def attend_back_kernel(
    keys, info, q_ref, kv_ref, start_ref, do_ref, ctx_ref, rl_ref, dq_ref, dkv_ref, acc, sides
):
    span = q_ref.shape[1]
    per = keys // span
    length = kv_ref.shape[1]
    row = pl.program_id(0)
    me, first, last_start = info[row, 0], info[row, 1], info[row, 2]
    lane = lax.broadcasted_iota(jnp.int32, (span, LANES), 1)
    low_q = lane < HD
    low_k = lax.broadcasted_iota(jnp.int32, (keys, LANES), 1) < HD
    one = jnp.ones((keys, LANES), BF)
    for h in range(GW // HD):
        lanes = slice((h // 2) * LANES, (h // 2 + 1) * LANES)
        mine = low_q if h % 2 == 0 else jnp.logical_not(low_q)
        scaled = do_ref[0, :, lanes].astype(F32) * rl_ref[0, :, lanes]
        own = jnp.where(mine, scaled, 0.0)
        delta = -jnp.sum(own * ctx_ref[0, :, lanes].astype(F32), axis=1, keepdims=True)
        one_part = delta.astype(BF).astype(F32)
        two_part = (delta - one_part).astype(BF).astype(F32)
        three_part = delta - one_part - two_part
        base = HD if h % 2 == 0 else 0
        extra = jnp.where(
            lane == base,
            one_part,
            jnp.where(lane == base + 1, two_part, jnp.where(lane == base + 2, three_part, 0.0)),
        )
        sides[0, h] = jnp.where(mine, q_ref[0, :, lanes].astype(F32), 0.0).astype(BF)
        sides[1, h] = own.astype(BF)
        sides[2, h] = jnp.where(mine, scaled, extra).astype(BF)
    acc[...] = jnp.zeros_like(acc)

    def block(g, masked):
        group = g
        here = pl.ds(pl.multiple_of(group * keys, keys), keys)
        kv = kv_ref[0, here, :]
        vk = jnp.concatenate([kv[:, HD:], kv[:, :HD]], axis=1)
        key_sides = (kv, vk)
        value_sides = (jnp.where(low_k, vk, one), jnp.where(low_k, one, kv))
        if masked:
            position = key_positions((keys, span), 0, group, per, span)
            own = me * span + lax.broadcasted_iota(jnp.int32, (keys, span), 1)
            seen = (position <= own) & (position >= start_ref[0][:1, :])
        grad_key = grad_value = 0.0
        for h in range(GW // HD):
            e = jnp.exp2(dg(key_sides[h % 2], sides[0, h], NT))
            if masked:
                e = jnp.where(seen, e, 0.0)
            ds = (e * dg(value_sides[h % 2], sides[2, h], NT)).astype(BF)
            grad_value = grad_value + mm(e.astype(BF), sides[1, h])
            grad_key = grad_key + mm(ds, sides[0, h])
            acc[h] += dg(ds, key_sides[h % 2], TN)
        grad_key = (grad_key + pltpu.roll(grad_key, HD, 1)) * LN2
        grad_value = grad_value + pltpu.roll(grad_value, HD, 1)
        dkv_ref[0, here, :] = jnp.where(low_k, grad_key, grad_value).astype(BF)

    def step(g, carry):
        visited = (g >= first) & (g <= me // per)
        edge = (g == me // per) | (g * keys < last_start)

        @pl.when(jnp.logical_not(visited))
        def _():
            group = g
            dkv_ref[0, pl.ds(pl.multiple_of(group * keys, keys), keys), :] = jnp.zeros((keys, LANES), BF)

        pl.when(visited & edge)(lambda: block(g, True))
        pl.when(visited & jnp.logical_not(edge))(lambda: block(g, False))
        return carry

    lax.fori_loop(0, length // keys, step, 0)
    for pair in range(GW // LANES):
        lanes = slice(pair * LANES, (pair + 1) * LANES)
        dq_ref[0, :, lanes] = jnp.where(low_q, acc[2 * pair], acc[2 * pair + 1]) * (HD**-0.5)


def attend_back(info, q, kv, start, do, ctx, rl):
    rows, span, _ = q.shape
    length = kv.shape[1]
    keys = min(512, length)
    own = lambda r, h, info: (r, 0, h)
    spec = pltpu.PrefetchScalarGridSpec(
        num_scalar_prefetch=1,
        grid=(rows, KVH),
        in_specs=[
            pl.BlockSpec((1, span, GW), own),
            pl.BlockSpec((1, length, LANES), own),
            pl.BlockSpec((1, 8, span), lambda r, h, info: (r, 0, 0)),
            pl.BlockSpec((1, span, GW), own),
            pl.BlockSpec((1, span, GW), own),
            pl.BlockSpec((1, span, GW), own),
        ],
        out_specs=[pl.BlockSpec((1, span, GW), own), pl.BlockSpec((1, length, LANES), own)],
        scratch_shapes=[
            pltpu.VMEM((GW // HD, span, LANES), F32),
            pltpu.VMEM((3, GW // HD, span, LANES), BF),
        ],
    )
    return pl.pallas_call(
        functools.partial(attend_back_kernel, keys),
        grid_spec=spec,
        out_shape=[jax.ShapeDtypeStruct(q.shape, F32), jax.ShapeDtypeStruct(kv.shape, BF)],
        compiler_params=params(axes=2),
        cost_estimate=pl.CostEstimate(
            flops=40 * rows * H * span * length * HD,
            bytes_accessed=rows * (length * 2560 + span * QW * 16),
            transcendentals=rows * H * span * length,
        ),
        name="attend_back",
    )(info, q, kv, start, do, ctx, rl)


def xor_of(a, b, n):
    total, bit = 0, 1
    while bit < n:
        total = total + bit * lax.rem(lax.div(a, bit) + lax.div(b, bit), 2)
        bit *= 2
    return total


def feed_kernel(
    n, live_ref, x_own, g_all, gu_ref, gut_ref, dt_ref, d_ref,
    x_all, hid_ref, dgu_ref, out_ref, flat_ref,
    x_buf, g_buf, terms, core, link, stage,
    x_send, x_recv, core_send, core_recv, link_send, link_recv, loads, keep,
):
    me = lax.axis_index("mp")
    rows, span, width = x_own.shape
    slots = gu_ref.shape[0]
    r, j = pl.program_id(0), pl.program_id(1)
    k = n - 1 - j
    now = r * n + j
    half = span // 2

    def gather(row):
        return Gather(
            n,
            me,
            lambda h: x_own.at[row, pl.ds(h * half, half)],
            lambda i, h: x_all.at[row, flip(me, i), pl.ds(h * half, half)],
            x_send.at[row],
            x_recv.at[row],
        )

    def scatter(row):
        return Scatter(
            n,
            me,
            lambda ref, h: ref.at[pl.ds(h * half, half)],
            lambda i: core.at[row, i],
            lambda h, i: link.at[row, h, i],
            lambda i: stage.at[i],
            (core_send.at[row], core_recv.at[row], link_send.at[row], link_recv.at[row]),
        )

    def load(step):
        row, slot = lax.div(step, n), n - 1 - lax.rem(step, n)
        block = xor_of(me, slot, n)
        to = lax.rem(step, 2)
        return (
            pltpu.make_async_copy(x_all.at[row, block], x_buf.at[to], loads.at[0, to]),
            pltpu.make_async_copy(g_all.at[row, block], g_buf.at[to], loads.at[1, to]),
        )

    def own_copy(row):
        return pltpu.make_async_copy(x_own.at[row], x_all.at[row, me], keep.at[row])

    @pl.when(now == 0)
    def _():
        greet(n, me)
        for row in range(rows):
            own_copy(row).start()
        first = gather(0)
        first.start()
        for i, h in first.even:
            first.forward(i, h)
            if (i, h) == first.even[len(first.even) // 2]:
                for row in range(1, rows):
                    gather(row).start()
        first.rest()
        for row in range(rows):
            own_copy(row).wait()
        for c in load(0):
            c.start()

    for row in range(1, rows):
        events = gather(row).even
        for at in range(1, n - 1):
            todo = [e for i, e in enumerate(events) if 1 + i * (n - 2) // len(events) == at]
            if todo:

                @pl.when(now == (row - 1) * n + at)
                def _(todo=todo, row=row):
                    for i, h in todo:
                        gather(row).forward(i, h)

        @pl.when(now == row * n - 1)
        def _(row=row):
            gather(row).rest()

    @pl.when(now + 1 < rows * n)
    def _():
        for c in load(now + 1):
            c.start()

    for c in load(now):
        c.wait()
    to = lax.rem(now, 2)
    x, g = x_buf.at[to], g_buf.at[to]
    grad = mm(g[...], dt_ref[...])
    for t in range(slots):
        both = mm(x[...], gu_ref[t])
        gate, upper = both[:, :TILE], both[:, TILE:]
        live = live_ref[t]
        sig = jax.nn.sigmoid(gate)
        silu = gate * sig
        gh = grad[:, t * TILE : (t + 1) * TILE] * live
        hid_ref[0, 0, :, t * TILE : (t + 1) * TILE] = (silu * upper * live).astype(BF)
        dgu_ref[0, 0, :, 2 * t * TILE : (2 * t + 1) * TILE] = (
            gh * upper * (sig * (1.0 + gate * (1.0 - sig)))
        ).astype(BF)
        dgu_ref[0, 0, :, (2 * t + 1) * TILE : (2 * t + 2) * TILE] = (gh * silu).astype(BF)

    for i in range(1, n, 2):

        @pl.when((r > 0) & (k == i))
        def _(i=i):
            scatter(r - 1).core_copy(i, terms.at[i // 2]).wait_send()

    at = lax.rem(k, 2) * lax.div(k, 2) + (1 - lax.rem(k, 2)) * (n // 2)
    terms[at] = mm(dgu_ref[0, 0], gut_ref[...]).astype(BF)
    out_ref[0, 0] = mm(hid_ref[0, 0], d_ref[...]).astype(BF)
    mine = terms.at[n // 2]
    sums = scatter(r)
    for i in range(1, n):

        @pl.when(k == i)
        def _(i=i):
            if i % 2:
                sums.odd(i, terms.at[i // 2])
            else:

                @pl.when(r > 0)
                def _():
                    for h in (0, 1):
                        scatter(r - 1).link_copy(i, h).wait_send()

                sums.even(i, mine)

    @pl.when(k == 0)
    def _():
        sums.core_copy(1, core.at[r, 0]).wait_recv()
        add_up(flat_ref.at[r], [mine, core.at[r, 0]])

    def close(row):
        last = scatter(row)
        for h in (0, 1):
            here = last.part(flat_ref.at[row], h)
            joined = [here]
            for i in last.addends(0, h):
                last.link_copy(i, h).wait_recv()
                joined.append(last.link(h, i // 2 - 1))
            add_up(here, joined)

    for row in range(rows - 1):

        @pl.when(now == (row + 1) * n + n // 2)
        def _(row=row):
            close(row)

    @pl.when(now == rows * n - 1)
    def _():
        close(rows - 1)
        scatter(rows - 1).drain(mine)
        for row in range(rows):
            gather(row).drain()


def feed(n, live, x, g, gu, gut, dt, d):
    rows, span, width = x.shape
    slots = gu.shape[0]
    vmem = pl.BlockSpec(memory_space=pltpu.VMEM)
    hbm = pl.BlockSpec(memory_space=pl.ANY)

    def place(r, j):
        return (r, xor_of(lax.axis_index("mp"), n - 1 - j, n), 0, 0)

    half = span // 2
    return pl.pallas_call(
        functools.partial(feed_kernel, n),
        grid=(rows, n),
        in_specs=[pl.BlockSpec(memory_space=pltpu.SMEM), hbm, hbm, vmem, vmem, vmem, vmem],
        out_specs=[
            hbm,
            pl.BlockSpec((1, 1, span, slots * TILE), place),
            pl.BlockSpec((1, 1, span, 2 * slots * TILE), place),
            pl.BlockSpec((1, 1, span, width), place),
            vmem,
        ],
        out_shape=[
            jax.ShapeDtypeStruct((rows, n, span, width), BF),
            jax.ShapeDtypeStruct((rows, n, span, slots * TILE), BF),
            jax.ShapeDtypeStruct((rows, n, span, 2 * slots * TILE), BF),
            jax.ShapeDtypeStruct((rows, n, span, width), BF),
            jax.ShapeDtypeStruct((rows, span, width), F32),
        ],
        scratch_shapes=[
            pltpu.VMEM((2, span, width), BF),
            pltpu.VMEM((2, span, width), BF),
            pltpu.VMEM((n // 2 + 1, span, width), BF),
            pltpu.VMEM((rows, n // 2, span, width), BF),
            pltpu.VMEM((rows, 2, n // 2 - 1, half, width), BF),
            pltpu.VMEM((n // 2 - 1, span, width), BF),
            pltpu.SemaphoreType.DMA((rows, n, 2)),
            pltpu.SemaphoreType.DMA((rows, n, 2)),
            pltpu.SemaphoreType.DMA((rows, n // 2)),
            pltpu.SemaphoreType.DMA((rows, n // 2)),
            pltpu.SemaphoreType.DMA((rows, 2, n // 2 - 1)),
            pltpu.SemaphoreType.DMA((rows, 2, n // 2 - 1)),
            pltpu.SemaphoreType.DMA((2, 2)),
            pltpu.SemaphoreType.DMA((rows,)),
        ],
        compiler_params=params(mib=62, axes=2, key=1),
        cost_estimate=pl.CostEstimate(
            flops=2 * 9 * rows * n * span * slots * TILE * width,
            bytes_accessed=8 * rows * n * span * width + 12 * slots * TILE * width,
            transcendentals=rows * n * span * slots * TILE,
        ),
        name="feed",
    )(live, x, g, gu, gut, dt, d)


def weight_kernel(finish, a_ref, b_ref, o_ref, acc):
    k = pl.program_id(1)

    @pl.when(k == 0)
    def _():
        acc[...] = jnp.zeros_like(acc)

    acc[...] += dg(a_ref[...], b_ref[...], TN)

    @pl.when(k == pl.num_programs(1) - 1)
    def _():
        finish(o_ref, acc)


def weight_grad(left, right, block, stacked):
    tokens, lw = left.shape
    rw = right.shape[1]
    block = min(block, lw)
    step = 512
    if stacked:
        slots = rw // 256
        out_spec = pl.BlockSpec((slots, block, 256), lambda i, k: (0, i, 0))
        out_shape = jax.ShapeDtypeStruct((slots, lw, 256), BF)

        def finish(o_ref, acc):
            for t in range(slots):
                o_ref[t] = acc[:, t * 256 : (t + 1) * 256].astype(BF)
    else:
        out_spec = pl.BlockSpec((block, rw), lambda i, k: (i, 0))
        out_shape = jax.ShapeDtypeStruct((lw, rw), BF)

        def finish(o_ref, acc):
            o_ref[...] = acc[...].astype(BF)

    return pl.pallas_call(
        functools.partial(weight_kernel, finish),
        grid=(lw // block, tokens // step),
        in_specs=[
            pl.BlockSpec((step, block), lambda i, k: (k, i)),
            pl.BlockSpec((step, rw), lambda i, k: (k, 0)),
        ],
        out_specs=out_spec,
        out_shape=out_shape,
        scratch_shapes=[pltpu.VMEM((block, rw), F32)],
        compiler_params=params(axes=2),
        cost_estimate=pl.CostEstimate(
            flops=2 * tokens * lw * rw,
            bytes_accessed=2 * tokens * (lw + rw) + 2 * lw * rw,
            transcendentals=0,
        ),
        name="weight_grad",
    )(left, right)


def shards(
    n,
    hidden_in,
    doc_ids,
    tile_slot,
    attention_gain,
    query_gain,
    key_gain,
    attend_weight,
    output_weight,
    feed_gain,
    gate_up_slots,
    down_slots,
    out_grad,
):
    rows, span, width = hidden_in.shape
    length = doc_ids.shape[1]
    slots = gate_up_slots.shape[0]
    tokens = rows * span
    me = lax.axis_index("mp")
    offset = me * span

    kw = KVH * HD
    keys_w = attend_weight[:, QW : QW + kw].reshape(-1, KVH, HD)
    values_w = attend_weight[:, QW + kw :].reshape(-1, KVH, HD)
    attend_w = jnp.concatenate(
        [attend_weight[:, :QW], jnp.concatenate([keys_w, values_w], 2).reshape(-1, 2 * kw)], 1
    )
    starts = doc_starts(doc_ids)
    local_start = lax.dynamic_slice_in_dim(starts, offset, span, 1)
    local_pos = offset + jnp.arange(span, dtype=jnp.int32)[None] - local_start
    cos, sin = rotary_tables(local_pos.reshape(tokens))
    gq = jnp.tile(query_gain, 2)[None]
    gk = jnp.concatenate([key_gain, jnp.ones_like(key_gain)])[None]
    lane = jnp.arange(LANES) // HD
    ones = (lane[:, None] == lane[None, :]).astype(BF)
    key_block = min(512, length)
    info = jnp.stack(
        [
            jnp.full((rows,), me, jnp.int32),
            local_start[:, 0] // key_block,
            local_start[:, -1],
        ],
        1,
    ).astype(jnp.int32)
    start_col = jnp.broadcast_to(local_start[:, :, None], (rows, span, LANES))
    start_row = jnp.broadcast_to(local_start[:, None, :], (rows, 8, span))

    x_own = hidden_in.reshape(tokens, width)
    x_value = x_own.astype(F32)
    scale_a = rms_scale(x_value)
    normed_ab, raw, q, attend_all, kv_all = project(
        n, rows, x_own, attention_gain[None], attend_w, cos, sin, gq, gk, ones
    )
    q = q.reshape(rows, span, QW)
    kv_all = kv_all.reshape(rows, length, -1)
    attend_full = attend_all.reshape(width, -1)
    output_full = lax.all_gather(output_weight, "mp", axis=0, tiled=True)
    out_grad_now, output_full = lax.optimization_barrier((out_grad, output_full))
    grads_all = lax.all_gather(out_grad_now.astype(BF), "mp", axis=1, tiled=True)
    ctx, rl = attend(info, q, kv_all, start_col)
    context_b = ctx.reshape(tokens, QW)
    middle = x_value + mm(context_b, output_full)
    scale_f = rms_scale(middle)
    normed_fb = (middle * scale_f * feed_gain).astype(BF).reshape(rows, span, width)

    slot_index = me * slots + jnp.arange(slots, dtype=jnp.int32)
    live = jnp.any(tile_slot[None, :] == slot_index[:, None], axis=1).astype(F32)
    gu_t = jnp.swapaxes(gate_up_slots, 1, 2).reshape(slots * 2 * TILE, width)
    d_flat = down_slots.reshape(slots * TILE, width)
    d_t = d_flat.T
    everything = rows * n * span
    normed_all, hidden, grad_both, partial_out, grad_normed_f = feed(
        n,
        live,
        normed_fb,
        grads_all.reshape(rows, n, span, width),
        gate_up_slots,
        gu_t,
        d_t,
        d_flat,
    )
    grad_gate_up = weight_grad(
        normed_all.reshape(everything, width), grad_both.reshape(everything, -1), 1024, True
    )
    grad_down = weight_grad(
        hidden.reshape(everything, -1), grads_all.reshape(everything, width), 768, False
    ).reshape(slots, TILE, width)
    ffn_out = lax.psum_scatter(
        partial_out.reshape(rows, length, width), "mp", scatter_dimension=1, tiled=True
    )
    gate_up_total, down_total = lax.psum((grad_gate_up, grad_down), "dp")
    grad_normed_f = grad_normed_f.reshape(tokens, width)

    weighted = grad_normed_f * feed_gain
    inner = jnp.mean(weighted * middle, axis=-1, keepdims=True)
    gain_feed = jnp.sum(grad_normed_f * middle * scale_f, axis=0)
    grad_middle = out_grad.reshape(tokens, width) + scale_f * (
        weighted - middle * scale_f * scale_f * inner
    )
    grad_attn_b = grad_middle.astype(BF)
    grad_context = dg(grad_attn_b, output_full, NT).astype(BF).reshape(rows, span, QW)
    grad_output = dg(context_b, grad_attn_b, TN).astype(BF)

    dq, dkv = attend_back(info, q, kv_all, start_row, grad_context, ctx, rl)
    layer_out = middle + ffn_out.reshape(tokens, width).astype(F32)
    grad_joined_b, sum_q, sum_k, attend_share, output_share = unproject(
        n,
        dq.reshape(tokens, QW),
        dkv.reshape(rows, n, span, -1),
        raw,
        cos,
        sin,
        gq,
        gk,
        ones,
        normed_ab,
        grad_output.reshape(n, -1, width),
    )
    grad_normed_a = dg(grad_joined_b, attend_full, NT)

    attend_share, output_share, gate_up_total, down_total = lax.optimization_barrier(
        (attend_share, output_share, gate_up_total, down_total)
    )
    attend_total, output_total = lax.psum((attend_share, output_share), "dp")
    attend_total = attend_total.astype(F32)
    kv_total = attend_total[:, QW:].reshape(-1, KVH, 2, HD)
    attend_total = jnp.concatenate(
        [
            attend_total[:, :QW],
            kv_total[:, :, 0].reshape(-1, kw),
            kv_total[:, :, 1].reshape(-1, kw),
        ],
        1,
    )
    weighted_a = grad_normed_a * attention_gain
    inner_a = jnp.mean(weighted_a * x_value, axis=-1, keepdims=True)
    gain_attention = jnp.sum(grad_normed_a * x_value * scale_a, axis=0)
    input_grad = grad_middle + scale_a * (weighted_a - x_value * scale_a * scale_a * inner_a)

    gains = jnp.concatenate([gain_attention, gain_feed, sum_q[0], sum_k[0]])
    gains = lax.psum(gains, ("dp", "mp"))
    gain_query = gains[2 * width : 2 * width + HD] + gains[2 * width + HD : 2 * width + 2 * HD]
    gain_key = gains[2 * width + LANES : 2 * width + LANES + HD]
    shape = (rows, span, width)
    return (
        layer_out.reshape(shape),
        input_grad.reshape(shape),
        attend_total,
        output_total.astype(F32),
        gate_up_total.astype(F32),
        down_total.astype(F32),
        gains[:width],
        gain_query,
        gain_key,
        gains[width : 2 * width],
    )


def solution(mesh):
    placed = (
        P("dp", "mp", None),
        P("dp", None),
        P(),
        P(),
        P(),
        P(),
        P("mp", None),
        P("mp", None),
        P(),
        P("mp", None, None),
        P("mp", None, None),
        P("dp", "mp", None),
    )
    return jax.shard_map(
        functools.partial(shards, mesh.shape["mp"]),
        mesh=mesh,
        in_specs=placed,
        out_specs=(
            P("dp", "mp", None),
            P("dp", "mp", None),
            P("mp", None),
            P("mp", None),
            P("mp", None, None),
            P("mp", None, None),
            P(),
            P(),
            P(),
            P(),
        ),
        check_vma=False,
    )
```

time: 1600 us -> 982 us (0.61)
  waiting for transfers between devices: 893 us -> 232 us
  Pallas kernels: 0 us -> 588 us
  matrix products: 409 us -> 26.3 us
  other arithmetic: 161 us -> 42.5 us
  local copies, waits for them, and re-layouts: 71.4 us -> 27.6 us
    pallas_call x0 -> x7, Pallas kernels: none -> 588 us  [the longest x1 222 us: feed(): pl.pallas_call(functools.partial(feed_kernel, n), grid=(rows, n), in_spec...]
    dot_general x18 -> x4, matrix products: 409 us -> 26.3 us  [the longest x3 22 us: dg(): return lax.dot_general(a, b, dims, preferred_element_type=F32)]
    reduce_scatter x6 -> x1, waiting for transfers between devices: 361 us -> 51.1 us  [shards(): lax.psum_scatter(partial_out.reshape(rows, length, width), 'mp', scatter_...]
    psum x1 -> x2, waiting for transfers between devices: 321 us -> 135 us  [the longest x1 131 us: shards(): gate_up_total, down_total = lax.psum((grad_gate_up, grad_down), 'dp')]
    all_gather x6 -> x2, waiting for transfers between devices: 209 us -> 45.8 us  [the longest x1 45.8 us: shards(): output_full = lax.all_gather(output_weight, 'mp', axis=0, tiled=True)]
    convert_element_type x11 -> x7, other arithmetic: 93.3 us -> 17.5 us  [the longest x1 5.92 us: shards(): gate_up_total.astype(F32)]
    reduce_sum x9 -> x2, other arithmetic: 46.4 us -> 5.27 us  [the longest x1 4.79 us: shards(): gain_feed = jnp.sum(grad_normed_f * middle * scale_f, axis=0)]
  transfers between devices with their start and end apart: 13 -> 5, of which waited for: 8 -> 4; matrix products, arithmetic and copies ran while one was open for 23% -> 9% of each run, Pallas kernels for 0% -> 38%
where the time goes in v1:
time: 982 us; the launch traced here: 973 us
  Pallas kernels  588 us (60%)
  waiting for transfers between devices  232 us (24%)
  other arithmetic  42.5 us (4%)
  blocking collectives  40.8 us (4%)
  local copies, waits for them, and re-layouts  27.6 us (3%)
  matrix products  26.3 us (3%)
  between operations  14.6 us (1%)
    pallas_call x1, Pallas kernels, feed(): pl.pallas_call(functools.partial(feed_kernel, n), grid=(rows, n), in_spec...  222 us
    pallas_call x1, Pallas kernels, unproject(): pl.pallas_call(functools.partial(unproject_kernel, n), in_specs=[vmem] *...  151 us
    psum x1, waiting for transfers between devices, shards(): gate_up_total, down_total = lax.psum((grad_gate_up, grad_down), 'dp')  131 us
    pallas_call x1, Pallas kernels, project(): pl.pallas_call(functools.partial(project_kernel, n), in_specs=[vmem, vmem...  115 us
    pallas_call x2, Pallas kernels, weight_grad(): pl.pallas_call(functools.partial(weight_kernel, finish), grid=(lw // bloc...  57.5 us
    reduce_scatter x1, waiting for transfers between devices, shards(): lax.psum_scatter(partial_out.reshape(rows, length, width), 'mp', scatter_...  51.1 us
    all_gather x1, waiting for transfers between devices, shards(): output_full = lax.all_gather(output_weight, 'mp', axis=0, tiled=True)  45.8 us
    psum x1, blocking collectives, shards(): gains = lax.psum(gains, ('dp', 'mp'))  40.8 us
  transfers between devices with their start and end apart: 5, of which 4 were waited for; matrix products, arithmetic and copies ran while one was open for 9% of the time, Pallas kernels for 38%

profile of v1, /device:TPU:0, one launch (start us, length us, event | category | flops | bytes accessed | tf_op | source)
XLA Modules:
  0.0 972.7 jit_solution(10636453173728110893)
XLA Ops:
  8.0 45.8 %all-gather.3.cloned.1.call-done = bf16[1280,2048]{1,0:T(8,128)(2,1)} async-done(((bf16[160,2048]{1,0:T(8,128)(2,1)}), bf16[1280,2048]{1,0:T(8,128)(2,1)}) %all-gather.3.cloned.1.call-update) | async-done | bytes 5242896 | tf_op jit(solution)/shard_map/all_gather | solution.py:1064
  53.7 3.9 convert_element_type.63
  64.0 9.6 copy.41
  73.6 2.8 copy.42.dt_ref
  77.6 2.1 pad_maximum_fusion.w_ref
  79.7 115.3 %project.1 = (bf16[512,2048]{1,0:T(8,128)(2,1)}, f32[512,1920]{1,0:T(8,128)}, bf16[512,1280]{1,0:T(8,128)(2,1)}, bf16[8,256,1920]{2,1,0:T(8,128)(2,1)}, bf16[2,8,256,640]{3,2,1,0:T(8,128)(2,1)}) custom-call(bf16[512,2048]{1,0:T(8,128)(2,1)} %bitcast.82, f32[1,2048]{1,0:T(1,128)} %bitcast.107, bf16[256,1920]{1,0:T(8,128)(2,1)} %pad_maximum_fusion.w_ref, ...), custom_call_target="tpu_custom_call" | custom-call | tf_op jit(solution)/shard_map/project/pallas_call | solution.py:394
  196.6 16.3 %attend.1 = (bf16[2,256,1280]{2,1,0:T(8,128)(2,1)}, f32[2,256,1280]{2,1,0:T(8,128)}) custom-call(s32[2,3]{1,0:T(2,128)} %pad_add_fusion.info, bf16[2,256,1280]{2,1,0:T(8,128)(2,1)} %bitcast.121, bf16[2,2048,640]{2,1,0:T(8,128)(2,1)} %bitcast.119, s32[2,256,128]{2,1,0:T(8,128)} %broadcast_in_dim.20.start_ref), custom_call_target="tpu_custom_call" | custom-call | flops 21474836480 | bytes 10485760 | tf_op jit(solution)/shard_map/attend/pallas_call | solution.py:608
  213.0 4.3 multiply_reduce_fusion.2
  217.4 2.0 copy-done
  219.4 1.7 multiply_convert_fusion
  221.1 221.8 %feed.1 = (bf16[2,8,256,2048]{3,2,1,0:T(8,128)(2,1)}, bf16[2,8,256,768]{3,2,1,0:T(8,128)(2,1)}, bf16[2,8,256,1536]{3,2,1,0:T(8,128)(2,1)}, bf16[2,8,256,2048]{3,2,1,0:T(8,128)(2,1)}, f32[2,256,2048]{2,1,0:T(8,128)}) custom-call(f32[6]{0:T(128)} %convert_element_type.61.live_ref, bf16[2,256,2048]{2,1,0:T(8,128)(2,1)} %bitcast.98, ...), custom_call_target="tpu_custom_call" | custom-call | flops 115964116992 | bytes 85983232 | tf_op jit(solution)/shard_map/feed/pallas_call | solution.py:909
  443.0 20.9 %weight_grad.3 = bf16[768,2048]{1,0:T(8,128)(2,1)} custom-call(bf16[4096,768]{1,0:T(8,128)(2,1)} %bitcast.125, bf16[4096,2048]{1,0:T(8,128)(2,1)} %bitcast.115), custom_call_target="tpu_custom_call" | custom-call | flops 12884901888 | bytes 26214400 | tf_op jit(solution)/shard_map/weight_grad/pallas_call | solution.py:987
  463.9 36.6 %weight_grad.2 = bf16[6,2048,256]{2,1,0:T(8,128)(2,1)} custom-call(bf16[4096,2048]{1,0:T(8,128)(2,1)} %bitcast.123, bf16[4096,1536]{1,0:T(8,128)(2,1)} %bitcast.124), custom_call_target="tpu_custom_call" | custom-call | flops 25769803776 | bytes 35651584 | tf_op jit(solution)/shard_map/weight_grad/pallas_call | solution.py:987
  500.6 1.5 copy-done.2
  502.6 4.8 fusion.9
  507.4 51.1 %reduce-scatter.2.cloned.1.call-done = bf16[2,256,2048]{2,1,0:T(8,128)(2,1)} async-done(((bf16[2,2048,2048]{2,1,0:T(8,128)(2,1)}), bf16[2,256,2048]{2,1,0:T(8,128)(2,1)}) %reduce-scatter.2.cloned.1.call-update) | async-done | bytes 2097168 | tf_op jit(solution)/shard_map/reduce_scatter | solution.py:1095
  558.5 7.9 bitcast_add_fusion
  566.3 4.7 convolution_convert_fusion
  571.0 6.5 convolution_convert_fusion.1
  578.1 26.8 %attend_back.1 = (f32[2,256,1280]{2,1,0:T(8,128)}, bf16[2,2048,640]{2,1,0:T(8,128)(2,1)}) custom-call(s32[2,3]{1,0:T(2,128)} %pad_add_fusion.info, bf16[2,256,1280]{2,1,0:T(8,128)(2,1)} %bitcast.122, bf16[2,2048,640]{2,1,0:T(8,128)(2,1)} %bitcast.120, s32[2,8,256]{2,1,0:T(8,128)} %broadcast_in_dim.21.start_ref, bf16[2,256,1280]{2,1,0:T(8,128)(2,1)} %bitcast.128, ...), custom_call_target="tpu_custom_call" | custom-call | flops 53687091200 | bytes 20971520 | tf_op jit(solution)/shard_map/attend_back/pallas_call | solution.py:719
  604.9 150.7 %unproject.1 = (bf16[512,1920]{1,0:T(8,128)(2,1)}, f32[8,128]{1,0:T(8,128)}, f32[8,128]{1,0:T(8,128)}, bf16[256,1920]{1,0:T(8,128)(2,1)}, bf16[160,2048]{1,0:T(8,128)(2,1)}) custom-call(f32[512,1280]{1,0:T(8,128)} %bitcast.96, bf16[2,8,256,640]{3,2,1,0:T(8,128)(2,1)} %bitcast.90, f32[512,1920]{1,0:T(8,128)} %get-tuple-element.45.raw_ref, ...), custom_call_target="tpu_custom_call" | custom-call | tf_op jit(solution)/shard_map/unproject/pallas_call | solution.py:521
  755.6 131.2 %all-reduce.9.cloned.1.call-done = (bf16[6,2048,256]{2,1,0:T(8,128)(2,1)}, bf16[6,128,2048]{2,1,0:T(8,128)(2,1)}) async-done(((bf16[6,2048,256]{2,1,0:T(8,128)(2,1)}, bf16[6,128,2048]{2,1,0:T(8,128)(2,1)}), (bf16[6,2048,256]{2,1,0:T(8,128)(2,1)}, bf16[6,128,2048]{2,1,0:T(8,128)(2,1)})) %all-reduce.9.cloned.1.call-update) | async-done | bytes 9437200 | tf_op jit(solution)/shard_map/psum | solution.py:1098
  886.9 10.8 %fusion.7 = (f32[2048]{0:T(1024)S(1)}, f32[512]{0:T(512)S(1)}, f32[512,2048]{1,0:T(8,128)}) fusion(f32[512]{0:T(512)S(1)} %bitcast.111, bf16[2,256,2048]{2,1,0:T(8,128)(2,1)S(1)} %copy-done.2, f32[2048]{0:T(1024)S(1)} %copy-done.11, bf16[512,1920]{1,0:T(8,128)(2,1)} %get-tuple-element.47, bf16[2048,1920]{1,0:T(8,128)(2,1)} %bitcast.116), kind=kOutput, calls=%fused_computation.12 | convolution fusion | flops 4033869312 | bytes 16142336 | tf_op jit(solution)/shard_map/dot_general | solution.py:45
  898.4 5.9 convert_element_type.72
  904.4 3.5 convert_element_type.73
  907.9 40.8 %psum.39 = f32[4352]{0:T(1024)S(1)} all-reduce(f32[4352]{0:T(1024)S(1)} %pad_maximum_fusion.2), channel_id=1, replica_groups=mesh['dp'=4,'mp'=8] {'dp','mp'}, use_global_device_ids=true, to_apply=%region_14.15 | all-reduce | flops 4352 | bytes 34816 | tf_op jit(solution)/shard_map/psum | solution.py:1148
  949.9 6.7 fusion.4
  956.6 3.5 all-reduce.7.cloned.1.call-done
  960.1 1.1 slice.82
  961.2 1.2 slice.81
  963.0 1.2 convert_element_type.71
  964.2 1.5 concatenate.22
  (109 shorter events, 13.5 us)
Async XLA Ops:
  7.2 46.6 %all-gather.3.cloned.1.call-start = ((), (), s32[]{:S(2)}) async-start(), calls=%async_computation.1 | async-start | bytes 5898240 | tf_op jit(solution)/shard_map/all_gather | solution.py:1064
  7.9 49.9 %copy-start.10 = (s32[2,2048]{1,0:T(2,128)S(1)}, s32[2,2048]{1,0:T(2,128)}, u32[]{:S(2)}) copy-start(s32[2,2048]{1,0:T(2,128)} %param.13) | copy-start | bytes 49156
  7.9 53.2 %copy-start.6 = (bf16[256,1920]{1,0:T(8,128)(2,1)S(1)}, bf16[256,1920]{1,0:T(8,128)(2,1)}, u32[]{:S(2)}) copy-start(bf16[256,1920]{1,0:T(8,128)(2,1)} %param.18) | copy-start | bytes 2949124
  7.9 213.2 %all-gather.5.cloned.1.call-start = ((), (), s32[]{:S(2)}) async-start(), calls=%async_computation.2 | async-start | bytes 18874368 | tf_op jit(solution)/shard_map/all_gather | solution.py:1066
  57.7 5.0 copy-start.16
  57.7 5.6 copy-start.17
  57.7 500.8 %reduce-scatter.2.cloned.1.call-start = ((), (), s32[]{:S(2)}) async-start(), calls=%async_computation.3 | async-start | bytes 18874368 | tf_op jit(solution)/shard_map/reduce_scatter | solution.py:1095
  59.1 136.7 %copy-start.14 = (s32[2,256]{1,0:T(2,128)}, s32[2,256]{1,0:T(2,128)S(1)}, u32[]{:S(2)}) copy-start(s32[2,256]{1,0:T(2,128)S(1)} %get-tuple-element.69) | copy-start | bytes 6148
  64.0 9.6 copy-start.4
  73.6 2.8 copy-start.18
  79.7 133.3 %slice-start.2 = ((s8[5242880]{0:T(1024)(128)(4,1)}), s8[4194304]{0:T(1024)(128)(4,1)S(1)}, s32[]{:S(2)}) async-start(s8[5242880]{0:T(1024)(128)(4,1)} %bitcast.117), calls=%async_computation.8 | async-start | bytes 8388608
  196.6 16.4 %copy-start.1 = (bf16[2,256,2048]{2,1,0:T(8,128)(2,1)S(1)}, bf16[2,256,2048]{2,1,0:T(8,128)(2,1)}, u32[]{:S(2)}) copy-start(bf16[2,256,2048]{2,1,0:T(8,128)(2,1)} %param.12) | copy-start | bytes 6291460
  196.6 16.4 %slice-start.3 = ((s8[5242880]{0:T(1024)(128)(4,1)}), s8[1048576]{0:T(1024)(128)(4,1)S(1)}, s32[]{:S(2)}) async-start(s8[5242880]{0:T(1024)(128)(4,1)} %bitcast.117), calls=%async_computation.9 | async-start | bytes 2097152
  213.0 6.4 copy-start.8
  217.4 2.0 copy-start
  217.4 2.0 copy-start.12
  443.0 443.9 %all-reduce.9.cloned.1.call-start = ((), (), s32[]{:S(2)}) async-start(), calls=%async_computation.5 | async-start | bytes 18874368 | tf_op jit(solution)/shard_map/psum | solution.py:1098
  500.5 1.6 copy-start.2
  500.5 2.1 copy-start.9
  500.5 2.1 copy-start.13
  500.5 459.6 %all-reduce.7.cloned.1.call-start = ((), (), s32[]{:S(2)}) async-start(), calls=%async_computation.4 | async-start | bytes 3276800 | tf_op jit(solution)/shard_map/psum | solution.py:1131
  507.4 58.9 %copy-start.19 = (bf16[2,256,1280]{2,1,0:T(8,128)(2,1)S(1)}, bf16[2,256,1280]{2,1,0:T(8,128)(2,1)}, u32[]{:S(2)}) copy-start(bf16[2,256,1280]{2,1,0:T(8,128)(2,1)} %get-tuple-element.37.ctx_ref) | copy-start | bytes 3932164
  566.3 4.7 copy-start.3
  571.0 6.5 copy-start.15
  604.9 282.0 %copy-start.11 = (f32[2048]{0:T(1024)S(1)}, f32[2048]{0:T(1024)}, u32[]{:S(2)}) copy-start(f32[2048]{0:T(1024)} %param.15) | copy-start | bytes 24580
  886.9 11.5 %slice-start = ((s8[6291456]{0:T(1024)(128)(4,1)}), s8[4194304]{0:T(1024)(128)(4,1)S(1)}, s32[]{:S(2)}) async-start(s8[6291456]{0:T(1024)(128)(4,1)} %bitcast.87), calls=%async_computation.6 | async-start | bytes 8388608
  886.9 11.5 %slice-start.1 = ((s8[6291456]{0:T(1024)(128)(4,1)}), s8[2097152]{0:T(1024)(128)(4,1)S(1)}, s32[]{:S(2)}) async-start(s8[6291456]{0:T(1024)(128)(4,1)} %bitcast.87), calls=%async_computation.7 | async-start | bytes 4194304
  898.4 5.9 copy-start.5
  960.1 2.9 copy-start.7
Sparse Core Ops, SparseCore 0:
  9.9 43.8 all-gather.2
  57.8 134.9 all-gather.4
  443.1 115.3 reduce-scatter.1
  561.5 325.3 all-reduce.8
  889.2 70.8 all-reduce.6

commit v2 on v1

--- a/solution.py
+++ b/solution.py
@@ -90,8 +90,9 @@
 
 
 class Gather:
-    def __init__(self, n, me, own, slot, send, recv):
+    def __init__(self, n, me, own, slot, send, recv, relative=False):
         self.n, self.me, self.own, self.slot, self.send, self.recv = n, me, own, slot, send, recv
+        self.relative = relative
         bits = link_bits(n)
         self.order = (bits + [1], bits[::-1] + [1])
         even = [(k, h) for k in range(2, n, 2) for h in (0, 1)]
@@ -104,7 +105,7 @@
     def copy(self, k, half, bit):
         return pltpu.make_async_remote_copy(
             src_ref=self.own(half) if k == 0 else self.slot(k, half),
-            dst_ref=self.slot(k, half),
+            dst_ref=self.slot(k ^ bit if self.relative else k, half),
             send_sem=self.send.at[k ^ bit, half],
             recv_sem=self.recv.at[k ^ bit, half],
             device_id={"mp": flip(self.me, bit)},
@@ -268,9 +269,9 @@
 
 
 def project_kernel(
-    n, x_ref, gain_ref, w_ref, cos_ref, sin_ref, gq_ref, gk_ref, ones_ref,
-    normed_ref, raw_ref, q_ref, w_out, kv_out,
-    w_all, kv_own, w_send, w_recv, kv_send, kv_recv, local,
+    n, x_ref, gain_ref, w_ref, o_ref, cos_ref, sin_ref, gq_ref, gk_ref, ones_ref,
+    normed_ref, raw_ref, q_ref, w_out, kv_out, o_out,
+    w_all, kv_own, w_send, w_recv, kv_send, kv_recv, o_send, o_recv, local,
 ):
     me = lax.axis_index("mp")
     depth = w_ref.shape[0]
@@ -280,7 +281,18 @@
     half = depth // 2
     own_w = pltpu.make_async_copy(w_ref, w_all.at[me], local.at[0])
     own_w.start()
+    own_o = pltpu.make_async_copy(o_ref, o_out.at[me], local.at[1 + rows])
+    own_o.start()
     greet(n, me)
+    wide = o_ref.shape[1] // 2
+    outs = Gather(
+        n,
+        me,
+        lambda h: o_ref.at[:, pl.ds(h * wide, wide)],
+        lambda k, h: o_out.at[flip(me, k), :, pl.ds(h * wide, wide)],
+        o_send,
+        o_recv,
+    )
     weights = Gather(
         n,
         me,
@@ -320,6 +332,7 @@
         weights.forward(k, h)
         if any(k == other for other, _ in weights.even[:i]):
             accumulate(k, False)
+    outs.start()
     for k in range(3, n, 2):
         for h in (0, 1):
             weights.arrive(k, h)
@@ -376,16 +389,20 @@
         finish(i, range(QW // LANES))
 
     for k, h in kvs.even:
+        outs.forward(k, h)
         kvs.forward(k, h)
+    outs.rest()
     kvs.rest()
     for c in keep:
         c.wait()
     out_w.wait()
+    own_o.wait()
     weights.drain()
+    outs.drain()
     kvs.drain()
 
 
-def project(n, rows, x, gain, w, cos, sin, gq, gk, ones):
+def project(n, rows, x, gain, w, o, cos, sin, gq, gk, ones):
     tokens, width = x.shape
     depth, columns = w.shape
     vmem = pl.BlockSpec(memory_space=pltpu.VMEM)
@@ -393,14 +410,15 @@
     kvw = columns - QW
     return pl.pallas_call(
         functools.partial(project_kernel, n),
-        in_specs=[vmem, vmem, hbm, vmem, vmem, vmem, vmem, vmem],
-        out_specs=[vmem, vmem, vmem, hbm, hbm],
+        in_specs=[vmem, vmem, hbm, hbm, vmem, vmem, vmem, vmem, vmem],
+        out_specs=[vmem, vmem, vmem, hbm, hbm, hbm],
         out_shape=[
             jax.ShapeDtypeStruct((tokens, width), BF),
             jax.ShapeDtypeStruct((tokens, columns), F32),
             jax.ShapeDtypeStruct((tokens, QW), BF),
             jax.ShapeDtypeStruct((n, depth, columns), BF),
             jax.ShapeDtypeStruct((rows, n, tokens // rows, kvw), BF),
+            jax.ShapeDtypeStruct((n,) + o.shape, BF),
         ],
         scratch_shapes=[
             pltpu.VMEM((n, depth, columns), BF),
@@ -409,11 +427,13 @@
             pltpu.SemaphoreType.DMA((n, 2)),
             pltpu.SemaphoreType.DMA((n, 2)),
             pltpu.SemaphoreType.DMA((n, 2)),
-            pltpu.SemaphoreType.DMA((1 + rows,)),
+            pltpu.SemaphoreType.DMA((n, 2)),
+            pltpu.SemaphoreType.DMA((n, 2)),
+            pltpu.SemaphoreType.DMA((2 + rows,)),
         ],
         compiler_params=params(axes=0, key=0),
         name="project",
-    )(x, gain, w, cos, sin, gq, gk, ones)
+    )(x, gain, w, o, cos, sin, gq, gk, ones)
 
 
 def unproject_kernel(
@@ -739,16 +759,14 @@
 
 
 def feed_kernel(
-    n, live_ref, x_own, g_all, gu_ref, gut_ref, dt_ref, d_ref,
-    x_all, hid_ref, dgu_ref, out_ref, flat_ref,
-    x_buf, g_buf, terms, core, link, stage,
-    x_send, x_recv, core_send, core_recv, link_send, link_recv, loads, keep,
+    n, live_ref, x_own, g_ref, gu_any, dt_any,
+    x_all, hid_ref, dgu_ref,
+    x_vm, gu_ref, dt_ref, x_send, x_recv, loads, keep,
 ):
     me = lax.axis_index("mp")
     rows, span, width = x_own.shape
     slots = gu_ref.shape[0]
     r, j = pl.program_id(0), pl.program_id(1)
-    k = n - 1 - j
     now = r * n + j
     half = span // 2
 
@@ -757,77 +775,63 @@
             n,
             me,
             lambda h: x_own.at[row, pl.ds(h * half, half)],
-            lambda i, h: x_all.at[row, flip(me, i), pl.ds(h * half, half)],
+            lambda i, h: x_vm.at[row, i, pl.ds(h * half, half)],
             x_send.at[row],
             x_recv.at[row],
+            True,
         )
 
-    def scatter(row):
-        return Scatter(
-            n,
-            me,
-            lambda ref, h: ref.at[pl.ds(h * half, half)],
-            lambda i: core.at[row, i],
-            lambda h, i: link.at[row, h, i],
-            lambda i: stage.at[i],
-            (core_send.at[row], core_recv.at[row], link_send.at[row], link_recv.at[row]),
-        )
-
-    def load(step):
-        row, slot = lax.div(step, n), n - 1 - lax.rem(step, n)
+    def store(row, slot):
         block = xor_of(me, slot, n)
-        to = lax.rem(step, 2)
-        return (
-            pltpu.make_async_copy(x_all.at[row, block], x_buf.at[to], loads.at[0, to]),
-            pltpu.make_async_copy(g_all.at[row, block], g_buf.at[to], loads.at[1, to]),
-        )
+        return pltpu.make_async_copy(x_vm.at[row, slot], x_all.at[row, block], keep.at[row, slot])
+
+    fetch = [
+        pltpu.make_async_copy(gu_any, gu_ref, loads.at[0]),
+        pltpu.make_async_copy(dt_any, dt_ref, loads.at[1]),
+    ]
 
     def own_copy(row):
-        return pltpu.make_async_copy(x_own.at[row], x_all.at[row, me], keep.at[row])
+        return pltpu.make_async_copy(x_own.at[row], x_vm.at[row, 0], loads.at[2 + row])
+
+    def events(row, upto):
+        todo = gather(row).even
+        ends = [0] * n
+        for k in range(2, n):
+            ends[k] = ends[k - 1]
+            if k % 2 == 0:
+                ends[k] = max(ends[k - 1], 1 + max(i for i, e in enumerate(todo) if e[0] == k))
+        return todo[ends[upto - 1] if upto else 0 : ends[upto]]
 
     @pl.when(now == 0)
     def _():
-        greet(n, me)
         for row in range(rows):
             own_copy(row).start()
-        first = gather(0)
-        first.start()
-        for i, h in first.even:
-            first.forward(i, h)
-            if (i, h) == first.even[len(first.even) // 2]:
-                for row in range(1, rows):
-                    gather(row).start()
-        first.rest()
-        for row in range(rows):
-            own_copy(row).wait()
-        for c in load(0):
+        for c in fetch:
             c.start()
-
-    for row in range(1, rows):
-        events = gather(row).even
-        for at in range(1, n - 1):
-            todo = [e for i, e in enumerate(events) if 1 + i * (n - 2) // len(events) == at]
-            if todo:
-
-                @pl.when(now == (row - 1) * n + at)
-                def _(todo=todo, row=row):
-                    for i, h in todo:
-                        gather(row).forward(i, h)
-
-        @pl.when(now == row * n - 1)
-        def _(row=row):
-            gather(row).rest()
-
-    @pl.when(now + 1 < rows * n)
-    def _():
-        for c in load(now + 1):
-            c.start()
-
-    for c in load(now):
-        c.wait()
-    to = lax.rem(now, 2)
-    x, g = x_buf.at[to], g_buf.at[to]
-    grad = mm(g[...], dt_ref[...])
+        greet(n, me)
+        gather(0).start()
+        own_copy(0).wait()
+        for c in fetch:
+            c.wait()
+
+    for row in range(rows):
+        for k in range(n):
+
+            @pl.when(now == row * n + k)
+            def _(row=row, k=k):
+                if k == 0 and row:
+                    own_copy(row).wait()
+                for i, e in enumerate(events(row, k)):
+                    gather(row).forward(*e)
+                    if row + 1 < rows and k == 2 and i == 1:
+                        gather(row + 1).start()
+                if k % 2:
+                    for h in (0, 1):
+                        gather(row).arrive(k, h)
+
+    store(r, j).start()
+    x = x_vm.at[r, j]
+    grad = mm(g_ref[0, 0], dt_ref[...])
     for t in range(slots):
         both = mm(x[...], gu_ref[t])
         gate, upper = both[:, :TILE], both[:, TILE:]
@@ -841,6 +845,90 @@
         ).astype(BF)
         dgu_ref[0, 0, :, (2 * t + 1) * TILE : (2 * t + 2) * TILE] = (gh * silu).astype(BF)
 
+    @pl.when(now == rows * n - 1)
+    def _():
+        for row in range(rows):
+            gather(row).drain()
+            for k in range(n):
+                store(row, k).wait()
+
+
+def feed(n, live, x, g, gu, dt):
+    rows, span, width = x.shape
+    slots = gu.shape[0]
+    hbm = pl.BlockSpec(memory_space=pl.ANY)
+
+    def place(r, j):
+        return (r, xor_of(lax.axis_index("mp"), j, n), 0, 0)
+
+    return pl.pallas_call(
+        functools.partial(feed_kernel, n),
+        grid=(rows, n),
+        in_specs=[
+            pl.BlockSpec(memory_space=pltpu.SMEM),
+            hbm,
+            pl.BlockSpec((1, 1, span, width), place),
+            hbm,
+            hbm,
+        ],
+        out_specs=[
+            hbm,
+            pl.BlockSpec((1, 1, span, slots * TILE), place),
+            pl.BlockSpec((1, 1, span, 2 * slots * TILE), place),
+        ],
+        out_shape=[
+            jax.ShapeDtypeStruct((rows, n, span, width), BF),
+            jax.ShapeDtypeStruct((rows, n, span, slots * TILE), BF),
+            jax.ShapeDtypeStruct((rows, n, span, 2 * slots * TILE), BF),
+        ],
+        scratch_shapes=[
+            pltpu.VMEM((rows, n, span, width), BF),
+            pltpu.VMEM(gu.shape, BF),
+            pltpu.VMEM(dt.shape, BF),
+            pltpu.SemaphoreType.DMA((rows, n, 2)),
+            pltpu.SemaphoreType.DMA((rows, n, 2)),
+            pltpu.SemaphoreType.DMA((2 + rows,)),
+            pltpu.SemaphoreType.DMA((rows, n)),
+        ],
+        compiler_params=params(mib=56, axes=2, key=1),
+        cost_estimate=pl.CostEstimate(
+            flops=2 * 3 * rows * n * span * slots * TILE * width,
+            bytes_accessed=6 * rows * n * span * width + 6 * slots * TILE * width,
+            transcendentals=rows * n * span * slots * TILE,
+        ),
+        name="feed",
+    )(live, x, g, gu, dt)
+
+
+def tile_sum_kernel(
+    n, a_ref, w_any, o_ref,
+    w_ref, terms, core, link, stage, core_send, core_recv, link_send, link_recv, load,
+):
+    me = lax.axis_index("mp")
+    rows, span, width = o_ref.shape
+    r, j = pl.program_id(0), pl.program_id(1)
+    k = n - 1 - j
+    now = r * n + j
+    half = span // 2
+
+    def scatter(row):
+        return Scatter(
+            n,
+            me,
+            lambda ref, h: ref.at[pl.ds(h * half, half)],
+            lambda i: core.at[row, i],
+            lambda h, i: link.at[row, h, i],
+            lambda i: stage.at[i],
+            (core_send.at[row], core_recv.at[row], link_send.at[row], link_recv.at[row]),
+        )
+
+    @pl.when(now == 0)
+    def _():
+        fetch = pltpu.make_async_copy(w_any, w_ref, load.at[0])
+        fetch.start()
+        greet(n, me)
+        fetch.wait()
+
     for i in range(1, n, 2):
 
         @pl.when((r > 0) & (k == i))
@@ -848,8 +936,7 @@
             scatter(r - 1).core_copy(i, terms.at[i // 2]).wait_send()
 
     at = lax.rem(k, 2) * lax.div(k, 2) + (1 - lax.rem(k, 2)) * (n // 2)
-    terms[at] = mm(dgu_ref[0, 0], gut_ref[...]).astype(BF)
-    out_ref[0, 0] = mm(hid_ref[0, 0], d_ref[...]).astype(BF)
+    terms[at] = mm(a_ref[0, 0], w_ref[...]).astype(BF)
     mine = terms.at[n // 2]
     sums = scatter(r)
     for i in range(1, n):
@@ -870,12 +957,12 @@
     @pl.when(k == 0)
     def _():
         sums.core_copy(1, core.at[r, 0]).wait_recv()
-        add_up(flat_ref.at[r], [mine, core.at[r, 0]])
+        add_up(o_ref.at[r], [mine, core.at[r, 0]])
 
     def close(row):
         last = scatter(row)
         for h in (0, 1):
-            here = last.part(flat_ref.at[row], h)
+            here = last.part(o_ref.at[row], h)
             joined = [here]
             for i in last.addends(0, h):
                 last.link_copy(i, h).wait_recv()
@@ -892,62 +979,42 @@
     def _():
         close(rows - 1)
         scatter(rows - 1).drain(mine)
-        for row in range(rows):
-            gather(row).drain()
-
-
-def feed(n, live, x, g, gu, gut, dt, d):
-    rows, span, width = x.shape
-    slots = gu.shape[0]
-    vmem = pl.BlockSpec(memory_space=pltpu.VMEM)
-    hbm = pl.BlockSpec(memory_space=pl.ANY)
+
+
+def tile_sum(n, a, w, key):
+    rows, _, span, depth = a.shape
+    width = w.shape[1]
+    half = span // 2
 
     def place(r, j):
         return (r, xor_of(lax.axis_index("mp"), n - 1 - j, n), 0, 0)
 
-    half = span // 2
     return pl.pallas_call(
-        functools.partial(feed_kernel, n),
+        functools.partial(tile_sum_kernel, n),
         grid=(rows, n),
-        in_specs=[pl.BlockSpec(memory_space=pltpu.SMEM), hbm, hbm, vmem, vmem, vmem, vmem],
-        out_specs=[
-            hbm,
-            pl.BlockSpec((1, 1, span, slots * TILE), place),
-            pl.BlockSpec((1, 1, span, 2 * slots * TILE), place),
-            pl.BlockSpec((1, 1, span, width), place),
-            vmem,
-        ],
-        out_shape=[
-            jax.ShapeDtypeStruct((rows, n, span, width), BF),
-            jax.ShapeDtypeStruct((rows, n, span, slots * TILE), BF),
-            jax.ShapeDtypeStruct((rows, n, span, 2 * slots * TILE), BF),
-            jax.ShapeDtypeStruct((rows, n, span, width), BF),
-            jax.ShapeDtypeStruct((rows, span, width), F32),
-        ],
+        in_specs=[pl.BlockSpec((1, 1, span, depth), place), pl.BlockSpec(memory_space=pl.ANY)],
+        out_specs=pl.BlockSpec(memory_space=pltpu.VMEM),
+        out_shape=jax.ShapeDtypeStruct((rows, span, width), F32),
         scratch_shapes=[
-            pltpu.VMEM((2, span, width), BF),
-            pltpu.VMEM((2, span, width), BF),
+            pltpu.VMEM(w.shape, BF),
             pltpu.VMEM((n // 2 + 1, span, width), BF),
             pltpu.VMEM((rows, n // 2, span, width), BF),
             pltpu.VMEM((rows, 2, n // 2 - 1, half, width), BF),
             pltpu.VMEM((n // 2 - 1, span, width), BF),
-            pltpu.SemaphoreType.DMA((rows, n, 2)),
-            pltpu.SemaphoreType.DMA((rows, n, 2)),
             pltpu.SemaphoreType.DMA((rows, n // 2)),
             pltpu.SemaphoreType.DMA((rows, n // 2)),
             pltpu.SemaphoreType.DMA((rows, 2, n // 2 - 1)),
             pltpu.SemaphoreType.DMA((rows, 2, n // 2 - 1)),
-            pltpu.SemaphoreType.DMA((2, 2)),
-            pltpu.SemaphoreType.DMA((rows,)),
-        ],
-        compiler_params=params(mib=62, axes=2, key=1),
+            pltpu.SemaphoreType.DMA((1,)),
+        ],
+        compiler_params=params(mib=56, axes=2, key=key),
         cost_estimate=pl.CostEstimate(
-            flops=2 * 9 * rows * n * span * slots * TILE * width,
-            bytes_accessed=8 * rows * n * span * width + 12 * slots * TILE * width,
-            transcendentals=rows * n * span * slots * TILE,
+            flops=2 * rows * n * span * depth * width,
+            bytes_accessed=2 * rows * n * span * depth + 2 * depth * width,
+            transcendentals=0,
         ),
-        name="feed",
-    )(live, x, g, gu, gut, dt, d)
+        name="tile_sum",
+    )(a, w)
 
 
 def weight_kernel(finish, a_ref, b_ref, o_ref, acc):
@@ -1055,15 +1122,15 @@
     x_own = hidden_in.reshape(tokens, width)
     x_value = x_own.astype(F32)
     scale_a = rms_scale(x_value)
-    normed_ab, raw, q, attend_all, kv_all = project(
-        n, rows, x_own, attention_gain[None], attend_w, cos, sin, gq, gk, ones
+    normed_ab, raw, q, attend_all, kv_all, output_all = project(
+        n, rows, x_own, attention_gain[None], attend_w, output_weight, cos, sin, gq, gk, ones
     )
     q = q.reshape(rows, span, QW)
     kv_all = kv_all.reshape(rows, length, -1)
     attend_full = attend_all.reshape(width, -1)
-    output_full = lax.all_gather(output_weight, "mp", axis=0, tiled=True)
-    out_grad_now, output_full = lax.optimization_barrier((out_grad, output_full))
-    grads_all = lax.all_gather(out_grad_now.astype(BF), "mp", axis=1, tiled=True)
+    output_full = output_all.reshape(QW, width)
+    grad_branch, output_full = lax.optimization_barrier((out_grad.astype(BF), output_full))
+    grads_all = lax.all_gather(grad_branch, "mp", axis=1, tiled=True)
     ctx, rl = attend(info, q, kv_all, start_col)
     context_b = ctx.reshape(tokens, QW)
     middle = x_value + mm(context_b, output_full)
@@ -1076,27 +1143,20 @@
     d_flat = down_slots.reshape(slots * TILE, width)
     d_t = d_flat.T
     everything = rows * n * span
-    normed_all, hidden, grad_both, partial_out, grad_normed_f = feed(
-        n,
-        live,
-        normed_fb,
-        grads_all.reshape(rows, n, span, width),
-        gate_up_slots,
-        gu_t,
-        d_t,
-        d_flat,
-    )
-    grad_gate_up = weight_grad(
-        normed_all.reshape(everything, width), grad_both.reshape(everything, -1), 1024, True
+    normed_all, hidden, grad_both = feed(
+        n, live, normed_fb, grads_all.reshape(rows, n, span, width), gate_up_slots, d_t
     )
     grad_down = weight_grad(
         hidden.reshape(everything, -1), grads_all.reshape(everything, width), 768, False
     ).reshape(slots, TILE, width)
-    ffn_out = lax.psum_scatter(
-        partial_out.reshape(rows, length, width), "mp", scatter_dimension=1, tiled=True
+    grad_gate_up = weight_grad(
+        normed_all.reshape(everything, width), grad_both.reshape(everything, -1), 1024, True
     )
     gate_up_total, down_total = lax.psum((grad_gate_up, grad_down), "dp")
-    grad_normed_f = grad_normed_f.reshape(tokens, width)
+    grad_both, grad_gate_up, grad_down = lax.optimization_barrier(
+        (grad_both, grad_gate_up, grad_down)
+    )
+    grad_normed_f = tile_sum(n, grad_both, gu_t, 3).reshape(tokens, width)
 
     weighted = grad_normed_f * feed_gain
     inner = jnp.mean(weighted * middle, axis=-1, keepdims=True)
@@ -1109,7 +1169,6 @@
     grad_output = dg(context_b, grad_attn_b, TN).astype(BF)
 
     dq, dkv = attend_back(info, q, kv_all, start_row, grad_context, ctx, rl)
-    layer_out = middle + ffn_out.reshape(tokens, width).astype(F32)
     grad_joined_b, sum_q, sum_k, attend_share, output_share = unproject(
         n,
         dq.reshape(tokens, QW),
@@ -1125,6 +1184,8 @@
     )
     grad_normed_a = dg(grad_joined_b, attend_full, NT)
 
+    hidden, attend_share = lax.optimization_barrier((hidden, attend_share))
+    layer_out = middle + tile_sum(n, hidden, d_flat, 4).reshape(tokens, width)
     attend_share, output_share, gate_up_total, down_total = lax.optimization_barrier(
         (attend_share, output_share, gate_up_total, down_total)
     )

time: 982 us -> 863 us (0.88)
  waiting for transfers between devices: 232 us -> 100 us
  Pallas kernels: 588 us -> 604 us
    pallas_call x0 -> x2, Pallas kernels: none -> 185 us  [tile_sum(): pl.pallas_call(functools.partial(tile_sum_kernel, n), grid=(rows, n), in_...]
    pallas_call x1, Pallas kernels: 222 us -> 82.3 us  [feed(): pl.pallas_call(functools.partial(feed_kernel, n), grid=(rows, n), in_spec...]
    psum x1, waiting for transfers between devices: 131 us -> 0.02 us  [shards(): gate_up_total, down_total = lax.psum((grad_gate_up, grad_down), 'dp')]
    reduce_scatter x1 -> x0, waiting for transfers between devices: 51.1 us -> none  [shards(): lax.psum_scatter(partial_out.reshape(rows, length, width), 'mp', scatter_...]
    psum x1, waiting for transfers between devices: 3.46 us -> 50.5 us  [shards(): attend_total, output_total = lax.psum((attend_share, output_share), 'dp')]
    pallas_call x1, Pallas kernels: 115 us -> 89.5 us  [project(): pl.pallas_call(functools.partial(project_kernel, n), in_specs=[vmem, vmem...]
    all_gather x2 -> x1, waiting for transfers between devices: 45.8 us -> 49.8 us  [shards(): grads_all = lax.all_gather(grad_branch, 'mp', axis=1, tiled=True)]
  transfers between devices with their start and end apart: 5 -> 3, of which waited for: 4 -> 2; matrix products, arithmetic and copies ran while one was open for 9% -> 8% of each run, Pallas kernels for 38% -> 44%
where the time goes in v2:
time: 863 us; the launch traced here: 857 us
  Pallas kernels  604 us (70%)
  waiting for transfers between devices  100 us (12%)
  blocking collectives  42.8 us (5%)
  other arithmetic  38.5 us (4%)
  local copies, waits for them, and re-layouts  31 us (4%)
  matrix products  24.7 us (3%)
  between operations  14.3 us (2%)
    pallas_call x2, Pallas kernels, tile_sum(): pl.pallas_call(functools.partial(tile_sum_kernel, n), grid=(rows, n), in_...  185 us
    pallas_call x1, Pallas kernels, unproject(): pl.pallas_call(functools.partial(unproject_kernel, n), in_specs=[vmem] *...  151 us
    pallas_call x1, Pallas kernels, project(): pl.pallas_call(functools.partial(project_kernel, n), in_specs=[vmem, vmem...  89.5 us
    pallas_call x1, Pallas kernels, feed(): pl.pallas_call(functools.partial(feed_kernel, n), grid=(rows, n), in_spec...  82.3 us
    pallas_call x2, Pallas kernels, weight_grad(): pl.pallas_call(functools.partial(weight_kernel, finish), grid=(lw // bloc...  54.5 us
    psum x1, waiting for transfers between devices, shards(): attend_total, output_total = lax.psum((attend_share, output_share), 'dp')  50.5 us
    all_gather x1, waiting for transfers between devices, shards(): grads_all = lax.all_gather(grad_branch, 'mp', axis=1, tiled=True)  49.8 us
    psum x1, blocking collectives, shards(): gains = lax.psum(gains, ('dp', 'mp'))  42.8 us
  transfers between devices with their start and end apart: 3, of which 2 were waited for; matrix products, arithmetic and copies ran while one was open for 8% of the time, Pallas kernels for 44%

profile of v2, /device:TPU:0, one launch (start us, length us, event | category | flops | bytes accessed | tf_op | source)
XLA Modules:
  0.0 856.7 jit_solution(5535824419214617161)
XLA Ops:
  8.4 2.0 slice.66
  16.8 3.8 convert_element_type.55
  20.6 2.3 pad_maximum_fusion.w_ref
  22.9 89.5 %project.1 = (bf16[512,2048]{1,0:T(8,128)(2,1)}, f32[512,1920]{1,0:T(8,128)}, bf16[512,1280]{1,0:T(8,128)(2,1)}, bf16[8,256,1920]{2,1,0:T(8,128)(2,1)}, bf16[2,8...) custom-call(bf16[512,2048]{1,0:T(8,128)(2,1)} %bitcast.81, f32[1,2048]{1,0:T(1,128)} %bitcast.105, ...), custom_call_target="tpu_custom_call" | custom-call | tf_op jit(solution)/shard_map/project/pallas_call | solution.py:411
  113.4 2.8 copy.41.dt_any
  116.2 9.0 %copy.42 = bf16[6,256,2048]{2,1,0:T(8,128)(2,1)} copy(bf16[6,256,2048]{1,2,0:T(8,128)(2,1)} %bitcast.83) | data formatting | bytes 12582912 | tf_op jit(solution)/shard_map/transpose | solution.py:1142
  127.8 16.1 %attend.1 = (bf16[2,256,1280]{2,1,0:T(8,128)(2,1)}, f32[2,256,1280]{2,1,0:T(8,128)}) custom-call(s32[2,3]{1,0:T(2,128)} %pad_add_fusion.info, bf16[2,256,1280]{2,1,0:T(8,128)(2,1)} %bitcast.121, bf16[2,2048,640]{2,1,0:T(8,128)(2,1)} %bitcast.115, s32[2,256,128]{2,1,0:T(8,128)} %broadcast_in_dim.20.start_ref), custom_call_target="tpu_custom_call" | custom-call | flops 21474836480 | bytes 10485760 | tf_op jit(solution)/shard_map/attend/pallas_call | solution.py:628
  143.9 5.4 multiply_reduce_fusion.2
  149.3 2.0 copy-done
  151.3 1.7 multiply_convert_fusion
  153.1 49.8 %all-gather.2.cloned.1.call-done = bf16[2,2048,2048]{2,1,0:T(8,128)(2,1)} async-done(((bf16[2,256,2048]{2,1,0:T(8,128)(2,1)}), bf16[2,2048,2048]{2,1,0:T(8,128)(2,1)}) %all-gather.2.cloned.1.call-update) | async-done | bytes 16777232 | tf_op jit(solution)/shard_map/all_gather | solution.py:1133
  202.8 82.3 %feed.1 = (bf16[2,8,256,2048]{3,2,1,0:T(8,128)(2,1)}, bf16[2,8,256,768]{3,2,1,0:T(8,128)(2,1)}, bf16[2,8,256,1536]{3,2,1,0:T(8,128)(2,1)}) custom-call(f32[6]{0:T(128)} %convert_element_type.56.live_ref, bf16[2,256,2048]{2,1,0:T(8,128)(2,1)} %bitcast.96, bf16[2,8,256,2048]{3,2,1,0:T(8,128)(2,1)} %bitcast.112, bf16[6,2048,256]{2,1,0:T(8,128)(2,1)} %gu_any.1, ...), custom_call_target="tpu_custom_call" | custom-call | flops 38654705664 | bytes 59768832 | tf_op jit(solution)/shard_map/feed/pallas_call | solution.py:864
  285.1 19.0 %weight_grad.3 = bf16[768,2048]{1,0:T(8,128)(2,1)} custom-call(bf16[4096,768]{1,0:T(8,128)(2,1)} %bitcast.125, bf16[4096,2048]{1,0:T(8,128)(2,1)} %bitcast.113), custom_call_target="tpu_custom_call" | custom-call | flops 12884901888 | bytes 26214400 | tf_op jit(solution)/shard_map/weight_grad/pallas_call | solution.py:1054
  304.1 35.5 %weight_grad.2 = bf16[6,2048,256]{2,1,0:T(8,128)(2,1)} custom-call(bf16[4096,2048]{1,0:T(8,128)(2,1)} %bitcast.123, bf16[4096,1536]{1,0:T(8,128)(2,1)} %bitcast.124), custom_call_target="tpu_custom_call" | custom-call | flops 25769803776 | bytes 35651584 | tf_op jit(solution)/shard_map/weight_grad/pallas_call | solution.py:1054
  339.9 95.2 %tile_sum.2 = f32[2,256,2048]{2,1,0:T(8,128)} custom-call(bf16[2,8,256,1536]{3,2,1,0:T(8,128)(2,1)} %get-tuple-element.46.a_ref, bf16[1536,2048]{1,0:T(8,128)(2,1)} %bitcast.84), custom_call_target="tpu_custom_call" | custom-call | flops 25769803776 | bytes 18874368 | tf_op jit(solution)/shard_map/tile_sum/pallas_call | solution.py:992
  435.1 3.4 fusion.9
  438.6 1.4 copy-done.5
  439.9 1.2 bitcast_add_fusion.1
  441.2 4.7 convolution_convert_fusion
  446.5 4.0 convolution_convert_fusion.1
  451.1 26.8 %attend_back.1 = (f32[2,256,1280]{2,1,0:T(8,128)}, bf16[2,2048,640]{2,1,0:T(8,128)(2,1)}) custom-call(s32[2,3]{1,0:T(2,128)} %pad_add_fusion.info, bf16[2,256,1280]{2,1,0:T(8,128)(2,1)} %bitcast.122, bf16[2,2048,640]{2,1,0:T(8,128)(2,1)} %bitcast.116, s32[2,8,256]{2,1,0:T(8,128)} %broadcast_in_dim.21.start_ref, bf16[2,256,1280]{2,1,0:T(8,128)(2,1)} %bitcast.128, ...), custom_call_target="tpu_custom_call" | custom-call | flops 53687091200 | bytes 20971520 | tf_op jit(solution)/shard_map/attend_back/pallas_call | solution.py:739
  478.0 150.5 %unproject.1 = (bf16[512,1920]{1,0:T(8,128)(2,1)}, f32[8,128]{1,0:T(8,128)}, f32[8,128]{1,0:T(8,128)}, bf16[256,1920]{1,0:T(8,128)(2,1)}, bf16[160,2048]{1,0:T(8,128)(2,1)}) custom-call(f32[512,1280]{1,0:T(8,128)} %bitcast.94, bf16[2,8,256,640]{3,2,1,0:T(8,128)(2,1)} %bitcast.88, f32[512,1920]{1,0:T(8,128)} %get-tuple-element.50.raw_ref, ...), custom_call_target="tpu_custom_call" | custom-call | tf_op jit(solution)/shard_map/unproject/pallas_call | solution.py:541
  629.2 10.7 %fusion.7 = (f32[2048]{0:T(1024)S(1)}, f32[512]{0:T(512)S(1)}, f32[512,2048]{1,0:T(8,128)}) fusion(f32[512]{0:T(512)S(1)} %bitcast.109, bf16[2,256,2048]{2,1,0:T(8,128)(2,1)S(1)} %copy-done.3, f32[2048]{0:T(1024)S(1)} %copy-done.13, bf16[512,1920]{1,0:T(8,128)(2,1)} %get-tuple-element.54, bf16[2048,1920]{1,0:T(8,128)(2,1)} %bitcast.114), kind=kOutput, calls=%fused_computation.12 | convolution fusion | flops 4033869312 | bytes 16142336 | tf_op jit(solution)/shard_map/dot_general | solution.py:45
  639.9 42.8 %psum.39 = f32[4352]{0:T(1024)S(1)} all-reduce(f32[4352]{0:T(1024)S(1)} %pad_maximum_fusion.2), channel_id=1, replica_groups=mesh['dp'=4,'mp'=8] {'dp','mp'}, use_global_device_ids=true, to_apply=%region_13.14 | all-reduce | flops 4352 | bytes 34816 | tf_op jit(solution)/shard_map/psum | solution.py:1209
  683.9 89.6 %tile_sum.3 = f32[2,256,2048]{2,1,0:T(8,128)} custom-call(bf16[2,8,256,768]{3,2,1,0:T(8,128)(2,1)} %get-tuple-element.53.a_ref, bf16[768,2048]{1,0:T(8,128)(2,1)} %bitcast.91), custom_call_target="tpu_custom_call" | custom-call | flops 12884901888 | bytes 9437184 | tf_op jit(solution)/shard_map/tile_sum/pallas_call | solution.py:992
  773.6 6.7 bitcast_add_fusion
  781.1 3.3 fusion.4
  784.4 5.9 convert_element_type.64
  790.3 3.5 convert_element_type.65
  793.9 50.5 %all-reduce.7.cloned.1.call-done = (bf16[256,1920]{1,0:T(8,128)(2,1)}, bf16[160,2048]{1,0:T(8,128)(2,1)}) async-done(((bf16[256,1920]{1,0:T(8,128)(2,1)}, bf16[160,2048]{1,0:T(8,128)(2,1)}), (bf16[256,1920]{1,0:T(8,128)(2,1)}, bf16[160,2048]{1,0:T(8,128)(2,1)})) %all-reduce.7.cloned.1.call-update) | async-done | bytes 1638416 | tf_op jit(solution)/shard_map/psum | solution.py:1192
  847.3 1.2 convert_element_type.63
  848.5 1.5 concatenate.22
  (108 shorter events, 18.4 us)
Async XLA Ops:
  7.2 8.5 copy-start.17
  7.2 9.1 %copy-start.18 = (f32[64]{0:T(128)S(1)}, f32[64]{0:T(128)}, u32[]{:S(2)}) copy-start(f32[64]{0:T(128)} %param.17) | copy-start | bytes 772
  7.2 195.6 %all-gather.2.cloned.1.call-start = ((), (), s32[]{:S(2)}) async-start(), calls=%async_computation | async-start | bytes 18874368 | tf_op jit(solution)/shard_map/all_gather | solution.py:1133
  12.5 114.6 %copy-start.14 = (s32[2,256]{1,0:T(2,128)}, s32[2,256]{1,0:T(2,128)S(1)}, u32[]{:S(2)}) copy-start(s32[2,256]{1,0:T(2,128)S(1)} %get-tuple-element.73) | copy-start | bytes 6148
  20.6 92.0 %copy-start.19 = (s32[44]{0:T(128)S(1)}, s32[44]{0:T(128)}, u32[]{:S(2)}) copy-start(s32[44]{0:T(128)} %param.14) | copy-start | bytes 532
  20.6 92.7 %copy-start.9 = (bf16[6,128,2048]{2,1,0:T(8,128)(2,1)S(1)}, bf16[6,128,2048]{2,1,0:T(8,128)(2,1)}, u32[]{:S(2)}) copy-start(bf16[6,128,2048]{2,1,0:T(8,128)(2,1)} %param.22) | copy-start | bytes 9437188
  112.4 661.2 %all-reduce.9.cloned.1.call-start = ((), (), s32[]{:S(2)}) async-start(), calls=%async_computation.2 | async-start | bytes 18874368 | tf_op jit(solution)/shard_map/psum | solution.py:1155
  116.2 9.0 %copy-start.2 = (bf16[2,256,2048]{2,1,0:T(8,128)(2,1)S(1)}, bf16[2,256,2048]{2,1,0:T(8,128)(2,1)}, u32[]{:S(2)}) copy-start(bf16[2,256,2048]{2,1,0:T(8,128)(2,1)} %param.12) | copy-start | bytes 6291460
  143.9 7.4 copy-start.12
  149.3 2.0 copy-start
  339.7 504.7 %all-reduce.7.cloned.1.call-start = ((), (), s32[]{:S(2)}) async-start(), calls=%async_computation.1 | async-start | bytes 3276800 | tf_op jit(solution)/shard_map/psum | solution.py:1192
  339.9 95.2 %copy-start.1 = (f32[512,2048]{1,0:T(8,128)S(1)}, f32[512,2048]{1,0:T(8,128)}, u32[]{:S(2)}) copy-start(f32[512,2048]{1,0:T(8,128)} %copy-done) | copy-start | bytes 12582916
  435.1 3.5 copy-start.4
  435.1 4.8 copy-start.5
  439.9 1.3 copy-start.20
  439.9 6.0 slice-start.2
  441.2 4.7 copy-start.6
  441.2 5.3 slice-start.3
  446.5 4.0 copy-start.15
  478.0 151.2 %copy-start.3 = (bf16[2,256,2048]{2,1,0:T(8,128)(2,1)S(1)}, bf16[2,256,2048]{2,1,0:T(8,128)(2,1)}, u32[]{:S(2)}) copy-start(bf16[2,256,2048]{2,1,0:T(8,128)(2,1)} %param.12) | copy-start | bytes 6291460
  478.0 151.2 %copy-start.13 = (f32[2048]{0:T(1024)S(1)}, f32[2048]{0:T(1024)}, u32[]{:S(2)}) copy-start(f32[2048]{0:T(1024)} %param.15) | copy-start | bytes 24580
  478.0 151.2 %copy-start.16 = (f32[1,2,2,128]{3,1,2,0:T(2,128)S(1)}, f32[1,2,2,128]{3,1,2,0:T(2,128)}, u32[]{:S(2)}) copy-start(f32[1,2,2,128]{3,1,2,0:T(2,128)} %copy.53) | copy-start | bytes 6148
  773.6 6.7 copy-start.7
  773.6 7.4 copy-start.8
  780.3 4.1 slice-start
  781.0 3.3 slice-start.1
  784.4 5.9 copy-start.10
  844.4 2.9 copy-start.11
Sparse Core Ops, SparseCore 0:
  112.5 90.2 all-gather.1
  339.8 325.8 all-reduce.8
  773.7 70.6 all-reduce.6

commit v3 on v2

--- a/solution.py
+++ b/solution.py
@@ -15,6 +15,8 @@
 QW = H * HD
 LANES = 128
 GW = (H // KVH) * HD
+DOCS = 3
+AWAY = 256.0
 LOG2E = 1.4426950408889634
 LN2 = 0.6931471805599453
 BF = jnp.bfloat16
@@ -37,6 +39,9 @@
     )
 
 
+TINY = pl.CostEstimate(flops=1, bytes_accessed=1, transcendentals=0)
+
+
 def mm(a, b):
     return jnp.dot(a, b, preferred_element_type=F32)
 
@@ -87,6 +92,88 @@
     for bit in bits:
         pl.semaphore_signal(barrier, inc=1, device_id={"mp": flip(me, bit)}, device_id_type=MESH)
     pl.semaphore_wait(barrier, len(bits))
+
+
+def greet_all(n, me, m, line):
+    barrier = pltpu.get_barrier_semaphore()
+    bits = [1] + link_bits(n)
+    for bit in bits:
+        pl.semaphore_signal(barrier, inc=1, device_id={"mp": flip(me, bit)}, device_id_type=MESH)
+    for step in range(1, m):
+        other = lax.rem(line + step, m)
+        pl.semaphore_signal(barrier, inc=1, device_id={"dp": other}, device_id_type=MESH)
+    pl.semaphore_wait(barrier, len(bits) + m - 1)
+
+
+class Line:
+    def __init__(self, m, line, own, up, across, total, sems):
+        self.own, self.up, self.across, self.total, self.sems = own, up, across, total, sems
+        low = line < m // 2
+        self.inner = jnp.where(low, line + 1, line - 1)
+        self.outer = jnp.where(low, line - 1, line + 1)
+        self.has_outer = (line > 0) & (line < m - 1)
+        self.middle = (line == m // 2 - 1) | (line == m // 2)
+
+    def copy(self, kind, c):
+        src, dst, to = (
+            (self.own, self.up, self.inner),
+            (self.own, self.across, self.inner),
+            (self.total, self.total, self.outer),
+        )[kind]
+        return pltpu.make_async_remote_copy(
+            src_ref=src(c),
+            dst_ref=dst(c),
+            send_sem=self.sems.at[2 * kind, c],
+            recv_sem=self.sems.at[2 * kind + 1, c],
+            device_id={"dp": to},
+            device_id_type=MESH,
+        )
+
+    def launch(self, c):
+        @pl.when(jnp.logical_not(self.has_outer))
+        def _():
+            self.copy(0, c).start()
+
+    def inward(self, c):
+        @pl.when(self.has_outer)
+        def _():
+            self.copy(0, c).wait_recv()
+            add_up(self.own(c), [self.own(c), self.up(c)])
+
+            @pl.when(self.middle)
+            def _():
+                self.copy(1, c).start()
+
+            @pl.when(jnp.logical_not(self.middle))
+            def _():
+                self.copy(0, c).start()
+
+    def outward(self, c):
+        @pl.when(self.middle)
+        def _():
+            self.copy(1, c).wait_recv()
+            add_up(self.total(c), [self.own(c), self.across(c)])
+
+        @pl.when(jnp.logical_not(self.middle))
+        def _():
+            self.copy(2, c).wait_recv()
+
+        @pl.when(self.has_outer)
+        def _():
+            self.copy(2, c).start()
+
+    def drain(self, c):
+        @pl.when(self.middle)
+        def _():
+            self.copy(1, c).wait_send()
+
+        @pl.when(jnp.logical_not(self.middle))
+        def _():
+            self.copy(0, c).wait_send()
+
+        @pl.when(self.has_outer)
+        def _():
+            self.copy(2, c).wait_send()
 
 
 class Gather:
@@ -104,14 +191,17 @@
 
     def copy(self, k, half, bit):
         return pltpu.make_async_remote_copy(
-            src_ref=self.own(half) if k == 0 else self.slot(k, half),
-            dst_ref=self.slot(k ^ bit if self.relative else k, half),
+            src_ref=self.own(half) if k == 0 else self.here(k, half),
+            dst_ref=self.slot(k ^ bit, half, k) if self.relative else self.slot(k, half),
             send_sem=self.send.at[k ^ bit, half],
             recv_sem=self.recv.at[k ^ bit, half],
             device_id={"mp": flip(self.me, bit)},
             device_id_type=MESH,
         )
 
+    def here(self, k, half):
+        return self.slot(k, half, k) if self.relative else self.slot(k, half)
+
     def onward(self, k, half):
         return self.order[half][(max(self.place(k, half)) + 1) if k else 0 :]
 
@@ -121,7 +211,7 @@
                 self.copy(0, half, self.order[half][i]).start()
 
     def arrive(self, k, half):
-        here = self.slot(k, half)
+        here = self.here(k, half)
         pltpu.make_async_remote_copy(
             src_ref=here,
             dst_ref=here,
@@ -148,9 +238,9 @@
 
 
 class Scatter:
-    def __init__(self, n, me, part, core, link, stage, sems):
+    def __init__(self, n, me, part, core, link, sems):
         self.n, self.me, self.part = n, me, part
-        self.core, self.link, self.stage = core, link, stage
+        self.core, self.link = core, link
         self.core_send, self.core_recv, self.link_send, self.link_recv = sems
         bits = link_bits(n)
         self.order = (bits[::-1], bits)
@@ -171,7 +261,7 @@
     def link_copy(self, k, half):
         bit = self.order[half][self.first(k, half)]
         return pltpu.make_async_remote_copy(
-            src_ref=self.part(self.stage(k // 2 - 1), half),
+            src_ref=self.part(self.core(k // 2), half),
             dst_ref=self.link(half, k // 2 - 1),
             send_sem=self.link_send.at[half, k // 2 - 1],
             recv_sem=self.link_recv.at[half, k // 2 - 1],
@@ -193,7 +283,7 @@
             for j in self.addends(k, half):
                 self.link_copy(j, half).wait_recv()
                 joined.append(self.link(half, j // 2 - 1))
-            add_up(self.part(self.stage(k // 2 - 1), half), joined)
+            add_up(joined[1], joined)
             self.link_copy(k, half).start()
 
     def own(self, ref, out):
@@ -231,7 +321,6 @@
     return [
         pltpu.VMEM((n // 2,) + shape, BF),
         pltpu.VMEM((2, n // 2 - 1) + half, BF),
-        pltpu.VMEM((n // 2 - 1,) + shape, BF),
         pltpu.SemaphoreType.DMA((n // 2,)),
         pltpu.SemaphoreType.DMA((n // 2,)),
         pltpu.SemaphoreType.DMA((2, n // 2 - 1)),
@@ -240,15 +329,14 @@
 
 
 def make_scatter(n, me, part, refs):
-    core, link, stage = refs[:3]
+    core, link = refs[:2]
     return Scatter(
         n,
         me,
         part,
         lambda i: core.at[i],
         lambda h, i: link.at[h, i],
-        lambda i: stage.at[i],
-        refs[3:7],
+        refs[2:6],
     )
 
 
@@ -437,9 +525,9 @@
 
 
 def unproject_kernel(
-    n, dq_ref, dkv_ref, raw_ref, cos_ref, sin_ref, gq_ref, gk_ref, ones_ref, normed_ref, gout_ref,
-    gj_ref, sq_ref, sk_ref, attend_ref, output_ref,
-    dkv_own, term, *scratch,
+    n, dq_ref, dkv_ref, raw_ref, cos_ref, sin_ref, gq_ref, gk_ref, ones_ref, gout_ref,
+    gj_ref, sq_ref, sk_ref, output_ref,
+    dkv_own, *scratch,
 ):
     me = lax.axis_index("mp")
     greet(n, me)
@@ -447,16 +535,10 @@
     rows = dkv_ref.shape[0]
     span = tokens // rows
     columns = raw_ref.shape[1]
-    depth = attend_ref.shape[0]
-
-    keys = make_scatter(n, me, lambda ref, h: ref.at[h], scratch[:7])
+    keys = make_scatter(n, me, lambda ref, h: ref.at[h], scratch[:6])
     half_w = output_ref.shape[1] // 2
     outs = make_scatter(
-        n, me, lambda ref, h: ref.at[:, pl.ds(h * half_w, half_w)], scratch[7:14]
-    )
-    half_d = depth // 2
-    weights = make_scatter(
-        n, me, lambda ref, h: ref.at[pl.ds(h * half_d, half_d)], scratch[14:21]
+        n, me, lambda ref, h: ref.at[:, pl.ds(h * half_w, half_w)], scratch[6:12]
     )
 
     def dkv_term(k):
@@ -515,47 +597,187 @@
     def _(i):
         back(i, range(QW // LANES, count), False)
 
-    for k in range(n - 1, -1, -1):
-        at = pl.ds(pl.multiple_of(flip(me, k) * depth, depth), depth)
-        here = term.at[k]
-        here[...] = dg(normed_ref[:, at], gj_ref[...], TN).astype(BF)
-        if k % 2:
-            weights.odd(k, here)
-        elif k:
-            weights.even(k, here)
     outs.own(out_term(0), output_ref)
-    weights.own(term.at[0], attend_ref)
     keys.drain(dkv_term(0))
     outs.drain(out_term(0))
-    weights.drain(term.at[0])
-
-
-def unproject(n, dq, dkv, raw, cos, sin, gq, gk, ones, normed, gout):
+
+
+def unproject(n, dq, dkv, raw, cos, sin, gq, gk, ones, gout):
     tokens, columns = raw.shape
     rows = dkv.shape[0]
     span = tokens // rows
     kvw = columns - QW
-    width = normed.shape[1]
-    depth = width // n
+    width = gout.shape[2]
     vmem = pl.BlockSpec(memory_space=pltpu.VMEM)
     return pl.pallas_call(
         functools.partial(unproject_kernel, n),
-        in_specs=[vmem] * 10,
-        out_specs=[vmem] * 5,
+        in_specs=[vmem] * 9,
+        out_specs=[vmem] * 4,
         out_shape=[
             jax.ShapeDtypeStruct((tokens, columns), BF),
             jax.ShapeDtypeStruct((8, LANES), F32),
             jax.ShapeDtypeStruct((8, LANES), F32),
-            jax.ShapeDtypeStruct((depth, columns), BF),
             jax.ShapeDtypeStruct((QW // n, width), BF),
         ],
-        scratch_shapes=[pltpu.VMEM((rows, span, kvw), F32), pltpu.VMEM((n, depth, columns), BF)]
+        scratch_shapes=[pltpu.VMEM((rows, span, kvw), F32)]
         + scatter_scratch(n, (rows, span, kvw), (span, kvw))
-        + scatter_scratch(n, (QW // n, width), (QW // n, width // 2))
+        + scatter_scratch(n, (QW // n, width), (QW // n, width // 2)),
+        compiler_params=params(mib=60, axes=0, key=2),
+        cost_estimate=TINY,
+        name="unproject",
+    )(dq, dkv, raw, cos, sin, gq, gk, ones, gout)
+
+
+GAIN_ROWS = 40
+
+
+def finish_kernel(
+    n, m, normed_ref, gj_ref, w_any, x_ref, mid_ref, gain_ref, output_ref, sums_ref,
+    grad_ref, attend_ref, out_ref, gains_ref,
+    w_ref, term, error, own_w, up_w, across_w, total_w, own_o, up_o, across_o, total_o, landed,
+    sem_w, sem_o, sem_g, load, *scratch,
+):
+    me, line = lax.axis_index("mp"), lax.axis_index("dp")
+    depth = w_ref.shape[1]
+    tokens, width = x_ref.shape
+    pieces, piece = own_w.shape[0], own_w.shape[1]
+    fetch = pltpu.make_async_copy(w_any, w_ref, load.at[0])
+    fetch.start()
+    greet_all(n, me, m, line)
+    half = depth // 2
+    sums = make_scatter(n, me, lambda ref, h: ref.at[pl.ds(h * half, half)], scratch)
+    at = lambda ref: lambda c: ref.at[c]
+    weights = Line(m, line, at(own_w), at(up_w), at(across_w), at(total_w), sem_w)
+    outs = Line(m, line, at(own_o), at(up_o), at(across_o), at(total_o), sem_o)
+    own_o[0] = output_ref[...]
+
+    chunk = error.shape[0]
+    gains_ref[...] = sums_ref[...]
+
+    def tokens_part(i):
+        here = pl.ds(pl.multiple_of(i * chunk, chunk), chunk)
+        for b in range(n):
+            error[:, b * depth : (b + 1) * depth] = dg(gj_ref[here, :], w_ref[b], NT)
+        small = min(32, chunk)
+
+        @pl.loop(0, chunk // small)
+        def _(s):
+            part = pl.ds(pl.multiple_of(s * small, small), small)
+            rows = pl.ds(pl.multiple_of(i * chunk + s * small, small), small)
+            e = error[part, :]
+            x = x_ref[rows, :].astype(F32)
+            scale = lax.rsqrt(jnp.mean(x * x, axis=-1, keepdims=True) + EPSILON)
+            u = e * gain_ref[...]
+            v = x * scale
+            inner = jnp.mean(u * v, axis=-1, keepdims=True)
+            grad_ref[rows, :] = mid_ref[rows, :] + scale * (u - v * inner)
+            total = jnp.sum(e * v, axis=0, keepdims=True)
+            for b in range(width // LANES):
+                gains_ref[b : b + 1, :] += total[:, b * LANES : (b + 1) * LANES]
+
+    def weight_part(k):
+        columns = pl.ds(pl.multiple_of(flip(me, k) * depth, depth), depth)
+        term[k] = dg(normed_ref[:, columns], gj_ref[...], TN).astype(BF)
+
+    parts = tokens // chunk
+    left = list(range(parts))
+    outs.launch(0)
+    outs.inward(0)
+    for k in range(n - 1, 0, -1):
+        weight_part(k)
+        if k % 2:
+            sums.odd(k, term.at[k])
+        else:
+            sums.even(k, term.at[k])
+        if k == n - 1:
+            fetch.wait()
+    weight_part(0)
+
+    def span_of(first, last):
+        @pl.loop(first, last)
+        def _(i):
+            tokens_part(i)
+
+    span_of(0, parts // 2)
+    outs.outward(0)
+    span_of(parts // 2, parts)
+    sums.own(term.at[0], attend_ref)
+    for c in range(pieces):
+        own_w[c] = attend_ref[c * piece : (c + 1) * piece, :].astype(BF)
+        weights.launch(c)
+        weights.inward(c)
+    steps = [("mp", flip(me, 1 << i)) for i in range(n.bit_length() - 1)]
+    steps += [("dp", flip(line, 1 << i)) for i in range(m.bit_length() - 1)]
+
+    def exchange(i):
+        axis, to = steps[i]
+        return pltpu.make_async_remote_copy(
+            src_ref=landed.at[2 * i],
+            dst_ref=landed.at[2 * i + 1],
+            send_sem=sem_g.at[0, i],
+            recv_sem=sem_g.at[1, i],
+            device_id={axis: to},
+            device_id_type=MESH,
+        )
+
+    done = 0
+    for i in range(len(steps)):
+        landed[2 * i] = gains_ref[...]
+        exchange(i).start()
+        if done < pieces and i % 2:
+            weights.outward(done)
+            done += 1
+        exchange(i).wait_recv()
+        gains_ref[...] = landed[2 * i] + landed[2 * i + 1]
+    for c in range(done, pieces):
+        weights.outward(c)
+    for c in range(pieces):
+        attend_ref[c * piece : (c + 1) * piece, :] = total_w[c].astype(F32)
+    out_ref[...] = total_o[0].astype(F32)
+    for c in range(pieces):
+        weights.drain(c)
+    outs.drain(0)
+    for i in range(len(steps)):
+        exchange(i).wait_send()
+    sums.drain(term.at[0])
+
+
+def finish(n, m, normed, gj, w, x, middle, gain, output_share, sums):
+    tokens, width = x.shape
+    columns = gj.shape[1]
+    depth = width // n
+    pieces = 4
+    vmem = pl.BlockSpec(memory_space=pltpu.VMEM)
+    steps = n.bit_length() + m.bit_length() - 2
+    return pl.pallas_call(
+        functools.partial(finish_kernel, n, m),
+        in_specs=[vmem, vmem, pl.BlockSpec(memory_space=pl.ANY)] + [vmem] * 5,
+        out_specs=[vmem] * 4,
+        out_shape=[
+            jax.ShapeDtypeStruct((tokens, width), F32),
+            jax.ShapeDtypeStruct((depth, columns), F32),
+            jax.ShapeDtypeStruct(output_share.shape, F32),
+            jax.ShapeDtypeStruct((GAIN_ROWS, LANES), F32),
+        ],
+        scratch_shapes=[
+            pltpu.VMEM(w.shape, BF),
+            pltpu.VMEM((n, depth, columns), BF),
+            pltpu.VMEM((min(256, tokens), width), F32),
+        ]
+        + [pltpu.VMEM((pieces, depth // pieces, columns), BF)] * 4
+        + [pltpu.VMEM((1,) + output_share.shape, BF)] * 4
+        + [
+            pltpu.VMEM((2 * steps, GAIN_ROWS, LANES), F32),
+            pltpu.SemaphoreType.DMA((6, pieces)),
+            pltpu.SemaphoreType.DMA((6, 1)),
+            pltpu.SemaphoreType.DMA((2, steps)),
+            pltpu.SemaphoreType.DMA((1,)),
+        ]
         + scatter_scratch(n, (depth, columns), (depth // 2, columns)),
-        compiler_params=params(mib=60, axes=0, key=2),
-        name="unproject",
-    )(dq, dkv, raw, cos, sin, gq, gk, ones, normed, gout)
+        compiler_params=params(mib=60, axes=0, key=5),
+        cost_estimate=TINY,
+        name="finish",
+    )(normed, gj, w, x, middle, gain, output_share, sums)
 
 
 def key_positions(shape, axis, group, per, span):
@@ -640,13 +862,31 @@
 
 
 def attend_back_kernel(
-    keys, info, q_ref, kv_ref, start_ref, do_ref, ctx_ref, rl_ref, dq_ref, dkv_ref, acc, sides
+    keys, n, q_ref, kv_ref, qa_ref, ka_ref, do_ref, ctx_ref, rl_ref, a_ref, w_any,
+    dq_ref, dkv_ref, o_ref, acc, sides, *scratch,
 ):
     span = q_ref.shape[1]
     per = keys // span
     length = kv_ref.shape[1]
-    row = pl.program_id(0)
-    me, first, last_start = info[row, 0], info[row, 1], info[row, 2]
+    me = lax.axis_index("mp")
+    rows = o_ref.shape[0]
+    now = pl.program_id(0) * KVH + pl.program_id(1)
+    sums = TileSum(n, me, o_ref, w_any, scratch)
+    batch = a_ref.shape[1]
+    steps = rows * n // batch
+
+    @pl.when(now == 0)
+    def _():
+        sums.start()
+
+    @pl.when(now < steps)
+    def _():
+        @pl.loop(0, batch)
+        def _(i):
+            tile = now * batch + i
+            slot = n - 1 - lax.rem(tile, n)
+            sums.step(tile, a_ref.at[0, lax.rem(xor_of(me, slot, n), batch)])
+
     lane = lax.broadcasted_iota(jnp.int32, (span, LANES), 1)
     low_q = lane < HD
     low_k = lax.broadcasted_iota(jnp.int32, (keys, LANES), 1) < HD
@@ -666,25 +906,26 @@
             one_part,
             jnp.where(lane == base + 1, two_part, jnp.where(lane == base + 2, three_part, 0.0)),
         )
-        sides[0, h] = jnp.where(mine, q_ref[0, :, lanes].astype(F32), 0.0).astype(BF)
+        query = q_ref[0, :, lanes].astype(F32)
+        sides[0, h] = jnp.where(mine, query, 0.0).astype(BF)
         sides[1, h] = own.astype(BF)
         sides[2, h] = jnp.where(mine, scaled, extra).astype(BF)
+        sides[3, h] = jnp.where(mine, query, qa_ref[0].astype(F32)).astype(BF)
     acc[...] = jnp.zeros_like(acc)
 
     def block(g, masked):
-        group = g
-        here = pl.ds(pl.multiple_of(group * keys, keys), keys)
+        here = pl.ds(pl.multiple_of(g * keys, keys), keys)
         kv = kv_ref[0, here, :]
+        ka = ka_ref[0, here, :]
         vk = jnp.concatenate([kv[:, HD:], kv[:, :HD]], axis=1)
-        key_sides = (kv, vk)
+        key_sides = (jnp.where(low_k, kv, ka), jnp.where(low_k, ka, vk))
         value_sides = (jnp.where(low_k, vk, one), jnp.where(low_k, one, kv))
         if masked:
-            position = key_positions((keys, span), 0, group, per, span)
-            own = me * span + lax.broadcasted_iota(jnp.int32, (keys, span), 1)
-            seen = (position <= own) & (position >= start_ref[0][:1, :])
+            position = g * keys + lax.broadcasted_iota(jnp.int32, (keys, span), 0)
+            seen = position <= me * span + lax.broadcasted_iota(jnp.int32, (keys, span), 1)
         grad_key = grad_value = 0.0
         for h in range(GW // HD):
-            e = jnp.exp2(dg(key_sides[h % 2], sides[0, h], NT))
+            e = jnp.exp2(dg(key_sides[h % 2], sides[3, h], NT))
             if masked:
                 e = jnp.where(seen, e, 0.0)
             ds = (e * dg(value_sides[h % 2], sides[2, h], NT)).astype(BF)
@@ -695,59 +936,75 @@
         grad_value = grad_value + pltpu.roll(grad_value, HD, 1)
         dkv_ref[0, here, :] = jnp.where(low_k, grad_key, grad_value).astype(BF)
 
-    def step(g, carry):
-        visited = (g >= first) & (g <= me // per)
-        edge = (g == me // per) | (g * keys < last_start)
-
-        @pl.when(jnp.logical_not(visited))
-        def _():
-            group = g
-            dkv_ref[0, pl.ds(pl.multiple_of(group * keys, keys), keys), :] = jnp.zeros((keys, LANES), BF)
-
-        pl.when(visited & edge)(lambda: block(g, True))
-        pl.when(visited & jnp.logical_not(edge))(lambda: block(g, False))
-        return carry
-
-    lax.fori_loop(0, length // keys, step, 0)
+    last = lax.div(me, per)
+
+    @pl.loop(0, last)
+    def _(g):
+        block(g, False)
+
+    block(last, True)
+
+    @pl.loop(last + 1, length // keys)
+    def _(g):
+        dkv_ref[0, pl.ds(pl.multiple_of(g * keys, keys), keys), :] = jnp.zeros((keys, LANES), BF)
+
     for pair in range(GW // LANES):
         lanes = slice(pair * LANES, (pair + 1) * LANES)
         dq_ref[0, :, lanes] = jnp.where(low_q, acc[2 * pair], acc[2 * pair + 1]) * (HD**-0.5)
 
-
-def attend_back(info, q, kv, start, do, ctx, rl):
+    @pl.when(now == rows * KVH - 1)
+    def _():
+        sums.end()
+
+
+def attend_back(n, q, kv, qa, ka, do, ctx, rl, a, w):
     rows, span, _ = q.shape
     length = kv.shape[1]
     keys = min(512, length)
-    own = lambda r, h, info: (r, 0, h)
-    spec = pltpu.PrefetchScalarGridSpec(
-        num_scalar_prefetch=1,
+    depth, width = w.shape
+    batch = 2
+    while rows * n // batch > rows * KVH:
+        batch *= 2
+    own = lambda r, h: (r, 0, h)
+
+    def place(r, h):
+        tile = jnp.minimum(r * KVH + h, rows * n // batch - 1) * batch
+        slot = n - 1 - lax.rem(tile, n)
+        return (lax.div(tile, n), lax.div(xor_of(lax.axis_index("mp"), slot, n), batch), 0, 0)
+
+    return pl.pallas_call(
+        functools.partial(attend_back_kernel, keys, n),
         grid=(rows, KVH),
         in_specs=[
             pl.BlockSpec((1, span, GW), own),
             pl.BlockSpec((1, length, LANES), own),
-            pl.BlockSpec((1, 8, span), lambda r, h, info: (r, 0, 0)),
+            pl.BlockSpec((1, span, LANES), lambda r, h: (r, 0, 0)),
+            pl.BlockSpec((1, length, LANES), lambda r, h: (r, 0, 0)),
             pl.BlockSpec((1, span, GW), own),
             pl.BlockSpec((1, span, GW), own),
             pl.BlockSpec((1, span, GW), own),
-        ],
-        out_specs=[pl.BlockSpec((1, span, GW), own), pl.BlockSpec((1, length, LANES), own)],
+            pl.BlockSpec((1, batch, span, depth), place),
+            pl.BlockSpec(memory_space=pl.ANY),
+        ],
+        out_specs=[
+            pl.BlockSpec((1, span, GW), own),
+            pl.BlockSpec((1, length, LANES), own),
+            pl.BlockSpec(memory_space=pltpu.VMEM),
+        ],
+        out_shape=[
+            jax.ShapeDtypeStruct(q.shape, F32),
+            jax.ShapeDtypeStruct(kv.shape, BF),
+            jax.ShapeDtypeStruct((rows, span, width), F32),
+        ],
         scratch_shapes=[
             pltpu.VMEM((GW // HD, span, LANES), F32),
-            pltpu.VMEM((3, GW // HD, span, LANES), BF),
-        ],
-    )
-    return pl.pallas_call(
-        functools.partial(attend_back_kernel, keys),
-        grid_spec=spec,
-        out_shape=[jax.ShapeDtypeStruct(q.shape, F32), jax.ShapeDtypeStruct(kv.shape, BF)],
-        compiler_params=params(axes=2),
-        cost_estimate=pl.CostEstimate(
-            flops=40 * rows * H * span * length * HD,
-            bytes_accessed=rows * (length * 2560 + span * QW * 16),
-            transcendentals=rows * H * span * length,
-        ),
+            pltpu.VMEM((4, GW // HD, span, LANES), BF),
+        ]
+        + tile_scratch(n, rows, span, w),
+        compiler_params=params(mib=60, axes=2, key=4),
+        cost_estimate=TINY,
         name="attend_back",
-    )(info, q, kv, start, do, ctx, rl)
+    )(q, kv, qa, ka, do, ctx, rl, a, w)
 
 
 def xor_of(a, b, n):
@@ -760,46 +1017,46 @@
 
 def feed_kernel(
     n, live_ref, x_own, g_ref, gu_any, dt_any,
-    x_all, hid_ref, dgu_ref,
-    x_vm, gu_ref, dt_ref, x_send, x_recv, loads, keep,
+    x_all, hid_ref, dgu_ref, gd_any,
+    x_vm, gu_ref, dt_ref, d_sum, out_d, x_send, x_recv, loads, stores, keep,
 ):
     me = lax.axis_index("mp")
     rows, span, width = x_own.shape
     slots = gu_ref.shape[0]
-    r, j = pl.program_id(0), pl.program_id(1)
-    now = r * n + j
+    r, p = pl.program_id(0), pl.program_id(1)
+    pairs = n // 2
+    now = r * pairs + p
     half = span // 2
 
     def gather(row):
+        def slot(i, h, k):
+            at = lax.rem(flip(me, k), 2) * span + h * half
+            return x_vm.at[row, i // 2, pl.ds(pl.multiple_of(at, half), half)]
+
         return Gather(
             n,
             me,
             lambda h: x_own.at[row, pl.ds(h * half, half)],
-            lambda i, h: x_vm.at[row, i, pl.ds(h * half, half)],
+            slot,
             x_send.at[row],
             x_recv.at[row],
             True,
         )
 
-    def store(row, slot):
-        block = xor_of(me, slot, n)
-        return pltpu.make_async_copy(x_vm.at[row, slot], x_all.at[row, block], keep.at[row, slot])
+    def own_copy(row):
+        at = pl.ds(pl.multiple_of(lax.rem(me, 2) * span, span), span)
+        return pltpu.make_async_copy(x_own.at[row], x_vm.at[row, 0, at], loads.at[2 + row])
 
     fetch = [
         pltpu.make_async_copy(gu_any, gu_ref, loads.at[0]),
         pltpu.make_async_copy(dt_any, dt_ref, loads.at[1]),
     ]
 
-    def own_copy(row):
-        return pltpu.make_async_copy(x_own.at[row], x_vm.at[row, 0], loads.at[2 + row])
-
     def events(row, upto):
         todo = gather(row).even
-        ends = [0] * n
-        for k in range(2, n):
-            ends[k] = ends[k - 1]
-            if k % 2 == 0:
-                ends[k] = max(ends[k - 1], 1 + max(i for i, e in enumerate(todo) if e[0] == k))
+        ends = [0] * pairs
+        for i in range(1, pairs):
+            ends[i] = max(ends[i - 1], 1 + max(j for j, e in enumerate(todo) if e[0] == 2 * i))
         return todo[ends[upto - 1] if upto else 0 : ends[upto]]
 
     @pl.when(now == 0)
@@ -810,27 +1067,31 @@
             c.start()
         greet(n, me)
         gather(0).start()
+        d_sum[...] = jnp.zeros_like(d_sum)
         own_copy(0).wait()
         for c in fetch:
             c.wait()
 
     for row in range(rows):
-        for k in range(n):
-
-            @pl.when(now == row * n + k)
-            def _(row=row, k=k):
-                if k == 0 and row:
+        for i in range(pairs):
+
+            @pl.when(now == row * pairs + i)
+            def _(row=row, i=i):
+                if i == 0 and row:
                     own_copy(row).wait()
-                for i, e in enumerate(events(row, k)):
+                for j, e in enumerate(events(row, i)):
                     gather(row).forward(*e)
-                    if row + 1 < rows and k == 2 and i == 1:
+                    if row + 1 < rows and i == 1 and j == 1:
                         gather(row + 1).start()
-                if k % 2:
-                    for h in (0, 1):
-                        gather(row).arrive(k, h)
-
-    store(r, j).start()
-    x = x_vm.at[r, j]
+                for h in (0, 1):
+                    gather(row).arrive(2 * i + 1, h)
+
+    def save(row, i):
+        block = lax.div(xor_of(me, 2 * i, n), 2)
+        return pltpu.make_async_copy(x_vm.at[row, i], x_all.at[row, block], keep.at[row, i])
+
+    save(r, p).start()
+    x = x_vm.at[r, p]
     grad = mm(g_ref[0, 0], dt_ref[...])
     for t in range(slots):
         both = mm(x[...], gu_ref[t])
@@ -845,234 +1106,306 @@
         ).astype(BF)
         dgu_ref[0, 0, :, (2 * t + 1) * TILE : (2 * t + 2) * TILE] = (gh * silu).astype(BF)
 
-    @pl.when(now == rows * n - 1)
+    cut = LANES
+
+    @pl.loop(0, slots * TILE // cut)
+    def _(i):
+        at = pl.ds(pl.multiple_of(i * cut, cut), cut)
+        d_sum[at, :] += dg(hid_ref[0, 0, :, at], g_ref[0, 0], TN)
+
+    @pl.when(now == rows * pairs - 1)
     def _():
+        def store(t):
+            return pltpu.make_async_copy(out_d.at[t % 2], gd_any.at[t], stores.at[t % 2])
+
+        for t in range(slots):
+            if t > 1:
+                store(t - 2).wait()
+            out_d[t % 2] = d_sum[t * TILE : (t + 1) * TILE, :].astype(BF)
+            store(t).start()
+        for t in range(max(slots - 2, 0), slots):
+            store(t).wait()
+        for row in range(rows):
+            for i in range(pairs):
+                save(row, i).wait()
         for row in range(rows):
             gather(row).drain()
-            for k in range(n):
-                store(row, k).wait()
 
 
 def feed(n, live, x, g, gu, dt):
     rows, span, width = x.shape
     slots = gu.shape[0]
     hbm = pl.BlockSpec(memory_space=pl.ANY)
-
-    def place(r, j):
-        return (r, xor_of(lax.axis_index("mp"), j, n), 0, 0)
+    pairs = n // 2
+
+    def place(r, p):
+        return (r, lax.div(xor_of(lax.axis_index("mp"), 2 * p, n), 2), 0, 0)
 
     return pl.pallas_call(
         functools.partial(feed_kernel, n),
-        grid=(rows, n),
+        grid=(rows, pairs),
         in_specs=[
             pl.BlockSpec(memory_space=pltpu.SMEM),
             hbm,
-            pl.BlockSpec((1, 1, span, width), place),
+            pl.BlockSpec((1, 1, 2 * span, width), place),
             hbm,
             hbm,
         ],
         out_specs=[
             hbm,
-            pl.BlockSpec((1, 1, span, slots * TILE), place),
-            pl.BlockSpec((1, 1, span, 2 * slots * TILE), place),
+            pl.BlockSpec((1, 1, 2 * span, slots * TILE), place),
+            pl.BlockSpec((1, 1, 2 * span, 2 * slots * TILE), place),
+            hbm,
         ],
         out_shape=[
-            jax.ShapeDtypeStruct((rows, n, span, width), BF),
-            jax.ShapeDtypeStruct((rows, n, span, slots * TILE), BF),
-            jax.ShapeDtypeStruct((rows, n, span, 2 * slots * TILE), BF),
+            jax.ShapeDtypeStruct((rows, pairs, 2 * span, width), BF),
+            jax.ShapeDtypeStruct((rows, pairs, 2 * span, slots * TILE), BF),
+            jax.ShapeDtypeStruct((rows, pairs, 2 * span, 2 * slots * TILE), BF),
+            jax.ShapeDtypeStruct((slots, TILE, width), BF),
         ],
         scratch_shapes=[
-            pltpu.VMEM((rows, n, span, width), BF),
+            pltpu.VMEM((rows, pairs, 2 * span, width), BF),
             pltpu.VMEM(gu.shape, BF),
             pltpu.VMEM(dt.shape, BF),
+            pltpu.VMEM((slots * TILE, width), F32),
+            pltpu.VMEM((2, TILE, width), BF),
             pltpu.SemaphoreType.DMA((rows, n, 2)),
             pltpu.SemaphoreType.DMA((rows, n, 2)),
             pltpu.SemaphoreType.DMA((2 + rows,)),
-            pltpu.SemaphoreType.DMA((rows, n)),
-        ],
-        compiler_params=params(mib=56, axes=2, key=1),
+            pltpu.SemaphoreType.DMA((2,)),
+            pltpu.SemaphoreType.DMA((rows, pairs)),
+        ],
+        compiler_params=params(mib=62, axes=2, key=1),
         cost_estimate=pl.CostEstimate(
-            flops=2 * 3 * rows * n * span * slots * TILE * width,
+            flops=2 * 6 * rows * n * span * slots * TILE * width,
             bytes_accessed=6 * rows * n * span * width + 6 * slots * TILE * width,
             transcendentals=rows * n * span * slots * TILE,
         ),
         name="feed",
-    )(live, x, g, gu, dt)
-
-
-def tile_sum_kernel(
-    n, a_ref, w_any, o_ref,
-    w_ref, terms, core, link, stage, core_send, core_recv, link_send, link_recv, load,
-):
-    me = lax.axis_index("mp")
-    rows, span, width = o_ref.shape
-    r, j = pl.program_id(0), pl.program_id(1)
-    k = n - 1 - j
-    now = r * n + j
-    half = span // 2
-
-    def scatter(row):
+    )(live, x, g.reshape(rows, pairs, 2 * span, width), gu, dt)
+
+
+class TileSum:
+    def __init__(self, n, me, o_ref, w_any, scratch):
+        self.n, self.me, self.o_ref, self.w_any = n, me, o_ref, w_any
+        self.w_ref, self.terms, self.core, self.link = scratch[:4]
+        self.sems, self.load = scratch[4:8], scratch[8]
+        self.rows, self.span, _ = o_ref.shape
+
+    def scatter(self, row):
+        half = self.span // 2
         return Scatter(
-            n,
-            me,
+            self.n,
+            self.me,
             lambda ref, h: ref.at[pl.ds(h * half, half)],
-            lambda i: core.at[row, i],
-            lambda h, i: link.at[row, h, i],
-            lambda i: stage.at[i],
-            (core_send.at[row], core_recv.at[row], link_send.at[row], link_recv.at[row]),
+            lambda i: self.core.at[row, i],
+            lambda h, i: self.link.at[row, h, i],
+            tuple(s.at[row] for s in self.sems),
         )
 
-    @pl.when(now == 0)
-    def _():
-        fetch = pltpu.make_async_copy(w_any, w_ref, load.at[0])
+    def start(self, meet=greet):
+        fetch = pltpu.make_async_copy(self.w_any, self.w_ref, self.load.at[0])
         fetch.start()
-        greet(n, me)
+        meet(self.n, self.me)
         fetch.wait()
 
-    for i in range(1, n, 2):
-
-        @pl.when((r > 0) & (k == i))
-        def _(i=i):
-            scatter(r - 1).core_copy(i, terms.at[i // 2]).wait_send()
-
-    at = lax.rem(k, 2) * lax.div(k, 2) + (1 - lax.rem(k, 2)) * (n // 2)
-    terms[at] = mm(a_ref[0, 0], w_ref[...]).astype(BF)
-    mine = terms.at[n // 2]
-    sums = scatter(r)
-    for i in range(1, n):
-
-        @pl.when(k == i)
-        def _(i=i):
-            if i % 2:
-                sums.odd(i, terms.at[i // 2])
-            else:
-
-                @pl.when(r > 0)
-                def _():
-                    for h in (0, 1):
-                        scatter(r - 1).link_copy(i, h).wait_send()
-
-                sums.even(i, mine)
-
-    @pl.when(k == 0)
-    def _():
-        sums.core_copy(1, core.at[r, 0]).wait_recv()
-        add_up(o_ref.at[r], [mine, core.at[r, 0]])
-
-    def close(row):
-        last = scatter(row)
+    def close(self, row):
+        last = self.scatter(row)
         for h in (0, 1):
-            here = last.part(o_ref.at[row], h)
+            here = last.part(self.o_ref.at[row], h)
             joined = [here]
             for i in last.addends(0, h):
                 last.link_copy(i, h).wait_recv()
                 joined.append(last.link(h, i // 2 - 1))
             add_up(here, joined)
 
-    for row in range(rows - 1):
-
-        @pl.when(now == (row + 1) * n + n // 2)
-        def _(row=row):
-            close(row)
+    def step(self, now, a_ref):
+        n, terms = self.n, self.terms
+        r = lax.div(now, n)
+        k = n - 1 - lax.rem(now, n)
+        for row in range(1, self.rows):
+
+            @pl.when(now == row * n + n // 2)
+            def _(row=row):
+                self.close(row - 1)
+
+        for i in range(1, n, 2):
+
+            @pl.when((r > 0) & (k == i))
+            def _(i=i):
+                self.scatter(r - 1).core_copy(i, terms.at[i // 2]).wait_send()
+
+        at = lax.rem(k, 2) * lax.div(k, 2) + (1 - lax.rem(k, 2)) * (n // 2)
+        terms[at] = mm(a_ref[...], self.w_ref[...]).astype(BF)
+        mine = terms.at[n // 2]
+        sums = self.scatter(r)
+        for i in range(1, n):
+
+            @pl.when(k == i)
+            def _(i=i):
+                if i % 2:
+                    sums.odd(i, terms.at[i // 2])
+                else:
+                    sums.even(i, mine)
+
+        @pl.when(k == 0)
+        def _():
+            sums.core_copy(1, self.core.at[r, 0]).wait_recv()
+            add_up(self.o_ref.at[r], [mine, self.core.at[r, 0]])
+
+    def end(self):
+        self.close(self.rows - 1)
+        self.scatter(self.rows - 1).drain(self.terms.at[self.n // 2])
+        for row in range(self.rows - 1):
+            for i in range(2, self.n, 2):
+                for h in (0, 1):
+                    self.scatter(row).link_copy(i, h).wait_send()
+
+
+def tile_scratch(n, rows, span, w):
+    width = w.shape[1]
+    return [
+        pltpu.VMEM(w.shape, BF),
+        pltpu.VMEM((n // 2 + 1, span, width), BF),
+        pltpu.VMEM((rows, n // 2, span, width), BF),
+        pltpu.VMEM((rows, 2, n // 2 - 1, span // 2, width), BF),
+        pltpu.SemaphoreType.DMA((rows, n // 2)),
+        pltpu.SemaphoreType.DMA((rows, n // 2)),
+        pltpu.SemaphoreType.DMA((rows, 2, n // 2 - 1)),
+        pltpu.SemaphoreType.DMA((rows, 2, n // 2 - 1)),
+        pltpu.SemaphoreType.DMA((1,)),
+    ]
+
+
+def spread_kernel(
+    n, m, a_ref, w_any, x_ref, b_ref, d_any,
+    o_ref, grad_ref, total_any,
+    acc, own, up, across, line_sems, moves, *scratch,
+):
+    me, line = lax.axis_index("mp"), lax.axis_index("dp")
+    rows = o_ref.shape[0]
+    now = pl.program_id(0) * n + pl.program_id(1)
+    per = rows * n // BLOCKS
+    sums = TileSum(n, me, o_ref, w_any, scratch)
+    chunks = own.shape[0]
+    at = lambda ref: lambda c: ref.at[c]
+    down = Line(m, line, at(own), at(up), at(across), at(up), line_sems)
+    bring = pltpu.make_async_copy(d_any, own, moves.at[0])
+    send = pltpu.make_async_copy(up, total_any, moves.at[1])
+
+    @pl.when(now == 0)
+    def _():
+        bring.start()
+        sums.start(lambda n, me: greet_all(n, me, m, line))
+        bring.wait()
+        for c in range(chunks):
+            down.launch(c)
+
+    sums.step(now, a_ref.at[0, 0])
+    for c in range(chunks):
+
+        @pl.when(now == 1 + c)
+        def _(c=c):
+            down.inward(c)
+
+        @pl.when(now == 3 + c)
+        def _(c=c):
+            down.outward(c)
+
+    k = lax.rem(now, per)
+    term = dg(x_ref[...], b_ref[...], TN)
+
+    @pl.when(k == 0)
+    def _():
+        acc[...] = term
+
+    @pl.when((k > 0) & (k < per - 1))
+    def _():
+        acc[...] += term
+
+    @pl.when(k == per - 1)
+    def _():
+        done = acc[...] + term
+        for t in range(grad_ref.shape[0]):
+            grad_ref[t] = done[:, 2 * t * TILE : 2 * (t + 1) * TILE].astype(BF)
 
     @pl.when(now == rows * n - 1)
     def _():
-        close(rows - 1)
-        scatter(rows - 1).drain(mine)
-
-
-def tile_sum(n, a, w, key):
+        for c in range(chunks):
+            down.drain(c)
+        send.start()
+        sums.end()
+        send.wait()
+
+
+BLOCKS = 4
+CHUNKS = 12
+
+
+def spread(n, m, a, w, x, down):
     rows, _, span, depth = a.shape
     width = w.shape[1]
-    half = span // 2
+    slots = depth // (2 * TILE)
+    everything = rows * n * span
+    per = rows * n // BLOCKS
+    part, block = everything // per, width // BLOCKS
+    flat = (slots * TILE // CHUNKS, width)
 
     def place(r, j):
         return (r, xor_of(lax.axis_index("mp"), n - 1 - j, n), 0, 0)
 
-    return pl.pallas_call(
-        functools.partial(tile_sum_kernel, n),
+    def token(r, j):
+        return lax.rem(r * n + j, per)
+
+    def column(r, j):
+        return lax.div(r * n + j, per)
+
+    hbm = pl.BlockSpec(memory_space=pl.ANY)
+    out, grad, total = pl.pallas_call(
+        functools.partial(spread_kernel, n, m),
         grid=(rows, n),
-        in_specs=[pl.BlockSpec((1, 1, span, depth), place), pl.BlockSpec(memory_space=pl.ANY)],
-        out_specs=pl.BlockSpec(memory_space=pltpu.VMEM),
-        out_shape=jax.ShapeDtypeStruct((rows, span, width), F32),
+        in_specs=[
+            pl.BlockSpec((1, 1, span, depth), place),
+            hbm,
+            pl.BlockSpec((part, block), lambda r, j: (token(r, j), column(r, j))),
+            pl.BlockSpec((part, depth), lambda r, j: (token(r, j), 0)),
+            hbm,
+        ],
+        out_specs=[
+            pl.BlockSpec(memory_space=pltpu.VMEM),
+            pl.BlockSpec((slots, block, 2 * TILE), lambda r, j: (0, column(r, j), 0)),
+            hbm,
+        ],
+        out_shape=[
+            jax.ShapeDtypeStruct((rows, span, width), F32),
+            jax.ShapeDtypeStruct((slots, width, 2 * TILE), BF),
+            jax.ShapeDtypeStruct((CHUNKS,) + flat, BF),
+        ],
         scratch_shapes=[
-            pltpu.VMEM(w.shape, BF),
-            pltpu.VMEM((n // 2 + 1, span, width), BF),
-            pltpu.VMEM((rows, n // 2, span, width), BF),
-            pltpu.VMEM((rows, 2, n // 2 - 1, half, width), BF),
-            pltpu.VMEM((n // 2 - 1, span, width), BF),
-            pltpu.SemaphoreType.DMA((rows, n // 2)),
-            pltpu.SemaphoreType.DMA((rows, n // 2)),
-            pltpu.SemaphoreType.DMA((rows, 2, n // 2 - 1)),
-            pltpu.SemaphoreType.DMA((rows, 2, n // 2 - 1)),
-            pltpu.SemaphoreType.DMA((1,)),
-        ],
-        compiler_params=params(mib=56, axes=2, key=key),
-        cost_estimate=pl.CostEstimate(
-            flops=2 * rows * n * span * depth * width,
-            bytes_accessed=2 * rows * n * span * depth + 2 * depth * width,
-            transcendentals=0,
-        ),
-        name="tile_sum",
-    )(a, w)
-
-
-def weight_kernel(finish, a_ref, b_ref, o_ref, acc):
-    k = pl.program_id(1)
-
-    @pl.when(k == 0)
-    def _():
-        acc[...] = jnp.zeros_like(acc)
-
-    acc[...] += dg(a_ref[...], b_ref[...], TN)
-
-    @pl.when(k == pl.num_programs(1) - 1)
-    def _():
-        finish(o_ref, acc)
-
-
-def weight_grad(left, right, block, stacked):
-    tokens, lw = left.shape
-    rw = right.shape[1]
-    block = min(block, lw)
-    step = 512
-    if stacked:
-        slots = rw // 256
-        out_spec = pl.BlockSpec((slots, block, 256), lambda i, k: (0, i, 0))
-        out_shape = jax.ShapeDtypeStruct((slots, lw, 256), BF)
-
-        def finish(o_ref, acc):
-            for t in range(slots):
-                o_ref[t] = acc[:, t * 256 : (t + 1) * 256].astype(BF)
-    else:
-        out_spec = pl.BlockSpec((block, rw), lambda i, k: (i, 0))
-        out_shape = jax.ShapeDtypeStruct((lw, rw), BF)
-
-        def finish(o_ref, acc):
-            o_ref[...] = acc[...].astype(BF)
-
-    return pl.pallas_call(
-        functools.partial(weight_kernel, finish),
-        grid=(lw // block, tokens // step),
-        in_specs=[
-            pl.BlockSpec((step, block), lambda i, k: (k, i)),
-            pl.BlockSpec((step, rw), lambda i, k: (k, 0)),
-        ],
-        out_specs=out_spec,
-        out_shape=out_shape,
-        scratch_shapes=[pltpu.VMEM((block, rw), F32)],
-        compiler_params=params(axes=2),
-        cost_estimate=pl.CostEstimate(
-            flops=2 * tokens * lw * rw,
-            bytes_accessed=2 * tokens * (lw + rw) + 2 * lw * rw,
-            transcendentals=0,
-        ),
-        name="weight_grad",
-    )(left, right)
+            pltpu.VMEM((block, depth), F32),
+            pltpu.VMEM((CHUNKS,) + flat, BF),
+            pltpu.VMEM((CHUNKS,) + flat, BF),
+            pltpu.VMEM((CHUNKS,) + flat, BF),
+            pltpu.SemaphoreType.DMA((6, CHUNKS)),
+            pltpu.SemaphoreType.DMA((2,)),
+        ]
+        + tile_scratch(n, rows, span, w),
+        compiler_params=params(mib=63, axes=2, key=3),
+        cost_estimate=TINY,
+        name="spread",
+    )(
+        a,
+        w,
+        x.reshape(everything, width),
+        a.reshape(everything, depth),
+        down.reshape((CHUNKS,) + flat),
+    )
+    return out, grad, total.reshape(down.shape)
 
 
 def shards(
     n,
+    m,
     hidden_in,
     doc_ids,
     tile_slot,
@@ -1117,17 +1450,19 @@
         1,
     ).astype(jnp.int32)
     start_col = jnp.broadcast_to(local_start[:, :, None], (rows, span, LANES))
-    start_row = jnp.broadcast_to(local_start[:, None, :], (rows, 8, span))
+    document = jnp.arange(LANES) % HD
+    member = (doc_ids[:, :, None] == document).astype(F32)
+    ka = jnp.where(document == DOCS, 1.0, member).astype(BF)
+    own_member = lax.dynamic_slice_in_dim(member, offset, span, 1)
+    qa = jnp.where(document == DOCS, -AWAY, own_member * AWAY).astype(BF)
 
     x_own = hidden_in.reshape(tokens, width)
     x_value = x_own.astype(F32)
-    scale_a = rms_scale(x_value)
     normed_ab, raw, q, attend_all, kv_all, output_all = project(
         n, rows, x_own, attention_gain[None], attend_w, output_weight, cos, sin, gq, gk, ones
     )
     q = q.reshape(rows, span, QW)
     kv_all = kv_all.reshape(rows, length, -1)
-    attend_full = attend_all.reshape(width, -1)
     output_full = output_all.reshape(QW, width)
     grad_branch, output_full = lax.optimization_barrier((out_grad.astype(BF), output_full))
     grads_all = lax.all_gather(grad_branch, "mp", axis=1, tiled=True)
@@ -1142,21 +1477,15 @@
     gu_t = jnp.swapaxes(gate_up_slots, 1, 2).reshape(slots * 2 * TILE, width)
     d_flat = down_slots.reshape(slots * TILE, width)
     d_t = d_flat.T
-    everything = rows * n * span
-    normed_all, hidden, grad_both = feed(
-        n, live, normed_fb, grads_all.reshape(rows, n, span, width), gate_up_slots, d_t
-    )
-    grad_down = weight_grad(
-        hidden.reshape(everything, -1), grads_all.reshape(everything, width), 768, False
-    ).reshape(slots, TILE, width)
-    grad_gate_up = weight_grad(
-        normed_all.reshape(everything, width), grad_both.reshape(everything, -1), 1024, True
-    )
-    gate_up_total, down_total = lax.psum((grad_gate_up, grad_down), "dp")
-    grad_both, grad_gate_up, grad_down = lax.optimization_barrier(
-        (grad_both, grad_gate_up, grad_down)
-    )
-    grad_normed_f = tile_sum(n, grad_both, gu_t, 3).reshape(tokens, width)
+    normed_all, hidden, grad_both, grad_down = feed(
+        n, live, normed_fb, grads_all, gate_up_slots, d_t
+    )
+    hidden = hidden.reshape(rows, n, span, -1)
+    grad_normed_f, grad_gate_up, down_total = spread(
+        n, m, grad_both.reshape(rows, n, span, -1), gu_t, normed_all, grad_down
+    )
+    gate_up_total = lax.psum(grad_gate_up, "dp")
+    grad_normed_f = grad_normed_f.reshape(tokens, width)
 
     weighted = grad_normed_f * feed_gain
     inner = jnp.mean(weighted * middle, axis=-1, keepdims=True)
@@ -1168,8 +1497,11 @@
     grad_context = dg(grad_attn_b, output_full, NT).astype(BF).reshape(rows, span, QW)
     grad_output = dg(context_b, grad_attn_b, TN).astype(BF)
 
-    dq, dkv = attend_back(info, q, kv_all, start_row, grad_context, ctx, rl)
-    grad_joined_b, sum_q, sum_k, attend_share, output_share = unproject(
+    dq, dkv, ffn_out = attend_back(
+        n, q, kv_all, qa, ka, grad_context, ctx, rl, hidden, d_flat
+    )
+    layer_out = middle + ffn_out.reshape(tokens, width)
+    grad_joined_b, sum_q, sum_k, output_share = unproject(
         n,
         dq.reshape(tokens, QW),
         dkv.reshape(rows, n, span, -1),
@@ -1179,18 +1511,29 @@
         gq,
         gk,
         ones,
+        grad_output.reshape(n, -1, width),
+    )
+    sums = jnp.concatenate(
+        [
+            jnp.zeros((width // LANES, LANES), F32),
+            gain_feed.reshape(-1, LANES),
+            sum_q[:1],
+            sum_k[:1],
+            jnp.zeros((GAIN_ROWS - 2 * (width // LANES) - 2, LANES), F32),
+        ]
+    )
+    input_grad, attend_total, output_total, gains = finish(
+        n,
+        m,
         normed_ab,
-        grad_output.reshape(n, -1, width),
-    )
-    grad_normed_a = dg(grad_joined_b, attend_full, NT)
-
-    hidden, attend_share = lax.optimization_barrier((hidden, attend_share))
-    layer_out = middle + tile_sum(n, hidden, d_flat, 4).reshape(tokens, width)
-    attend_share, output_share, gate_up_total, down_total = lax.optimization_barrier(
-        (attend_share, output_share, gate_up_total, down_total)
-    )
-    attend_total, output_total = lax.psum((attend_share, output_share), "dp")
-    attend_total = attend_total.astype(F32)
+        grad_joined_b,
+        attend_all,
+        x_own,
+        grad_middle,
+        attention_gain[None],
+        output_share,
+        sums,
+    )
     kv_total = attend_total[:, QW:].reshape(-1, KVH, 2, HD)
     attend_total = jnp.concatenate(
         [
@@ -1200,13 +1543,7 @@
         ],
         1,
     )
-    weighted_a = grad_normed_a * attention_gain
-    inner_a = jnp.mean(weighted_a * x_value, axis=-1, keepdims=True)
-    gain_attention = jnp.sum(grad_normed_a * x_value * scale_a, axis=0)
-    input_grad = grad_middle + scale_a * (weighted_a - x_value * scale_a * scale_a * inner_a)
-
-    gains = jnp.concatenate([gain_attention, gain_feed, sum_q[0], sum_k[0]])
-    gains = lax.psum(gains, ("dp", "mp"))
+    gains = gains.reshape(-1)
     gain_query = gains[2 * width : 2 * width + HD] + gains[2 * width + HD : 2 * width + 2 * HD]
     gain_key = gains[2 * width + LANES : 2 * width + LANES + HD]
     shape = (rows, span, width)
@@ -1214,7 +1551,7 @@
         layer_out.reshape(shape),
         input_grad.reshape(shape),
         attend_total,
-        output_total.astype(F32),
+        output_total,
         gate_up_total.astype(F32),
         down_total.astype(F32),
         gains[:width],
@@ -1240,7 +1577,7 @@
         P("dp", "mp", None),
     )
     return jax.shard_map(
-        functools.partial(shards, mesh.shape["mp"]),
+        functools.partial(shards, mesh.shape["mp"], mesh.shape["dp"]),
         mesh=mesh,
         in_specs=placed,
         out_specs=(

time: 863 us -> 800 us (0.927)
  waiting for transfers between devices: 100 us -> 50.9 us
  blocking collectives: 42.8 us -> 0 us
  Pallas kernels: 604 us -> 634 us
  matrix products: 24.7 us -> 15.6 us
    pallas_call x6 -> x4, Pallas kernels: 348 us -> 448 us  [the longest x1 132 us: finish(): pl.pallas_call(functools.partial(finish_kernel, n, m), in_specs=[vmem, vm...]
    pallas_call x1, Pallas kernels: 151 us -> 80.4 us  [unproject(): pl.pallas_call(functools.partial(unproject_kernel, n), in_specs=[vmem] *...]
    psum x2 -> x1, waiting for transfers between devices: 50.5 us -> 0.01 us  [shards(): gate_up_total = lax.psum(grad_gate_up, 'dp')]
    psum x1 -> x0, blocking collectives: 42.8 us -> none  [shards(): gains = lax.psum(gains, ('dp', 'mp'))]
    dot_general x3 -> x2, matrix products: 19.4 us -> 11.3 us  [dg(): return lax.dot_general(a, b, dims, preferred_element_type=F32)]
  transfers between devices with their start and end apart: 3 -> 2, of which waited for: 2 -> 1; matrix products, arithmetic and copies ran while one was open for 8% -> 8% of each run, Pallas kernels for 44% -> 41%
where the time goes in v3:
time: 800 us; the launch traced here: 794 us
  Pallas kernels  634 us (79%)
  waiting for transfers between devices  50.9 us (6%)
  other arithmetic  43.1 us (5%)
  local copies, waits for them, and re-layouts  35.1 us (4%)
  matrix products  15.6 us (2%)
  between operations  14.9 us (2%)
    pallas_call x1, Pallas kernels, finish(): pl.pallas_call(functools.partial(finish_kernel, n, m), in_specs=[vmem, vm...  132 us
    pallas_call x1, Pallas kernels, spread(): pl.pallas_call(functools.partial(spread_kernel, n, m), grid=(rows, n), in...  114 us
    pallas_call x1, Pallas kernels, feed(): pl.pallas_call(functools.partial(feed_kernel, n), grid=(rows, pairs), in_...  105 us
    pallas_call x1, Pallas kernels, attend_back(): pl.pallas_call(functools.partial(attend_back_kernel, keys, n), grid=(rows...  96.4 us
    pallas_call x1, Pallas kernels, project(): pl.pallas_call(functools.partial(project_kernel, n), in_specs=[vmem, vmem...  89.3 us
    pallas_call x1, Pallas kernels, unproject(): pl.pallas_call(functools.partial(unproject_kernel, n), in_specs=[vmem] *...  80.4 us
    all_gather x1, waiting for transfers between devices, shards(): grads_all = lax.all_gather(grad_branch, 'mp', axis=1, tiled=True)  50.9 us
    pallas_call x1, Pallas kernels, attend(): pl.pallas_call(functools.partial(attend_kernel, keys), grid_spec=spec, ou...  16.6 us
  transfers between devices with their start and end apart: 2, of which 1 were waited for; matrix products, arithmetic and copies ran while one was open for 8% of the time, Pallas kernels for 41%

profile of v3, /device:TPU:0, one launch (start us, length us, event | category | flops | bytes accessed | tf_op | source)
XLA Modules:
  0.0 794.3 jit_solution(13003490500176189216)
XLA Ops:
  7.3 1.1 fusion.5
  8.4 2.0 slice.72
  16.9 3.9 convert_element_type.58
  20.7 2.3 pad_maximum_fusion.w_ref
  23.0 89.3 %project.1 = (bf16[512,2048]{1,0:T(8,128)(2,1)}, f32[512,1920]{1,0:T(8,128)}, bf16[512,1280]{1,0:T(8,128)(2,1)}, bf16[8,256,1920]{2,1,0:T(8,128)(2,1)}, bf16[2,8...) custom-call(bf16[512,2048]{1,0:T(8,128)(2,1)} %bitcast.84, f32[1,2048]{1,0:T(1,128)} %bitcast.113, ...), custom_call_target="tpu_custom_call" | custom-call | tf_op jit(solution)/shard_map/project/pallas_call | solution.py:499
  113.6 2.8 copy.41.dt_any
  116.4 9.1 %copy.42 = bf16[6,256,2048]{2,1,0:T(8,128)(2,1)} copy(bf16[6,256,2048]{1,2,0:T(8,128)(2,1)} %bitcast.87) | data formatting | bytes 12582912 | tf_op jit(solution)/shard_map/transpose | solution.py:1477
  127.0 16.6 %attend.1 = (bf16[2,256,1280]{2,1,0:T(8,128)(2,1)}, f32[2,256,1280]{2,1,0:T(8,128)}) custom-call(s32[2,3]{1,0:T(2,128)} %pad_add_fusion.info, bf16[2,256,1280]{2,1,0:T(8,128)(2,1)} %bitcast.103, bf16[2,2048,640]{2,1,0:T(8,128)(2,1)} %bitcast.91, s32[2,256,128]{2,1,0:T(8,128)} %broadcast_in_dim.61.start_ref), custom_call_target="tpu_custom_call" | custom-call | flops 21474836480 | bytes 10485760 | tf_op jit(solution)/shard_map/attend/pallas_call | solution.py:850
  143.7 4.3 multiply_reduce_fusion.1
  148.0 2.0 copy-done
  150.0 1.8 multiply_convert_fusion
  151.8 50.9 %all-gather.2.cloned.1.call-done = bf16[2,2048,2048]{2,1,0:T(8,128)(2,1)} async-done(((bf16[2,256,2048]{2,1,0:T(8,128)(2,1)}), bf16[2,2048,2048]{2,1,0:T(8,128)(2,1)}) %all-gather.2.cloned.1.call-update) | async-done | bytes 16777232 | tf_op jit(solution)/shard_map/all_gather | solution.py:1468
  202.7 105.4 %feed.1 = (bf16[2,4,512,2048]{3,2,1,0:T(8,128)(2,1)}, bf16[2,4,512,768]{3,2,1,0:T(8,128)(2,1)}, bf16[2,4,512,1536]{3,2,1,0:T(8,128)(2,1)}, bf16[6,128,2048]{2,1,0:T(8,128)(2,1)}) custom-call(f32[6]{0:T(128)} %convert_element_type.62.live_ref, bf16[2,256,2048]{2,1,0:T(8,128)(2,1)} %bitcast.99, bf16[2,4,512,2048]{3,2,1,0:T(8,128)(2,1)} %bitcast.121, ...), custom_call_target="tpu_custom_call" | custom-call | flops 77309411328 | bytes 59768832 | tf_op jit(solution)/shard_map/feed/pallas_call | solution.py:1144
  308.1 113.7 %spread.1 = (f32[2,256,2048]{2,1,0:T(8,128)}, bf16[6,2048,256]{2,1,0:T(8,128)(2,1)}, bf16[12,64,2048]{2,1,0:T(8,128)(2,1)}) custom-call(bf16[2,8,256,1536]{3,2,1,0:T(8,128)(2,1)} %bitcast.78, bf16[1536,2048]{1,0:T(8,128)(2,1)} %bitcast.80, bf16[4096,2048]{1,0:T(8,128)(2,1)} %bitcast.81, bf16[4096,1536]{1,0:T(8,128)(2,1)} %bitcast.79, ...), custom_call_target="tpu_custom_call" | custom-call | flops 1 | bytes 1 | tf_op jit(solution)/shard_map/spread/pallas_call | solution.py:1364
  423.9 2.0 select_convert_fusion.ka_ref
  425.9 5.8 fusion.1
  431.7 1.2 copy-done.3
  433.0 3.9 bitcast_add_fusion.1.mid_ref
  437.0 4.0 convolution_convert_fusion.1
  441.0 96.4 %attend_back.1 = (f32[2,256,1280]{2,1,0:T(8,128)}, bf16[2,2048,640]{2,1,0:T(8,128)(2,1)}, f32[2,256,2048]{2,1,0:T(8,128)}) custom-call(bf16[2,256,1280]{2,1,0:T(8,128)(2,1)} %bitcast.104, bf16[2,2048,640]{2,1,0:T(8,128)(2,1)} %bitcast.92, bf16[2,256,128]{2,1,0:T(8,128)(2,1)} %select_convert_fusion.1.qa_ref, bf16[2,2048,128]{2,1,0:T(8,128)(2,1)} %select_convert_fusion.ka_ref, ...), custom_call_target="tpu_custom_call" | custom-call | flops 1 | bytes 1 | tf_op jit(solution)/shard_map/attend_back/pallas_call | solution.py:975
  537.4 7.3 convolution_convert_fusion
  544.6 80.4 %unproject.1 = (bf16[512,1920]{1,0:T(8,128)(2,1)}, f32[8,128]{1,0:T(8,128)}, f32[8,128]{1,0:T(8,128)}, bf16[160,2048]{1,0:T(8,128)(2,1)}) custom-call(f32[512,1280]{1,0:T(8,128)} %bitcast.97, bf16[2,8,256,640]{3,2,1,0:T(8,128)(2,1)} %bitcast.89, f32[512,1920]{1,0:T(8,128)} %get-tuple-element.54.raw_ref, f32[512,128]{1,0:T(8,128)} %copy.39.cos_ref, ...), custom_call_target="tpu_custom_call" | custom-call | flops 1 | bytes 1 | tf_op jit(solution)/shard_map/unproject/pallas_call | solution.py:612
  626.4 1.8 concatenate.22.sums_ref
  628.3 132.1 %finish.1 = (f32[512,2048]{1,0:T(8,128)}, f32[256,1920]{1,0:T(8,128)}, f32[160,2048]{1,0:T(8,128)}, f32[40,128]{1,0:T(8,128)}) custom-call(bf16[512,2048]{1,0:T(8,128)(2,1)} %get-tuple-element.51.normed_ref, bf16[512,1920]{1,0:T(8,128)(2,1)} %get-tuple-element.55.gj_ref, bf16[8,256,1920]{2,1,0:T(8,128)(2,1)} %get-tuple-element.56.w_any, ...), custom_call_target="tpu_custom_call" | custom-call | flops 1 | bytes 1 | tf_op jit(solution)/shard_map/finish/pallas_call | solution.py:752
  760.4 1.1 slice.78
  761.5 1.4 slice.77
  763.6 1.6 concatenate.23
  766.3 5.6 bitcast_convert_fusion
  772.0 2.8 bitcast_add_fusion
  774.8 8.9 %convert_element_type.67 = f32[6,2048,256]{2,1,0:T(8,128)} convert(bf16[6,2048,256]{2,1,0:T(8,128)(2,1)} %all-reduce.4.cloned.1.call-done) | non-fusion elementwise | flops 3145728 | bytes 18874368 | tf_op jit(solution)/shard_map/convert_element_type | solution.py:1555
  783.7 2.0 copy.60
  785.9 1.1 copy.61
  (95 shorter events, 14.7 us)
Async XLA Ops:
  7.2 8.6 %copy-start.14 = (f32[64]{0:T(128)S(1)}, f32[64]{0:T(128)}, u32[]{:S(2)}) copy-start(f32[64]{0:T(128)} %param.16) | copy-start | bytes 772
  7.2 9.2 %copy-start.15 = (f32[64]{0:T(128)S(1)}, f32[64]{0:T(128)}, u32[]{:S(2)}) copy-start(f32[64]{0:T(128)} %param.17) | copy-start | bytes 772
  7.2 195.5 %all-gather.2.cloned.1.call-start = ((), (), s32[]{:S(2)}) async-start(), calls=%async_computation | async-start | bytes 18874368 | tf_op jit(solution)/shard_map/all_gather | solution.py:1468
  20.7 92.2 %copy-start.16 = (s32[44]{0:T(128)S(1)}, s32[44]{0:T(128)}, u32[]{:S(2)}) copy-start(s32[44]{0:T(128)} %param.14) | copy-start | bytes 532
  20.7 92.9 %copy-start.5 = (bf16[6,128,2048]{2,1,0:T(8,128)(2,1)S(1)}, bf16[6,128,2048]{2,1,0:T(8,128)(2,1)}, u32[]{:S(2)}) copy-start(bf16[6,128,2048]{2,1,0:T(8,128)(2,1)} %param.22) | copy-start | bytes 9437188
  112.3 662.5 %all-reduce.4.cloned.1.call-start = ((), (), s32[]{:S(2)}) async-start(), calls=%async_computation.1 | async-start | bytes 12582912 | tf_op jit(solution)/shard_map/psum | solution.py:1487
  116.4 27.2 %slice-start = ((s8[5242880]{0:T(1024)(128)(4,1)}), s8[1048576]{0:T(1024)(128)(4,1)S(1)}, s32[]{:S(2)}) async-start(s8[5242880]{0:T(1024)(128)(4,1)} %bitcast.122), calls=%async_computation.2 | async-start | bytes 2097152
  127.0 16.6 %copy-start.6 = (bf16[2,256,2048]{2,1,0:T(8,128)(2,1)S(1)}, bf16[2,256,2048]{2,1,0:T(8,128)(2,1)}, u32[]{:S(2)}) copy-start(bf16[2,256,2048]{2,1,0:T(8,128)(2,1)} %param.12) | copy-start | bytes 6291460
  127.0 16.6 %slice-start.1 = ((s8[5242880]{0:T(1024)(128)(4,1)}), s8[4194304]{0:T(1024)(128)(4,1)S(1)}, s32[]{:S(2)}) async-start(s8[5242880]{0:T(1024)(128)(4,1)} %bitcast.122), calls=%async_computation.3 | async-start | bytes 8388608
  143.7 6.4 copy-start.12
  148.0 2.0 copy-start
  421.8 0.7 copy-start.11
  425.9 5.8 copy-start.1
  425.9 7.1 copy-start.3
  425.9 11.0 %slice-start.2 = ((s8[5242880]{0:T(1024)(128)(4,1)}), s8[4194304]{0:T(1024)(128)(4,1)S(1)}, s32[]{:S(2)}) async-start(s8[5242880]{0:T(1024)(128)(4,1)} %bitcast.125), calls=%async_computation.4 | async-start | bytes 8388608
  433.0 3.9 slice-start.3
  437.0 4.0 copy-start.4
  441.0 96.4 %copy-start.10 = (bf16[2,256,1280]{2,1,0:T(8,128)(2,1)S(1)}, bf16[2,256,1280]{2,1,0:T(8,128)(2,1)}, u32[]{:S(2)}) copy-start(bf16[2,256,1280]{2,1,0:T(8,128)(2,1)} %get-tuple-element.40.ctx_ref) | copy-start | bytes 3932164
  762.9 2.2 copy-start.13
  766.3 5.6 copy-start.2
  766.3 5.6 copy-start.7
  774.8 8.9 %copy-start.8 = (f32[512,2048]{1,0:T(8,128)S(1)}, f32[512,2048]{1,0:T(8,128)}, u32[]{:S(2)}) copy-start(f32[512,2048]{1,0:T(8,128)} %get-tuple-element.60) | copy-start | bytes 12582916
  783.7 2.3 copy-start.9
Sparse Core Ops, SparseCore 0:
  112.5 90.2 all-gather.1
  422.0 225.2 all-reduce.3

commit v4 on v3

--- a/solution.py
+++ b/solution.py
@@ -278,7 +278,7 @@
 
     def even(self, k, ref):
         self.core_copy(k + 1, self.core(k // 2)).wait_recv()
-        for half in (0, 1):
+        for half in sorted((0, 1), key=lambda h: -len(self.addends(k, h))):
             joined = [self.part(ref, half), self.part(self.core(k // 2), half)]
             for j in self.addends(k, half):
                 self.link_copy(j, half).wait_recv()
@@ -357,8 +357,8 @@
 
 
 def project_kernel(
-    n, x_ref, gain_ref, w_ref, o_ref, cos_ref, sin_ref, gq_ref, gk_ref, ones_ref,
-    normed_ref, raw_ref, q_ref, w_out, kv_out, o_out,
+    n, x_ref, gain_ref, w_ref, o_ref, cos_ref, sin_ref, gq_ref, gk_ref, ones_ref, grad_ref,
+    normed_ref, raw_ref, q_ref, branch_ref, w_out, kv_out, o_out,
     w_all, kv_own, w_send, w_recv, kv_send, kv_recv, o_send, o_recv, local,
 ):
     me = lax.axis_index("mp")
@@ -398,6 +398,7 @@
         x = x_ref[at, :].astype(F32)
         scale = lax.rsqrt(jnp.mean(x * x, axis=-1, keepdims=True) + EPSILON)
         normed_ref[at, :] = (x * scale * gain_ref[...]).astype(BF)
+        branch_ref[at, :] = grad_ref[at, :].astype(BF)
 
     chunk = min(256, tokens)
 
@@ -490,7 +491,7 @@
     kvs.drain()
 
 
-def project(n, rows, x, gain, w, o, cos, sin, gq, gk, ones):
+def project(n, rows, x, gain, w, o, cos, sin, gq, gk, ones, grad):
     tokens, width = x.shape
     depth, columns = w.shape
     vmem = pl.BlockSpec(memory_space=pltpu.VMEM)
@@ -498,12 +499,13 @@
     kvw = columns - QW
     return pl.pallas_call(
         functools.partial(project_kernel, n),
-        in_specs=[vmem, vmem, hbm, hbm, vmem, vmem, vmem, vmem, vmem],
-        out_specs=[vmem, vmem, vmem, hbm, hbm, hbm],
+        in_specs=[vmem, vmem, hbm, hbm, vmem, vmem, vmem, vmem, vmem, vmem],
+        out_specs=[vmem, vmem, vmem, vmem, hbm, hbm, hbm],
         out_shape=[
             jax.ShapeDtypeStruct((tokens, width), BF),
             jax.ShapeDtypeStruct((tokens, columns), F32),
             jax.ShapeDtypeStruct((tokens, QW), BF),
+            jax.ShapeDtypeStruct((tokens, width), BF),
             jax.ShapeDtypeStruct((n, depth, columns), BF),
             jax.ShapeDtypeStruct((rows, n, tokens // rows, kvw), BF),
             jax.ShapeDtypeStruct((n,) + o.shape, BF),
@@ -521,12 +523,12 @@
         ],
         compiler_params=params(axes=0, key=0),
         name="project",
-    )(x, gain, w, o, cos, sin, gq, gk, ones)
+    )(x, gain, w, o, cos, sin, gq, gk, ones, grad)
 
 
 def unproject_kernel(
-    n, dq_ref, dkv_ref, raw_ref, cos_ref, sin_ref, gq_ref, gk_ref, ones_ref, gout_ref,
-    gj_ref, sq_ref, sk_ref, output_ref,
+    n, dq_ref, dkv_ref, raw_ref, cos_ref, sin_ref, gq_ref, gk_ref, ones_ref, down_ref,
+    gj_ref, sq_ref, sk_ref, wide_ref,
     dkv_own, *scratch,
 ):
     me = lax.axis_index("mp")
@@ -536,23 +538,13 @@
     span = tokens // rows
     columns = raw_ref.shape[1]
     keys = make_scatter(n, me, lambda ref, h: ref.at[h], scratch[:6])
-    half_w = output_ref.shape[1] // 2
-    outs = make_scatter(
-        n, me, lambda ref, h: ref.at[:, pl.ds(h * half_w, half_w)], scratch[6:12]
-    )
 
     def dkv_term(k):
         return dkv_ref.at[:, flip(me, k)]
 
-    def out_term(k):
-        return gout_ref.at[flip(me, k)]
-
     for k in range(n - 1, 0, -2):
         keys.odd(k, dkv_term(k))
-    for k in range(n - 2, 0, -2):
-        keys.even(k, dkv_term(k))
-    for k in range(n - 1, 0, -2):
-        outs.odd(k, out_term(k))
+    keys.even(n - 2, dkv_term(n - 2))
 
     chunk = min(128, tokens)
     lane = lax.broadcasted_iota(jnp.int32, (chunk, LANES), 1)
@@ -584,30 +576,29 @@
 
     count = columns // LANES
 
-    @pl.loop(0, tokens // chunk)
-    def _(i):
+    parts = tokens // chunk
+    left = list(range(n - 4, 0, -2))
+    for i in range(parts):
         back(i, range(QW // LANES), True)
-
-    for k in range(n - 2, 0, -2):
-        outs.even(k, out_term(k))
-
+        if i == 0:
+            for k in left:
+                keys.even(k, dkv_term(k))
+
+    wide_ref[...] = down_ref[...].astype(F32)
     keys.own(dkv_term(0), dkv_own)
 
     @pl.loop(0, tokens // chunk)
     def _(i):
         back(i, range(QW // LANES, count), False)
 
-    outs.own(out_term(0), output_ref)
     keys.drain(dkv_term(0))
-    outs.drain(out_term(0))
-
-
-def unproject(n, dq, dkv, raw, cos, sin, gq, gk, ones, gout):
+
+
+def unproject(n, dq, dkv, raw, cos, sin, gq, gk, ones, down):
     tokens, columns = raw.shape
     rows = dkv.shape[0]
     span = tokens // rows
     kvw = columns - QW
-    width = gout.shape[2]
     vmem = pl.BlockSpec(memory_space=pltpu.VMEM)
     return pl.pallas_call(
         functools.partial(unproject_kernel, n),
@@ -617,41 +608,51 @@
             jax.ShapeDtypeStruct((tokens, columns), BF),
             jax.ShapeDtypeStruct((8, LANES), F32),
             jax.ShapeDtypeStruct((8, LANES), F32),
-            jax.ShapeDtypeStruct((QW // n, width), BF),
+            jax.ShapeDtypeStruct(down.shape, F32),
         ],
         scratch_shapes=[pltpu.VMEM((rows, span, kvw), F32)]
-        + scatter_scratch(n, (rows, span, kvw), (span, kvw))
-        + scatter_scratch(n, (QW // n, width), (QW // n, width // 2)),
+        + scatter_scratch(n, (rows, span, kvw), (span, kvw)),
         compiler_params=params(mib=60, axes=0, key=2),
         cost_estimate=TINY,
         name="unproject",
-    )(dq, dkv, raw, cos, sin, gq, gk, ones, gout)
+    )(dq, dkv, raw, cos, sin, gq, gk, ones, down)
 
 
 GAIN_ROWS = 40
 
 
 def finish_kernel(
-    n, m, normed_ref, gj_ref, w_any, x_ref, mid_ref, gain_ref, output_ref, sums_ref,
+    n, m, normed_ref, gj_ref, w_any, x_ref, mid_any, gain_ref, gout_any, sums_ref,
     grad_ref, attend_ref, out_ref, gains_ref,
-    w_ref, term, error, own_w, up_w, across_w, total_w, own_o, up_o, across_o, total_o, landed,
+    w_ref, term, error, mid_ref, gout_ref, own_w, up_w, across_w, own_o, up_o, across_o, landed,
     sem_w, sem_o, sem_g, load, *scratch,
 ):
     me, line = lax.axis_index("mp"), lax.axis_index("dp")
     depth = w_ref.shape[1]
     tokens, width = x_ref.shape
     pieces, piece = own_w.shape[0], own_w.shape[1]
-    fetch = pltpu.make_async_copy(w_any, w_ref, load.at[0])
-    fetch.start()
+    o_pieces, o_piece = own_o.shape[0], own_o.shape[1]
+    chunk = error.shape[0]
+    fetch = [pltpu.make_async_copy(w_any, w_ref, load.at[0])]
+    fetch += [
+        pltpu.make_async_copy(gout_any.at[flip(me, k)], gout_ref.at[k // 2], load.at[2 + k // 2])
+        for k in range(0, n, 2)
+    ]
+    for c in fetch:
+        c.start()
+
+    def bring(i):
+        here = pl.ds(pl.multiple_of(i * chunk, chunk), chunk)
+        return pltpu.make_async_copy(mid_any.at[here], mid_ref, load.at[1])
+
+    bring(0).start()
     greet_all(n, me, m, line)
-    half = depth // 2
-    sums = make_scatter(n, me, lambda ref, h: ref.at[pl.ds(h * half, half)], scratch)
+    half, half_w = depth // 2, width // 2
+    sums = make_scatter(n, me, lambda ref, h: ref.at[pl.ds(h * half, half)], scratch[:6])
+    outs = make_scatter(n, me, lambda ref, h: ref.at[:, pl.ds(h * half_w, half_w)], scratch[6:])
     at = lambda ref: lambda c: ref.at[c]
-    weights = Line(m, line, at(own_w), at(up_w), at(across_w), at(total_w), sem_w)
-    outs = Line(m, line, at(own_o), at(up_o), at(across_o), at(total_o), sem_o)
-    own_o[0] = output_ref[...]
-
-    chunk = error.shape[0]
+    weights = Line(m, line, at(own_w), at(up_w), at(across_w), at(up_w), sem_w)
+    out_line = Line(m, line, at(own_o), at(up_o), at(across_o), at(up_o), sem_o)
     gains_ref[...] = sums_ref[...]
 
     def tokens_part(i):
@@ -659,6 +660,7 @@
         for b in range(n):
             error[:, b * depth : (b + 1) * depth] = dg(gj_ref[here, :], w_ref[b], NT)
         small = min(32, chunk)
+        bring(i).wait()
 
         @pl.loop(0, chunk // small)
         def _(s):
@@ -670,42 +672,21 @@
             u = e * gain_ref[...]
             v = x * scale
             inner = jnp.mean(u * v, axis=-1, keepdims=True)
-            grad_ref[rows, :] = mid_ref[rows, :] + scale * (u - v * inner)
+            grad_ref[rows, :] = mid_ref[part, :] + scale * (u - v * inner)
             total = jnp.sum(e * v, axis=0, keepdims=True)
             for b in range(width // LANES):
                 gains_ref[b : b + 1, :] += total[:, b * LANES : (b + 1) * LANES]
 
+        if i + 1 < tokens // chunk:
+            bring(i + 1).start()
+
+    def mine(k):
+        return term.at[k // 2 if k % 2 else n // 2]
+
     def weight_part(k):
         columns = pl.ds(pl.multiple_of(flip(me, k) * depth, depth), depth)
-        term[k] = dg(normed_ref[:, columns], gj_ref[...], TN).astype(BF)
-
-    parts = tokens // chunk
-    left = list(range(parts))
-    outs.launch(0)
-    outs.inward(0)
-    for k in range(n - 1, 0, -1):
-        weight_part(k)
-        if k % 2:
-            sums.odd(k, term.at[k])
-        else:
-            sums.even(k, term.at[k])
-        if k == n - 1:
-            fetch.wait()
-    weight_part(0)
-
-    def span_of(first, last):
-        @pl.loop(first, last)
-        def _(i):
-            tokens_part(i)
-
-    span_of(0, parts // 2)
-    outs.outward(0)
-    span_of(parts // 2, parts)
-    sums.own(term.at[0], attend_ref)
-    for c in range(pieces):
-        own_w[c] = attend_ref[c * piece : (c + 1) * piece, :].astype(BF)
-        weights.launch(c)
-        weights.inward(c)
+        mine(k)[...] = dg(normed_ref[:, columns], gj_ref[...], TN).astype(BF)
+
     steps = [("mp", flip(me, 1 << i)) for i in range(n.bit_length() - 1)]
     steps += [("dp", flip(line, 1 << i)) for i in range(m.bit_length() - 1)]
 
@@ -720,64 +701,122 @@
             device_id_type=MESH,
         )
 
-    done = 0
+    for k in range(n - 1, 0, -2):
+        weight_part(k)
+        sums.odd(k, mine(k))
+        if k == n - 1:
+            weight_part(n - 2)
+            sums.even(n - 2, mine(n - 2))
+    for c in fetch:
+        c.wait()
+    tokens_part(0)
+    for k in range(n - 4, 0, -2):
+        weight_part(k)
+        sums.even(k, mine(k))
+    weight_part(0)
+    for i in range(1, tokens // chunk):
+        tokens_part(i)
     for i in range(len(steps)):
         landed[2 * i] = gains_ref[...]
         exchange(i).start()
-        if done < pieces and i % 2:
-            weights.outward(done)
-            done += 1
         exchange(i).wait_recv()
         gains_ref[...] = landed[2 * i] + landed[2 * i + 1]
-    for c in range(done, pieces):
-        weights.outward(c)
+    sums.own(mine(0), attend_ref)
     for c in range(pieces):
-        attend_ref[c * piece : (c + 1) * piece, :] = total_w[c].astype(F32)
-    out_ref[...] = total_o[0].astype(F32)
+        own_w[c] = attend_ref[c * piece : (c + 1) * piece, :].astype(BF)
+        weights.launch(c)
+
+    def out_term(k):
+        return gout_any.at[flip(me, k)] if k % 2 else gout_ref.at[k // 2]
+
+    for k in range(n - 1, 0, -2):
+        outs.odd(k, out_term(k))
+    todo = list(range(n - 2, 0, -2))
+    ahead = 2
+    for c in range(pieces + ahead):
+        if c < pieces:
+            weights.inward(c)
+        if c >= ahead:
+            weights.outward(c - ahead)
+        if todo:
+            k = todo.pop(0)
+            outs.even(k, out_term(k))
+    for k in todo:
+        outs.even(k, out_term(k))
+    outs.own(out_term(0), out_ref)
+    for c in range(o_pieces):
+        own_o[c] = out_ref[c * o_piece : (c + 1) * o_piece, :].astype(BF)
+        out_line.launch(c)
+    kw = KVH * HD
+
+    def widen(c):
+        rows = slice(c * piece, (c + 1) * piece)
+        attend_ref[rows, :QW] = up_w[c, :, :QW].astype(F32)
+        for h in range(KVH):
+            both = up_w[c, :, QW + 2 * h * HD : QW + 2 * (h + 1) * HD].astype(F32)
+            attend_ref[rows, QW + h * HD : QW + (h + 1) * HD] = both[:, :HD]
+            attend_ref[rows, QW + kw + h * HD : QW + kw + (h + 1) * HD] = both[:, HD:]
+
+    for c in range(max(o_pieces + ahead, pieces)):
+        if c < o_pieces:
+            out_line.inward(c)
+        if c < pieces:
+            widen(c)
+        if ahead <= c < o_pieces + ahead:
+            out_line.outward(c - ahead)
+    for c in range(o_pieces):
+        out_ref[c * o_piece : (c + 1) * o_piece, :] = up_o[c].astype(F32)
+        out_line.drain(c)
     for c in range(pieces):
         weights.drain(c)
-    outs.drain(0)
     for i in range(len(steps)):
         exchange(i).wait_send()
-    sums.drain(term.at[0])
-
-
-def finish(n, m, normed, gj, w, x, middle, gain, output_share, sums):
+    sums.drain(mine(0))
+    outs.drain(out_term(0))
+
+
+def finish(n, m, normed, gj, w, x, middle, gain, gout, sums):
     tokens, width = x.shape
     columns = gj.shape[1]
     depth = width // n
-    pieces = 4
+    share = gout.shape[1]
+    pieces, o_pieces = 8, 5
+    chunk = min(256, tokens)
     vmem = pl.BlockSpec(memory_space=pltpu.VMEM)
+    hbm = pl.BlockSpec(memory_space=pl.ANY)
     steps = n.bit_length() + m.bit_length() - 2
     return pl.pallas_call(
         functools.partial(finish_kernel, n, m),
-        in_specs=[vmem, vmem, pl.BlockSpec(memory_space=pl.ANY)] + [vmem] * 5,
+        in_specs=[vmem, vmem, hbm, vmem, hbm, vmem, hbm, vmem],
         out_specs=[vmem] * 4,
         out_shape=[
             jax.ShapeDtypeStruct((tokens, width), F32),
             jax.ShapeDtypeStruct((depth, columns), F32),
-            jax.ShapeDtypeStruct(output_share.shape, F32),
+            jax.ShapeDtypeStruct((share, width), F32),
             jax.ShapeDtypeStruct((GAIN_ROWS, LANES), F32),
         ],
         scratch_shapes=[
             pltpu.VMEM(w.shape, BF),
-            pltpu.VMEM((n, depth, columns), BF),
-            pltpu.VMEM((min(256, tokens), width), F32),
+            pltpu.VMEM((n // 2 + 1, depth, columns), BF),
+            pltpu.VMEM((chunk, width), F32),
+            pltpu.VMEM((chunk, width), F32),
+            pltpu.VMEM((n // 2, share, width), BF),
         ]
-        + [pltpu.VMEM((pieces, depth // pieces, columns), BF)] * 4
-        + [pltpu.VMEM((1,) + output_share.shape, BF)] * 4
+        + [pltpu.VMEM((pieces, depth // pieces, columns), BF)] * 3
+        + [pltpu.VMEM((o_pieces, share // o_pieces, width), BF)] * 3
         + [
             pltpu.VMEM((2 * steps, GAIN_ROWS, LANES), F32),
             pltpu.SemaphoreType.DMA((6, pieces)),
-            pltpu.SemaphoreType.DMA((6, 1)),
+            pltpu.SemaphoreType.DMA((6, o_pieces)),
             pltpu.SemaphoreType.DMA((2, steps)),
-            pltpu.SemaphoreType.DMA((1,)),
+            pltpu.SemaphoreType.DMA((2 + n // 2,)),
         ]
-        + scatter_scratch(n, (depth, columns), (depth // 2, columns)),
+        + scatter_scratch(n, (depth, columns), (depth // 2, columns))
+        + scatter_scratch(n, (share, width), (share, width // 2)),
         compiler_params=params(mib=60, axes=0, key=5),
         cost_estimate=TINY,
         name="finish",
-    )(normed, gj, w, x, middle, gain, output_share, sums)
+    )(normed, gj, w, x, middle, gain, gout, sums)
 
 
 def key_positions(shape, axis, group, per, span):
@@ -862,7 +901,7 @@
 
 
 def attend_back_kernel(
-    keys, n, q_ref, kv_ref, qa_ref, ka_ref, do_ref, ctx_ref, rl_ref, a_ref, w_any,
+    keys, n, q_ref, kv_ref, qa_ref, ka_ref, do_ref, ctx_ref, rl_ref, a_ref, w_any, base_any,
     dq_ref, dkv_ref, o_ref, acc, sides, *scratch,
 ):
     span = q_ref.shape[1]
@@ -871,7 +910,7 @@
     me = lax.axis_index("mp")
     rows = o_ref.shape[0]
     now = pl.program_id(0) * KVH + pl.program_id(1)
-    sums = TileSum(n, me, o_ref, w_any, scratch)
+    sums = TileSum(n, me, o_ref, w_any, scratch, base_any)
     batch = a_ref.shape[1]
     steps = rows * n // batch
 
@@ -884,7 +923,7 @@
         @pl.loop(0, batch)
         def _(i):
             tile = now * batch + i
-            slot = n - 1 - lax.rem(tile, n)
+            _, slot = tile_at(tile, n)
             sums.step(tile, a_ref.at[0, lax.rem(xor_of(me, slot, n), batch)])
 
     lane = lax.broadcasted_iota(jnp.int32, (span, LANES), 1)
@@ -957,20 +996,17 @@
         sums.end()
 
 
-def attend_back(n, q, kv, qa, ka, do, ctx, rl, a, w):
+def attend_back(n, q, kv, qa, ka, do, ctx, rl, a, w, base):
     rows, span, _ = q.shape
     length = kv.shape[1]
     keys = min(512, length)
     depth, width = w.shape
-    batch = 2
-    while rows * n // batch > rows * KVH:
-        batch *= 2
+    batch = n // 4
     own = lambda r, h: (r, 0, h)
 
     def place(r, h):
-        tile = jnp.minimum(r * KVH + h, rows * n // batch - 1) * batch
-        slot = n - 1 - lax.rem(tile, n)
-        return (lax.div(tile, n), lax.div(xor_of(lax.axis_index("mp"), slot, n), batch), 0, 0)
+        row, slot = tile_at(jnp.minimum(r * KVH + h, rows * n // batch - 1) * batch, n)
+        return (row, lax.div(xor_of(lax.axis_index("mp"), slot, n), batch), 0, 0)
 
     return pl.pallas_call(
         functools.partial(attend_back_kernel, keys, n),
@@ -984,6 +1020,7 @@
             pl.BlockSpec((1, span, GW), own),
             pl.BlockSpec((1, span, GW), own),
             pl.BlockSpec((1, batch, span, depth), place),
+            pl.BlockSpec(memory_space=pl.ANY),
             pl.BlockSpec(memory_space=pl.ANY),
         ],
         out_specs=[
@@ -1004,7 +1041,7 @@
         compiler_params=params(mib=60, axes=2, key=4),
         cost_estimate=TINY,
         name="attend_back",
-    )(q, kv, qa, ka, do, ctx, rl, a, w)
+    )(q, kv, qa, ka, do, ctx, rl, a, w, base)
 
 
 def xor_of(a, b, n):
@@ -1185,9 +1222,23 @@
     )(live, x, g.reshape(rows, pairs, 2 * span, width), gu, dt)
 
 
+def pick(index, table):
+    total = 0
+    for i, v in enumerate(table):
+        total = total + v * jnp.where(index == i, 1, 0)
+    return total
+
+
+def tile_at(now, n):
+    unit = n // 4
+    at = lax.div(now, unit)
+    row = pick(at, (0, 1, 0, 0, 1, 1, 0, 1))
+    return row, pick(at, (3, 3, 2, 1, 2, 1, 0, 0)) * unit + unit - 1 - lax.rem(now, unit)
+
+
 class TileSum:
-    def __init__(self, n, me, o_ref, w_any, scratch):
-        self.n, self.me, self.o_ref, self.w_any = n, me, o_ref, w_any
+    def __init__(self, n, me, o_ref, w_any, scratch, base=None):
+        self.n, self.me, self.o_ref, self.w_any, self.base = n, me, o_ref, w_any, base
         self.w_ref, self.terms, self.core, self.link = scratch[:4]
         self.sems, self.load = scratch[4:8], scratch[8]
         self.rows, self.span, _ = o_ref.shape
@@ -1204,10 +1255,14 @@
         )
 
     def start(self, meet=greet):
-        fetch = pltpu.make_async_copy(self.w_any, self.w_ref, self.load.at[0])
-        fetch.start()
+        fetch = [pltpu.make_async_copy(self.w_any, self.w_ref, self.load.at[0])]
+        if self.base is not None:
+            fetch.append(pltpu.make_async_copy(self.base, self.o_ref, self.load.at[1]))
+        for c in fetch:
+            c.start()
         meet(self.n, self.me)
-        fetch.wait()
+        for c in fetch:
+            c.wait()
 
     def close(self, row):
         last = self.scatter(row)
@@ -1221,13 +1276,11 @@
 
     def step(self, now, a_ref):
         n, terms = self.n, self.terms
-        r = lax.div(now, n)
-        k = n - 1 - lax.rem(now, n)
-        for row in range(1, self.rows):
-
-            @pl.when(now == row * n + n // 2)
-            def _(row=row):
-                self.close(row - 1)
+        r, k = tile_at(now, n)
+
+        @pl.when(now == 2 * n - n // 4)
+        def _():
+            self.close(0)
 
         for i in range(1, n, 2):
 
@@ -1251,7 +1304,8 @@
         @pl.when(k == 0)
         def _():
             sums.core_copy(1, self.core.at[r, 0]).wait_recv()
-            add_up(self.o_ref.at[r], [mine, self.core.at[r, 0]])
+            here = self.o_ref.at[r]
+            add_up(here, [mine, self.core.at[r, 0]] + ([] if self.base is None else [here]))
 
     def end(self):
         self.close(self.rows - 1)
@@ -1273,7 +1327,7 @@
         pltpu.SemaphoreType.DMA((rows, n // 2)),
         pltpu.SemaphoreType.DMA((rows, 2, n // 2 - 1)),
         pltpu.SemaphoreType.DMA((rows, 2, n // 2 - 1)),
-        pltpu.SemaphoreType.DMA((1,)),
+        pltpu.SemaphoreType.DMA((2,)),
     ]
 
 
@@ -1352,7 +1406,8 @@
     flat = (slots * TILE // CHUNKS, width)
 
     def place(r, j):
-        return (r, xor_of(lax.axis_index("mp"), n - 1 - j, n), 0, 0)
+        row, slot = tile_at(r * n + j, n)
+        return (row, xor_of(lax.axis_index("mp"), slot, n), 0, 0)
 
     def token(r, j):
         return lax.rem(r * n + j, per)
@@ -1458,14 +1513,26 @@
 
     x_own = hidden_in.reshape(tokens, width)
     x_value = x_own.astype(F32)
-    normed_ab, raw, q, attend_all, kv_all, output_all = project(
-        n, rows, x_own, attention_gain[None], attend_w, output_weight, cos, sin, gq, gk, ones
+    normed_ab, raw, q, grad_branch, attend_all, kv_all, output_all = project(
+        n,
+        rows,
+        x_own,
+        attention_gain[None],
+        attend_w,
+        output_weight,
+        cos,
+        sin,
+        gq,
+        gk,
+        ones,
+        out_grad.reshape(tokens, width),
     )
     q = q.reshape(rows, span, QW)
     kv_all = kv_all.reshape(rows, length, -1)
     output_full = output_all.reshape(QW, width)
-    grad_branch, output_full = lax.optimization_barrier((out_grad.astype(BF), output_full))
-    grads_all = lax.all_gather(grad_branch, "mp", axis=1, tiled=True)
+    grads_all = lax.all_gather(
+        grad_branch.reshape(rows, span, width), "mp", axis=1, tiled=True
+    )
     ctx, rl = attend(info, q, kv_all, start_col)
     context_b = ctx.reshape(tokens, QW)
     middle = x_value + mm(context_b, output_full)
@@ -1474,6 +1541,9 @@
 
     slot_index = me * slots + jnp.arange(slots, dtype=jnp.int32)
     live = jnp.any(tile_slot[None, :] == slot_index[:, None], axis=1).astype(F32)
+    gate_up_slots, down_slots, middle = lax.optimization_barrier(
+        (gate_up_slots, down_slots, middle)
+    )
     gu_t = jnp.swapaxes(gate_up_slots, 1, 2).reshape(slots * 2 * TILE, width)
     d_flat = down_slots.reshape(slots * TILE, width)
     d_t = d_flat.T
@@ -1497,11 +1567,20 @@
     grad_context = dg(grad_attn_b, output_full, NT).astype(BF).reshape(rows, span, QW)
     grad_output = dg(context_b, grad_attn_b, TN).astype(BF)
 
-    dq, dkv, ffn_out = attend_back(
-        n, q, kv_all, qa, ka, grad_context, ctx, rl, hidden, d_flat
-    )
-    layer_out = middle + ffn_out.reshape(tokens, width)
-    grad_joined_b, sum_q, sum_k, output_share = unproject(
+    dq, dkv, layer_out = attend_back(
+        n,
+        q,
+        kv_all,
+        qa,
+        ka,
+        grad_context,
+        ctx,
+        rl,
+        hidden,
+        d_flat,
+        middle.reshape(rows, span, width),
+    )
+    grad_joined_b, sum_q, sum_k, down_total = unproject(
         n,
         dq.reshape(tokens, QW),
         dkv.reshape(rows, n, span, -1),
@@ -1511,7 +1590,7 @@
         gq,
         gk,
         ones,
-        grad_output.reshape(n, -1, width),
+        down_total.reshape(slots * TILE, width),
     )
     sums = jnp.concatenate(
         [
@@ -1531,29 +1610,20 @@
         x_own,
         grad_middle,
         attention_gain[None],
-        output_share,
+        grad_output.reshape(n, -1, width),
         sums,
-    )
-    kv_total = attend_total[:, QW:].reshape(-1, KVH, 2, HD)
-    attend_total = jnp.concatenate(
-        [
-            attend_total[:, :QW],
-            kv_total[:, :, 0].reshape(-1, kw),
-            kv_total[:, :, 1].reshape(-1, kw),
-        ],
-        1,
     )
     gains = gains.reshape(-1)
     gain_query = gains[2 * width : 2 * width + HD] + gains[2 * width + HD : 2 * width + 2 * HD]
     gain_key = gains[2 * width + LANES : 2 * width + LANES + HD]
     shape = (rows, span, width)
     return (
-        layer_out.reshape(shape),
+        layer_out,
         input_grad.reshape(shape),
         attend_total,
         output_total,
         gate_up_total.astype(F32),
-        down_total.astype(F32),
+        down_total.reshape(slots, TILE, width),
         gains[:width],
         gain_query,
         gain_key,

time: 800 us -> 742 us (0.927)
  Pallas kernels: 634 us -> 587 us
  other arithmetic: 43.1 us -> 32.3 us
    pallas_call x1, Pallas kernels: 132 us -> 112 us  [finish(): pl.pallas_call(functools.partial(finish_kernel, n, m), in_specs=[vmem, vm...]
    pallas_call x1, Pallas kernels: 96.4 us -> 82.1 us  [attend_back(): pl.pallas_call(functools.partial(attend_back_kernel, keys, n), grid=(rows...]
    convert_element_type x2 -> x0, other arithmetic: 9.46 us -> none  [the longest x1 5.59 us: shards(): down_total.astype(F32)]
    pallas_call x1, Pallas kernels: 114 us -> 105 us  [spread(): pl.pallas_call(functools.partial(spread_kernel, n, m), grid=(rows, n), in...]
  transfers between devices with their start and end apart: 2 -> 2, of which waited for: 1 -> 1; matrix products, arithmetic and copies ran while one was open for 8% -> 7% of each run, Pallas kernels for 41% -> 39%
where the time goes in v4:
time: 742 us; the launch traced here: 737 us
  Pallas kernels  587 us (79%)
  waiting for transfers between devices  48 us (6%)
  local copies, waits for them, and re-layouts  35.5 us (5%)
  other arithmetic  32.3 us (4%)
  matrix products  18.8 us (3%)
  between operations  14.8 us (2%)
    pallas_call x1, Pallas kernels, finish(): pl.pallas_call(functools.partial(finish_kernel, n, m), in_specs=[vmem, vm...  112 us
    pallas_call x1, Pallas kernels, spread(): pl.pallas_call(functools.partial(spread_kernel, n, m), grid=(rows, n), in...  105 us
    pallas_call x1, Pallas kernels, feed(): pl.pallas_call(functools.partial(feed_kernel, n), grid=(rows, pairs), in_...  105 us
    pallas_call x1, Pallas kernels, project(): pl.pallas_call(functools.partial(project_kernel, n), in_specs=[vmem, vmem...  91.3 us
    pallas_call x1, Pallas kernels, attend_back(): pl.pallas_call(functools.partial(attend_back_kernel, keys, n), grid=(rows...  82.1 us
    pallas_call x1, Pallas kernels, unproject(): pl.pallas_call(functools.partial(unproject_kernel, n), in_specs=[vmem] *...  74.6 us
    all_gather x1, waiting for transfers between devices, shards(): lax.all_gather(grad_branch.reshape(rows, span, width), 'mp', axis=1, tile...  47.9 us
    pallas_call x1, Pallas kernels, attend(): pl.pallas_call(functools.partial(attend_kernel, keys), grid_spec=spec, ou...  16.2 us
  transfers between devices with their start and end apart: 2, of which 1 were waited for; matrix products, arithmetic and copies ran while one was open for 7% of the time, Pallas kernels for 39%

profile of v4, /device:TPU:0, one launch (start us, length us, event | category | flops | bytes accessed | tf_op | source)
XLA Modules:
  0.0 736.8 jit_solution(8432862771789897642)
XLA Ops:
  7.3 1.2 fusion.5
  8.5 0.9 slice_compare_fusion
  15.0 1.0 pad_maximum_fusion.w_ref
  16.0 91.3 %project.1 = (bf16[512,2048]{1,0:T(8,128)(2,1)}, f32[512,1920]{1,0:T(8,128)}, bf16[512,1280]{1,0:T(8,128)(2,1)}, bf16[512,2048]{1,0:T(8,128)(2,1)}, bf16[8,256,1...) custom-call(bf16[512,2048]{1,0:T(8,128)(2,1)} %bitcast.80, ...), custom_call_target="tpu_custom_call" | custom-call | tf_op jit(solution)/shard_map/project/pallas_call | solution.py:500
  109.4 16.2 %attend.1 = (bf16[2,256,1280]{2,1,0:T(8,128)(2,1)}, f32[2,256,1280]{2,1,0:T(8,128)}) custom-call(s32[2,3]{1,0:T(2,128)} %pad_add_fusion.info, bf16[2,256,1280]{2,1,0:T(8,128)(2,1)} %bitcast.100, bf16[2,2048,640]{2,1,0:T(8,128)(2,1)} %bitcast.88, s32[2,256,128]{2,1,0:T(8,128)} %broadcast_in_dim.65.start_ref), custom_call_target="tpu_custom_call" | custom-call | flops 21474836480 | bytes 10485760 | tf_op jit(solution)/shard_map/attend/pallas_call | solution.py:889
  125.7 8.0 %multiply_reduce_fusion.1 = (f32[512]{0:T(512)S(1)}, f32[512,2048]{1,0:T(8,128)}) fusion(bf16[512,1280]{1,0:T(8,128)(2,1)} %bitcast.98, bf16[1280,2048]{1,0:T(8,128)(2,1)} %bitcast.118, bf16[512,2048]{1,0:T(8,128)(2,1)S(1)} %bitcast.82), kind=kOutput, calls=%fused_computation.8 | convolution fusion | flops 2688548352 | bytes 12847104 | tf_op jit(solution)/shard_map/dot_general | solution.py:46
  133.7 2.8 copy.38.dt_any
  137.2 8.6 %copy.39 = bf16[6,256,2048]{2,1,0:T(8,128)(2,1)} copy(bf16[6,256,2048]{1,2,0:T(8,128)(2,1)} %bitcast.83) | data formatting | bytes 12582912 | tf_op jit(solution)/shard_map/transpose | solution.py:1547
  145.8 4.0 multiply_convert_fusion
  149.8 47.9 %all-gather.2.cloned.1.call-done = bf16[2,2048,2048]{2,1,0:T(8,128)(2,1)} async-done(((bf16[2,256,2048]{2,1,0:T(8,128)(2,1)}), bf16[2,2048,2048]{2,1,0:T(8,128)(2,1)}) %all-gather.2.cloned.1.call-update) | async-done | bytes 16777232 | tf_op jit(solution)/shard_map/all_gather | solution.py:1533
  197.7 105.3 %feed.1 = (bf16[2,4,512,2048]{3,2,1,0:T(8,128)(2,1)}, bf16[2,4,512,768]{3,2,1,0:T(8,128)(2,1)}, bf16[2,4,512,1536]{3,2,1,0:T(8,128)(2,1)}, bf16[6,128,2048]{2,1,0:T(8,128)(2,1)}) custom-call(f32[6]{0:T(128)} %convert_element_type.52.live_ref, bf16[2,256,2048]{2,1,0:T(8,128)(2,1)} %bitcast.96, bf16[2,4,512,2048]{3,2,1,0:T(8,128)(2,1)} %bitcast.117, ...), custom_call_target="tpu_custom_call" | custom-call | flops 77309411328 | bytes 59768832 | tf_op jit(solution)/shard_map/feed/pallas_call | solution.py:1181
  303.1 105.5 %spread.1 = (f32[2,256,2048]{2,1,0:T(8,128)}, bf16[6,2048,256]{2,1,0:T(8,128)(2,1)}, bf16[12,64,2048]{2,1,0:T(8,128)(2,1)}) custom-call(bf16[2,8,256,1536]{3,2,1,0:T(8,128)(2,1)} %bitcast.73, bf16[1536,2048]{1,0:T(8,128)(2,1)} %bitcast.75, bf16[4096,2048]{1,0:T(8,128)(2,1)} %bitcast.76, bf16[4096,1536]{1,0:T(8,128)(2,1)} %bitcast.74, ...), custom_call_target="tpu_custom_call" | custom-call | flops 1 | bytes 1 | tf_op jit(solution)/shard_map/spread/pallas_call | solution.py:1419
  410.6 2.0 select_convert_fusion.ka_ref
  412.7 5.8 fusion.1
  418.5 1.2 copy-done.1
  419.7 3.6 multiply_add_fusion.mid_any
  423.4 4.0 convolution_convert_fusion.1
  427.4 82.1 %attend_back.1 = (f32[2,256,1280]{2,1,0:T(8,128)}, bf16[2,2048,640]{2,1,0:T(8,128)(2,1)}, f32[2,256,2048]{2,1,0:T(8,128)}) custom-call(bf16[2,256,1280]{2,1,0:T(8,128)(2,1)} %bitcast.101, bf16[2,2048,640]{2,1,0:T(8,128)(2,1)} %bitcast.89, bf16[2,256,128]{2,1,0:T(8,128)(2,1)} %select_convert_fusion.1.qa_ref, bf16[2,2048,128]{2,1,0:T(8,128)(2,1)} %select_convert_fusion.ka_ref, ...), custom_call_target="tpu_custom_call" | custom-call | flops 1 | bytes 1 | tf_op jit(solution)/shard_map/attend_back/pallas_call | solution.py:1011
  509.5 74.6 %unproject.1 = (bf16[512,1920]{1,0:T(8,128)(2,1)}, f32[8,128]{1,0:T(8,128)}, f32[8,128]{1,0:T(8,128)}, f32[768,2048]{1,0:T(8,128)}) custom-call(f32[512,1280]{1,0:T(8,128)} %bitcast.95, bf16[2,8,256,640]{3,2,1,0:T(8,128)(2,1)} %bitcast.90, f32[512,1920]{1,0:T(8,128)} %get-tuple-element.58.raw_ref, f32[512,128]{1,0:T(8,128)} %copy.36.cos_ref, ...), custom_call_target="tpu_custom_call" | custom-call | flops 1 | bytes 1 | tf_op jit(solution)/shard_map/unproject/pallas_call | solution.py:603
  585.5 1.8 concatenate.19.sums_ref
  587.3 6.8 convolution_convert_fusion
  594.1 111.7 %finish.1 = (f32[512,2048]{1,0:T(8,128)}, f32[256,1920]{1,0:T(8,128)}, f32[160,2048]{1,0:T(8,128)}, f32[40,128]{1,0:T(8,128)}) custom-call(bf16[512,2048]{1,0:T(8,128)(2,1)} %get-tuple-element.55.normed_ref, bf16[512,1920]{1,0:T(8,128)(2,1)} %get-tuple-element.60.gj_ref, bf16[8,256,1920]{2,1,0:T(8,128)(2,1)} %get-tuple-element.61.w_any, ...), custom_call_target="tpu_custom_call" | custom-call | flops 1 | bytes 1 | tf_op jit(solution)/shard_map/finish/pallas_call | solution.py:788
  705.9 1.4 fusion.6
  707.2 1.3 slice_bitcast_fusion
  708.6 8.9 %convert_element_type.57 = f32[6,2048,256]{2,1,0:T(8,128)} convert(bf16[6,2048,256]{2,1,0:T(8,128)(2,1)} %all-reduce.4.cloned.1.call-done) | non-fusion elementwise | flops 3145728 | bytes 18874368 | tf_op jit(solution)/shard_map/convert_element_type | solution.py:1625
  717.4 2.1 copy.57
  719.6 1.6 copy-done.6
  721.1 2.1 copy.58
  723.3 1.2 copy-done.7
  724.4 1.3 copy.59
  725.7 1.1 copy.60
  726.8 2.7 copy.61
  (85 shorter events, 11.8 us)
Async XLA Ops:
  7.2 7.8 %slice-start.2 = ((bf16[256,1920]{1,0:T(8,128)(2,1)}), bf16[256,1280]{1,0:T(8,128)(2,1)S(1)}, s32[]{:S(2)}) async-start(bf16[256,1920]{1,0:T(8,128)(2,1)} %param.18), calls=%async_computation.4 | async-start | bytes 1310720 | tf_op jit(solution)/shard_map/slice | solution.py:1488
  7.2 6.7 copy-start.12
  7.2 7.2 copy-start.13
  7.2 190.5 %all-gather.2.cloned.1.call-start = ((), (), s32[]{:S(2)}) async-start(), calls=%async_computation | async-start | bytes 18874368 | tf_op jit(solution)/shard_map/all_gather | solution.py:1533
  107.4 601.2 %all-reduce.4.cloned.1.call-start = ((), (), s32[]{:S(2)}) async-start(), calls=%async_computation.1 | async-start | bytes 12582912 | tf_op jit(solution)/shard_map/psum | solution.py:1557
  109.4 16.2 %copy-start.4 = (bf16[2,256,2048]{2,1,0:T(8,128)(2,1)S(1)}, bf16[2,256,2048]{2,1,0:T(8,128)(2,1)}, u32[]{:S(2)}) copy-start(bf16[2,256,2048]{2,1,0:T(8,128)(2,1)} %param.12) | copy-start | bytes 6291460
  125.7 8.0 %copy-start.3 = (bf16[6,128,2048]{2,1,0:T(8,128)(2,1)S(1)}, bf16[6,128,2048]{2,1,0:T(8,128)(2,1)}, u32[]{:S(2)}) copy-start(bf16[6,128,2048]{2,1,0:T(8,128)(2,1)} %param.22) | copy-start | bytes 9437188
  133.6 2.8 copy-start.14
  137.1 8.6 %copy-start.11 = (f32[2048]{0:T(1024)S(1)}, f32[2048]{0:T(1024)}, u32[]{:S(2)}) copy-start(f32[2048]{0:T(1024)} %param.20) | copy-start | bytes 24580
  408.6 0.7 copy-start.10
  412.7 5.8 copy-start
  412.7 7.1 copy-start.1
  412.7 10.7 %slice-start.3 = ((s8[5242880]{0:T(1024)(128)(4,1)}), s8[4194304]{0:T(1024)(128)(4,1)S(1)}, s32[]{:S(2)}) async-start(s8[5242880]{0:T(1024)(128)(4,1)} %bitcast.119), calls=%async_computation.5 | async-start | bytes 8388608
  419.7 3.6 slice-start.4
  423.4 4.0 copy-start.2
  509.5 77.8 %copy-start.8 = (bf16[2,256,1280]{2,1,0:T(8,128)(2,1)S(1)}, bf16[2,256,1280]{2,1,0:T(8,128)(2,1)}, u32[]{:S(2)}) copy-start(bf16[2,256,1280]{2,1,0:T(8,128)(2,1)} %get-tuple-element.42.ctx_ref) | copy-start | bytes 3932164
  708.6 8.9 %copy-start.5 = (f32[2,256,2048]{2,1,0:T(8,128)S(1)}, f32[2,256,2048]{2,1,0:T(8,128)}, u32[]{:S(2)}) copy-start(f32[2,256,2048]{2,1,0:T(8,128)} %get-tuple-element.98) | copy-start | bytes 12582916
  717.4 3.7 copy-start.6
  717.4 9.4 %slice-start = ((s8[6291456]{0:T(1024)(128)(4,1)}), s8[4194304]{0:T(1024)(128)(4,1)S(1)}, s32[]{:S(2)}) async-start(s8[6291456]{0:T(1024)(128)(4,1)} %bitcast.84), calls=%async_computation.2 | async-start | bytes 8388608
  721.1 3.3 copy-start.7
  721.1 4.6 copy-start.9
  721.1 5.7 slice-start.1
Sparse Core Ops, SparseCore 0:
  107.5 90.2 all-gather.1
  408.7 222.8 all-reduce.3

commit v5 on v4

--- a/solution.py
+++ b/solution.py
@@ -357,18 +357,29 @@
 
 
 def project_kernel(
-    n, x_ref, gain_ref, w_ref, o_ref, cos_ref, sin_ref, gq_ref, gk_ref, ones_ref, grad_ref,
-    normed_ref, raw_ref, q_ref, branch_ref, w_out, kv_out, o_out,
-    w_all, kv_own, w_send, w_recv, kv_send, kv_recv, o_send, o_recv, local,
+    n, x_any, gain_ref, w_ref, o_ref, cos_ref, sin_ref, gq_ref, gk_ref, ones_ref, grad_any,
+    normed_any, raw_any, q_ref, branch_any, w_out, kv_out, o_out,
+    x_ref, grad_ref, normed_ref, raw_ref, branch_ref, moves, w_all, kv_own, w_send, w_recv, kv_send, kv_recv, o_send, o_recv, local,
 ):
     me = lax.axis_index("mp")
     depth = w_ref.shape[0]
-    tokens = x_ref.shape[0]
+    tokens, width = x_ref.shape
     rows = kv_out.shape[0]
     span = tokens // rows
     half = depth // 2
     own_w = pltpu.make_async_copy(w_ref, w_all.at[me], local.at[0])
     own_w.start()
+    early = [
+        pltpu.make_async_copy(x_any, x_ref, moves.at[0]),
+        pltpu.make_async_copy(grad_any, grad_ref, moves.at[1]),
+    ]
+    late = [
+        pltpu.make_async_copy(normed_ref, normed_any, moves.at[2]),
+        pltpu.make_async_copy(branch_ref, branch_any, moves.at[3]),
+        pltpu.make_async_copy(raw_ref, raw_any, moves.at[4]),
+    ]
+    for c in early:
+        c.start()
     own_o = pltpu.make_async_copy(o_ref, o_out.at[me], local.at[1 + rows])
     own_o.start()
     greet(n, me)
@@ -390,6 +401,8 @@
         w_recv,
     )
     weights.start()
+    for c in early:
+        c.wait()
     step = min(64, tokens)
 
     @pl.loop(0, tokens // step)
@@ -428,6 +441,8 @@
         accumulate(k, False)
     out_w = pltpu.make_async_copy(w_all, w_out, local.at[0])
     out_w.start()
+    for c in late:
+        c.start()
 
     chunk = min(128, tokens)
     lane = lax.broadcasted_iota(jnp.int32, (chunk, LANES), 1)
@@ -486,6 +501,8 @@
         c.wait()
     out_w.wait()
     own_o.wait()
+    for c in late:
+        c.wait()
     weights.drain()
     outs.drain()
     kvs.drain()
@@ -499,8 +516,8 @@
     kvw = columns - QW
     return pl.pallas_call(
         functools.partial(project_kernel, n),
-        in_specs=[vmem, vmem, hbm, hbm, vmem, vmem, vmem, vmem, vmem, vmem],
-        out_specs=[vmem, vmem, vmem, vmem, hbm, hbm, hbm],
+        in_specs=[hbm, vmem, hbm, hbm, vmem, vmem, vmem, vmem, vmem, hbm],
+        out_specs=[hbm, hbm, vmem, hbm, hbm, hbm, hbm],
         out_shape=[
             jax.ShapeDtypeStruct((tokens, width), BF),
             jax.ShapeDtypeStruct((tokens, columns), F32),
@@ -511,6 +528,12 @@
             jax.ShapeDtypeStruct((n,) + o.shape, BF),
         ],
         scratch_shapes=[
+            pltpu.VMEM((tokens, width), BF),
+            pltpu.VMEM((tokens, width), F32),
+            pltpu.VMEM((tokens, width), BF),
+            pltpu.VMEM((tokens, columns), F32),
+            pltpu.VMEM((tokens, width), BF),
+            pltpu.SemaphoreType.DMA((5,)),
             pltpu.VMEM((n, depth, columns), BF),
             pltpu.VMEM((tokens, kvw), BF),
             pltpu.SemaphoreType.DMA((n, 2)),
@@ -527,24 +550,39 @@
 
 
 def unproject_kernel(
-    n, dq_ref, dkv_ref, raw_ref, cos_ref, sin_ref, gq_ref, gk_ref, ones_ref, down_ref,
-    gj_ref, sq_ref, sk_ref, wide_ref,
-    dkv_own, *scratch,
+    n, dq_any, dkv_any, raw_any, cos_ref, sin_ref, gq_ref, gk_ref, ones_ref, down_any,
+    gj_ref, sq_ref, sk_ref, wide_any,
+    dkv_own, dkv_ref, dq_ref, raw_ref, down_ref, wide_ref, load, *scratch,
 ):
     me = lax.axis_index("mp")
+    early = [
+        pltpu.make_async_copy(dkv_any.at[:, flip(me, k)], dkv_ref.at[k // 2], load.at[4 + k // 2])
+        for k in range(n - 2, -1, -2)
+    ]
+    late = [
+        pltpu.make_async_copy(dq_any, dq_ref, load.at[0]),
+        pltpu.make_async_copy(raw_any, raw_ref, load.at[1]),
+        pltpu.make_async_copy(down_any, down_ref, load.at[2]),
+    ]
+    for c in early + late:
+        c.start()
     greet(n, me)
     tokens = dq_ref.shape[0]
-    rows = dkv_ref.shape[0]
+    rows = dkv_any.shape[0]
     span = tokens // rows
     columns = raw_ref.shape[1]
     keys = make_scatter(n, me, lambda ref, h: ref.at[h], scratch[:6])
 
     def dkv_term(k):
-        return dkv_ref.at[:, flip(me, k)]
+        return dkv_any.at[:, flip(me, k)] if k % 2 else dkv_ref.at[k // 2]
 
     for k in range(n - 1, 0, -2):
         keys.odd(k, dkv_term(k))
+    for c in early:
+        c.wait()
     keys.even(n - 2, dkv_term(n - 2))
+    for c in late:
+        c.wait()
 
     chunk = min(128, tokens)
     lane = lax.broadcasted_iota(jnp.int32, (chunk, LANES), 1)
@@ -585,6 +623,8 @@
                 keys.even(k, dkv_term(k))
 
     wide_ref[...] = down_ref[...].astype(F32)
+    keep = pltpu.make_async_copy(wide_ref, wide_any, load.at[3])
+    keep.start()
     keys.own(dkv_term(0), dkv_own)
 
     @pl.loop(0, tokens // chunk)
@@ -592,6 +632,7 @@
         back(i, range(QW // LANES, count), False)
 
     keys.drain(dkv_term(0))
+    keep.wait()
 
 
 def unproject(n, dq, dkv, raw, cos, sin, gq, gk, ones, down):
@@ -600,17 +641,26 @@
     span = tokens // rows
     kvw = columns - QW
     vmem = pl.BlockSpec(memory_space=pltpu.VMEM)
+    hbm = pl.BlockSpec(memory_space=pl.ANY)
     return pl.pallas_call(
         functools.partial(unproject_kernel, n),
-        in_specs=[vmem] * 9,
-        out_specs=[vmem] * 4,
+        in_specs=[hbm] * 3 + [vmem] * 5 + [hbm],
+        out_specs=[vmem] * 3 + [hbm],
         out_shape=[
             jax.ShapeDtypeStruct((tokens, columns), BF),
             jax.ShapeDtypeStruct((8, LANES), F32),
             jax.ShapeDtypeStruct((8, LANES), F32),
             jax.ShapeDtypeStruct(down.shape, F32),
         ],
-        scratch_shapes=[pltpu.VMEM((rows, span, kvw), F32)]
+        scratch_shapes=[
+            pltpu.VMEM((rows, span, kvw), F32),
+            pltpu.VMEM((n // 2, rows, span, kvw), BF),
+            pltpu.VMEM(dq.shape, F32),
+            pltpu.VMEM(raw.shape, F32),
+            pltpu.VMEM(down.shape, BF),
+            pltpu.VMEM(down.shape, F32),
+            pltpu.SemaphoreType.DMA((4 + n // 2,)),
+        ]
         + scatter_scratch(n, (rows, span, kvw), (span, kvw)),
         compiler_params=params(mib=60, axes=0, key=2),
         cost_estimate=TINY,
@@ -622,9 +672,10 @@
 
 
 def finish_kernel(
-    n, m, normed_ref, gj_ref, w_any, x_ref, mid_any, gain_ref, gout_any, sums_ref,
-    grad_ref, attend_ref, out_ref, gains_ref,
-    w_ref, term, error, mid_ref, gout_ref, own_w, up_w, across_w, own_o, up_o, across_o, landed,
+    n, m, normed_any, gj_any, w_any, x_any, mid_any, gain_ref, share_any, sums_ref,
+    grad_any, attend_ref, out_ref, gains_ref,
+    normed_ref, gj_ref, x_ref, grad_ref,
+    w_ref, term, error, mid_ref, own_w, up_w, across_w, own_o, up_o, across_o, landed,
     sem_w, sem_o, sem_g, load, *scratch,
 ):
     me, line = lax.axis_index("mp"), lax.axis_index("dp")
@@ -633,12 +684,17 @@
     pieces, piece = own_w.shape[0], own_w.shape[1]
     o_pieces, o_piece = own_o.shape[0], own_o.shape[1]
     chunk = error.shape[0]
-    fetch = [pltpu.make_async_copy(w_any, w_ref, load.at[0])]
-    fetch += [
-        pltpu.make_async_copy(gout_any.at[flip(me, k)], gout_ref.at[k // 2], load.at[2 + k // 2])
-        for k in range(0, n, 2)
+    early = [
+        pltpu.make_async_copy(normed_any, normed_ref, load.at[2]),
+        pltpu.make_async_copy(gj_any, gj_ref, load.at[3]),
+        pltpu.make_async_copy(share_any, own_o, load.at[4]),
     ]
-    for c in fetch:
+    fetch = [
+        pltpu.make_async_copy(w_any, w_ref, load.at[0]),
+        pltpu.make_async_copy(x_any, x_ref, load.at[5]),
+    ]
+    keep = pltpu.make_async_copy(grad_ref, grad_any, load.at[6])
+    for c in early + fetch:
         c.start()
 
     def bring(i):
@@ -647,9 +703,8 @@
 
     bring(0).start()
     greet_all(n, me, m, line)
-    half, half_w = depth // 2, width // 2
-    sums = make_scatter(n, me, lambda ref, h: ref.at[pl.ds(h * half, half)], scratch[:6])
-    outs = make_scatter(n, me, lambda ref, h: ref.at[:, pl.ds(h * half_w, half_w)], scratch[6:])
+    half = depth // 2
+    sums = make_scatter(n, me, lambda ref, h: ref.at[pl.ds(h * half, half)], scratch)
     at = lambda ref: lambda c: ref.at[c]
     weights = Line(m, line, at(own_w), at(up_w), at(across_w), at(up_w), sem_w)
     out_line = Line(m, line, at(own_o), at(up_o), at(across_o), at(up_o), sem_o)
@@ -701,6 +756,10 @@
             device_id_type=MESH,
         )
 
+    for c in early:
+        c.wait()
+    for c in range(o_pieces):
+        out_line.launch(c)
     for k in range(n - 1, 0, -2):
         weight_part(k)
         sums.odd(k, mine(k))
@@ -716,37 +775,18 @@
     weight_part(0)
     for i in range(1, tokens // chunk):
         tokens_part(i)
+    keep.start()
     for i in range(len(steps)):
         landed[2 * i] = gains_ref[...]
         exchange(i).start()
         exchange(i).wait_recv()
         gains_ref[...] = landed[2 * i] + landed[2 * i + 1]
+    for c in range(o_pieces):
+        out_line.inward(c)
     sums.own(mine(0), attend_ref)
     for c in range(pieces):
         own_w[c] = attend_ref[c * piece : (c + 1) * piece, :].astype(BF)
         weights.launch(c)
-
-    def out_term(k):
-        return gout_any.at[flip(me, k)] if k % 2 else gout_ref.at[k // 2]
-
-    for k in range(n - 1, 0, -2):
-        outs.odd(k, out_term(k))
-    todo = list(range(n - 2, 0, -2))
-    ahead = 2
-    for c in range(pieces + ahead):
-        if c < pieces:
-            weights.inward(c)
-        if c >= ahead:
-            weights.outward(c - ahead)
-        if todo:
-            k = todo.pop(0)
-            outs.even(k, out_term(k))
-    for k in todo:
-        outs.even(k, out_term(k))
-    outs.own(out_term(0), out_ref)
-    for c in range(o_pieces):
-        own_o[c] = out_ref[c * o_piece : (c + 1) * o_piece, :].astype(BF)
-        out_line.launch(c)
     kw = KVH * HD
 
     def widen(c):
@@ -757,66 +797,70 @@
             attend_ref[rows, QW + h * HD : QW + (h + 1) * HD] = both[:, :HD]
             attend_ref[rows, QW + kw + h * HD : QW + kw + (h + 1) * HD] = both[:, HD:]
 
-    for c in range(max(o_pieces + ahead, pieces)):
+    ahead = 2
+    for c in range(pieces + ahead):
+        if c < pieces:
+            weights.inward(c)
         if c < o_pieces:
-            out_line.inward(c)
-        if c < pieces:
-            widen(c)
-        if ahead <= c < o_pieces + ahead:
-            out_line.outward(c - ahead)
+            out_line.outward(c)
+            out_ref[c * o_piece : (c + 1) * o_piece, :] = up_o[c].astype(F32)
+        if c >= ahead:
+            weights.outward(c - ahead)
+            widen(c - ahead)
+    keep.wait()
     for c in range(o_pieces):
-        out_ref[c * o_piece : (c + 1) * o_piece, :] = up_o[c].astype(F32)
         out_line.drain(c)
     for c in range(pieces):
         weights.drain(c)
     for i in range(len(steps)):
         exchange(i).wait_send()
     sums.drain(mine(0))
-    outs.drain(out_term(0))
-
-
-def finish(n, m, normed, gj, w, x, middle, gain, gout, sums):
+
+
+def finish(n, m, normed, gj, w, x, middle, gain, share, sums):
     tokens, width = x.shape
     columns = gj.shape[1]
     depth = width // n
-    share = gout.shape[1]
     pieces, o_pieces = 8, 5
+    split = (o_pieces, share.shape[0] // o_pieces, width)
     chunk = min(256, tokens)
     vmem = pl.BlockSpec(memory_space=pltpu.VMEM)
     hbm = pl.BlockSpec(memory_space=pl.ANY)
     steps = n.bit_length() + m.bit_length() - 2
     return pl.pallas_call(
         functools.partial(finish_kernel, n, m),
-        in_specs=[vmem, vmem, hbm, vmem, hbm, vmem, hbm, vmem],
-        out_specs=[vmem] * 4,
+        in_specs=[hbm, hbm, hbm, hbm, hbm, vmem, hbm, vmem],
+        out_specs=[hbm, vmem, vmem, vmem],
         out_shape=[
             jax.ShapeDtypeStruct((tokens, width), F32),
             jax.ShapeDtypeStruct((depth, columns), F32),
-            jax.ShapeDtypeStruct((share, width), F32),
+            jax.ShapeDtypeStruct(share.shape, F32),
             jax.ShapeDtypeStruct((GAIN_ROWS, LANES), F32),
         ],
         scratch_shapes=[
+            pltpu.VMEM((tokens, width), BF),
+            pltpu.VMEM((tokens, columns), BF),
+            pltpu.VMEM((tokens, width), BF),
+            pltpu.VMEM((tokens, width), F32),
             pltpu.VMEM(w.shape, BF),
             pltpu.VMEM((n // 2 + 1, depth, columns), BF),
             pltpu.VMEM((chunk, width), F32),
             pltpu.VMEM((chunk, width), F32),
-            pltpu.VMEM((n // 2, share, width), BF),
         ]
         + [pltpu.VMEM((pieces, depth // pieces, columns), BF)] * 3
-        + [pltpu.VMEM((o_pieces, share // o_pieces, width), BF)] * 3
+        + [pltpu.VMEM(split, BF)] * 3
         + [
             pltpu.VMEM((2 * steps, GAIN_ROWS, LANES), F32),
             pltpu.SemaphoreType.DMA((6, pieces)),
             pltpu.SemaphoreType.DMA((6, o_pieces)),
             pltpu.SemaphoreType.DMA((2, steps)),
-            pltpu.SemaphoreType.DMA((2 + n // 2,)),
+            pltpu.SemaphoreType.DMA((7,)),
         ]
-        + scatter_scratch(n, (depth, columns), (depth // 2, columns))
-        + scatter_scratch(n, (share, width), (share, width // 2)),
+        + scatter_scratch(n, (depth, columns), (depth // 2, columns)),
         compiler_params=params(mib=60, axes=0, key=5),
         cost_estimate=TINY,
         name="finish",
-    )(normed, gj, w, x, middle, gain, gout, sums)
+    )(normed, gj, w, x, middle, gain, share.reshape(split), sums)
 
 
 def key_positions(shape, axis, group, per, span):
@@ -902,7 +946,7 @@
 
 def attend_back_kernel(
     keys, n, q_ref, kv_ref, qa_ref, ka_ref, do_ref, ctx_ref, rl_ref, a_ref, w_any, base_any,
-    dq_ref, dkv_ref, o_ref, acc, sides, *scratch,
+    gout_any, dq_ref, dkv_ref, o_ref, share_ref, acc, sides, gout_ref, moves, *scratch,
 ):
     span = q_ref.shape[1]
     per = keys // span
@@ -911,6 +955,31 @@
     rows = o_ref.shape[0]
     now = pl.program_id(0) * KVH + pl.program_id(1)
     sums = TileSum(n, me, o_ref, w_any, scratch, base_any)
+    half_w = share_ref.shape[1] // 2
+    outs = make_scatter(
+        n, me, lambda ref, h: ref.at[:, pl.ds(h * half_w, half_w)], scratch[-6:]
+    )
+
+    def out_term(k):
+        return gout_any.at[flip(me, k)] if k % 2 else gout_ref.at[k // 2]
+
+    def bring(k):
+        return pltpu.make_async_copy(gout_any.at[flip(me, k)], out_term(k), moves.at[k // 2])
+
+    def out_event(i):
+        if i == 0:
+            for k in range(0, n, 2):
+                bring(k).start()
+            for k in range(n - 1, 0, -2):
+                outs.odd(k, out_term(k))
+        elif i < n // 2:
+            k = n - 2 * i
+            bring(k).wait()
+            outs.even(k, out_term(k))
+        else:
+            bring(0).wait()
+            outs.own(out_term(0), share_ref)
+
     batch = a_ref.shape[1]
     steps = rows * n // batch
 
@@ -925,6 +994,14 @@
             tile = now * batch + i
             _, slot = tile_at(tile, n)
             sums.step(tile, a_ref.at[0, lax.rem(xor_of(me, slot, n), batch)])
+
+    count = n // 2 + 1
+    for i in range(count):
+        when = 1 + i if i < 2 else 5 + (i - 2) * 4 // (count - 2)
+
+        @pl.when(now == (when if i < count - 1 else rows * KVH - 1))
+        def _(i=i):
+            out_event(i)
 
     lane = lax.broadcasted_iota(jnp.int32, (span, LANES), 1)
     low_q = lane < HD
@@ -962,6 +1039,7 @@
         if masked:
             position = g * keys + lax.broadcasted_iota(jnp.int32, (keys, span), 0)
             seen = position <= me * span + lax.broadcasted_iota(jnp.int32, (keys, span), 1)
+        turned = [s.T for s in key_sides]
         grad_key = grad_value = 0.0
         for h in range(GW // HD):
             e = jnp.exp2(dg(key_sides[h % 2], sides[3, h], NT))
@@ -970,7 +1048,7 @@
             ds = (e * dg(value_sides[h % 2], sides[2, h], NT)).astype(BF)
             grad_value = grad_value + mm(e.astype(BF), sides[1, h])
             grad_key = grad_key + mm(ds, sides[0, h])
-            acc[h] += dg(ds, key_sides[h % 2], TN)
+            acc[h] += mm(turned[h % 2], ds)
         grad_key = (grad_key + pltpu.roll(grad_key, HD, 1)) * LN2
         grad_value = grad_value + pltpu.roll(grad_value, HD, 1)
         dkv_ref[0, here, :] = jnp.where(low_k, grad_key, grad_value).astype(BF)
@@ -989,14 +1067,15 @@
 
     for pair in range(GW // LANES):
         lanes = slice(pair * LANES, (pair + 1) * LANES)
-        dq_ref[0, :, lanes] = jnp.where(low_q, acc[2 * pair], acc[2 * pair + 1]) * (HD**-0.5)
+        dq_ref[0, :, lanes] = jnp.where(low_q, acc[2 * pair].T, acc[2 * pair + 1].T) * (HD**-0.5)
 
     @pl.when(now == rows * KVH - 1)
     def _():
         sums.end()
-
-
-def attend_back(n, q, kv, qa, ka, do, ctx, rl, a, w, base):
+        outs.drain(out_term(0))
+
+
+def attend_back(n, q, kv, qa, ka, do, ctx, rl, a, w, base, gout):
     rows, span, _ = q.shape
     length = kv.shape[1]
     keys = min(512, length)
@@ -1022,26 +1101,32 @@
             pl.BlockSpec((1, batch, span, depth), place),
             pl.BlockSpec(memory_space=pl.ANY),
             pl.BlockSpec(memory_space=pl.ANY),
+            pl.BlockSpec(memory_space=pl.ANY),
         ],
         out_specs=[
             pl.BlockSpec((1, span, GW), own),
             pl.BlockSpec((1, length, LANES), own),
+            pl.BlockSpec(memory_space=pltpu.VMEM),
             pl.BlockSpec(memory_space=pltpu.VMEM),
         ],
         out_shape=[
             jax.ShapeDtypeStruct(q.shape, F32),
             jax.ShapeDtypeStruct(kv.shape, BF),
             jax.ShapeDtypeStruct((rows, span, width), F32),
+            jax.ShapeDtypeStruct(gout.shape[1:], BF),
         ],
         scratch_shapes=[
-            pltpu.VMEM((GW // HD, span, LANES), F32),
+            pltpu.VMEM((GW // HD, LANES, span), F32),
             pltpu.VMEM((4, GW // HD, span, LANES), BF),
+            pltpu.VMEM((n // 2,) + gout.shape[1:], BF),
+            pltpu.SemaphoreType.DMA((n // 2,)),
         ]
-        + tile_scratch(n, rows, span, w),
+        + tile_scratch(n, rows, span, w)
+        + scatter_scratch(n, gout.shape[1:], (gout.shape[1], width // 2)),
         compiler_params=params(mib=60, axes=2, key=4),
         cost_estimate=TINY,
         name="attend_back",
-    )(q, kv, qa, ka, do, ctx, rl, a, w, base)
+    )(q, kv, qa, ka, do, ctx, rl, a, w, base, gout)
 
 
 def xor_of(a, b, n):
@@ -1053,9 +1138,9 @@
 
 
 def feed_kernel(
-    n, live_ref, x_own, g_ref, gu_any, dt_any,
+    n, live_ref, x_own, g_ref, g_any, gu_any, dt_any,
     x_all, hid_ref, dgu_ref, gd_any,
-    x_vm, gu_ref, dt_ref, d_sum, out_d, x_send, x_recv, loads, stores, keep,
+    x_vm, gu_ref, dt_ref, d_sum, out_d, g_two, back, x_send, x_recv, loads, stores, keep,
 ):
     me = lax.axis_index("mp")
     rows, span, width = x_own.shape
@@ -1096,6 +1181,13 @@
             ends[i] = max(ends[i - 1], 1 + max(j for j, e in enumerate(todo) if e[0] == 2 * i))
         return todo[ends[upto - 1] if upto else 0 : ends[upto]]
 
+    def ahead(i):
+        block = lax.div(xor_of(me, 2 * lax.rem(i, pairs), n), 2)
+        to = lax.rem(i, 2)
+        return pltpu.make_async_copy(
+            g_any.at[lax.div(i, pairs), block], g_two.at[to], loads.at[2 + rows + to]
+        )
+
     @pl.when(now == 0)
     def _():
         for row in range(rows):
@@ -1104,11 +1196,28 @@
             c.start()
         greet(n, me)
         gather(0).start()
+        ahead(0).start()
         d_sum[...] = jnp.zeros_like(d_sum)
         own_copy(0).wait()
         for c in fetch:
             c.wait()
 
+        @pl.loop(0, rows * pairs)
+        def _(i):
+            @pl.when(i + 1 < rows * pairs)
+            def _():
+                ahead(i + 1).start()
+
+            ahead(i).wait()
+            back[i] = mm(g_two[lax.rem(i, 2)], dt_ref[...]).astype(BF)
+
+            @pl.when(i == rows * pairs - 2)
+            def _():
+                for e in gather(0).even[:2]:
+                    gather(0).forward(*e)
+                for row in range(1, rows):
+                    gather(row).start()
+
     for row in range(rows):
         for i in range(pairs):
 
@@ -1116,10 +1225,9 @@
             def _(row=row, i=i):
                 if i == 0 and row:
                     own_copy(row).wait()
-                for j, e in enumerate(events(row, i)):
-                    gather(row).forward(*e)
-                    if row + 1 < rows and i == 1 and j == 1:
-                        gather(row + 1).start()
+                for e in events(row, i):
+                    if row or e not in gather(0).even[:2]:
+                        gather(row).forward(*e)
                 for h in (0, 1):
                     gather(row).arrive(2 * i + 1, h)
 
@@ -1129,14 +1237,13 @@
 
     save(r, p).start()
     x = x_vm.at[r, p]
-    grad = mm(g_ref[0, 0], dt_ref[...])
     for t in range(slots):
         both = mm(x[...], gu_ref[t])
         gate, upper = both[:, :TILE], both[:, TILE:]
         live = live_ref[t]
         sig = jax.nn.sigmoid(gate)
         silu = gate * sig
-        gh = grad[:, t * TILE : (t + 1) * TILE] * live
+        gh = back[now, :, t * TILE : (t + 1) * TILE].astype(F32) * live
         hid_ref[0, 0, :, t * TILE : (t + 1) * TILE] = (silu * upper * live).astype(BF)
         dgu_ref[0, 0, :, 2 * t * TILE : (2 * t + 1) * TILE] = (
             gh * upper * (sig * (1.0 + gate * (1.0 - sig)))
@@ -1175,6 +1282,8 @@
     hbm = pl.BlockSpec(memory_space=pl.ANY)
     pairs = n // 2
 
+    g = g.reshape(rows, pairs, 2 * span, width)
+
     def place(r, p):
         return (r, lax.div(xor_of(lax.axis_index("mp"), 2 * p, n), 2), 0, 0)
 
@@ -1185,6 +1294,7 @@
             pl.BlockSpec(memory_space=pltpu.SMEM),
             hbm,
             pl.BlockSpec((1, 1, 2 * span, width), place),
+            hbm,
             hbm,
             hbm,
         ],
@@ -1206,9 +1316,11 @@
             pltpu.VMEM(dt.shape, BF),
             pltpu.VMEM((slots * TILE, width), F32),
             pltpu.VMEM((2, TILE, width), BF),
+            pltpu.VMEM((2, 2 * span, width), BF),
+            pltpu.VMEM((rows * pairs, 2 * span, slots * TILE), BF),
             pltpu.SemaphoreType.DMA((rows, n, 2)),
             pltpu.SemaphoreType.DMA((rows, n, 2)),
-            pltpu.SemaphoreType.DMA((2 + rows,)),
+            pltpu.SemaphoreType.DMA((4 + rows,)),
             pltpu.SemaphoreType.DMA((2,)),
             pltpu.SemaphoreType.DMA((rows, pairs)),
         ],
@@ -1219,7 +1331,7 @@
             transcendentals=rows * n * span * slots * TILE,
         ),
         name="feed",
-    )(live, x, g.reshape(rows, pairs, 2 * span, width), gu, dt)
+    )(live, x, g, g, gu, dt)
 
 
 def pick(index, table):
@@ -1544,6 +1656,7 @@
     gate_up_slots, down_slots, middle = lax.optimization_barrier(
         (gate_up_slots, down_slots, middle)
     )
+    middle, qa, ka = lax.optimization_barrier((middle, qa, ka))
     gu_t = jnp.swapaxes(gate_up_slots, 1, 2).reshape(slots * 2 * TILE, width)
     d_flat = down_slots.reshape(slots * TILE, width)
     d_t = d_flat.T
@@ -1567,7 +1680,7 @@
     grad_context = dg(grad_attn_b, output_full, NT).astype(BF).reshape(rows, span, QW)
     grad_output = dg(context_b, grad_attn_b, TN).astype(BF)
 
-    dq, dkv, layer_out = attend_back(
+    dq, dkv, layer_out, output_share = attend_back(
         n,
         q,
         kv_all,
@@ -1579,6 +1692,7 @@
         hidden,
         d_flat,
         middle.reshape(rows, span, width),
+        grad_output.reshape(n, -1, width),
     )
     grad_joined_b, sum_q, sum_k, down_total = unproject(
         n,
@@ -1610,7 +1724,7 @@
         x_own,
         grad_middle,
         attention_gain[None],
-        grad_output.reshape(n, -1, width),
+        output_share,
         sums,
     )
     gains = gains.reshape(-1)

time: 742 us -> 710 us (0.957)
  Pallas kernels: 587 us -> 556 us
    pallas_call x3, Pallas kernels: 278 us -> 234 us  [the longest x1 106 us: finish(): pl.pallas_call(functools.partial(finish_kernel, n, m), in_specs=[hbm, hbm...]
    pallas_call x1, Pallas kernels: 82.1 us -> 105 us  [attend_back(): pl.pallas_call(functools.partial(attend_back_kernel, keys, n), grid=(rows...]
    pallas_call x1, Pallas kernels: 105 us -> 94.8 us  [feed(): pl.pallas_call(functools.partial(feed_kernel, n), grid=(rows, pairs), in_...]
  transfers between devices with their start and end apart: 2 -> 2, of which waited for: 1 -> 1; matrix products, arithmetic and copies ran while one was open for 7% -> 8% of each run, Pallas kernels for 39% -> 38%
where the time goes in v5:
time: 710 us; the launch traced here: 704 us
  Pallas kernels  556 us (78%)
  waiting for transfers between devices  48 us (7%)
  local copies, waits for them, and re-layouts  35.5 us (5%)
  other arithmetic  32.3 us (5%)
  matrix products  16.8 us (2%)
  between operations  14.8 us (2%)
    pallas_call x1, Pallas kernels, spread(): pl.pallas_call(functools.partial(spread_kernel, n, m), grid=(rows, n), in...  106 us
    pallas_call x1, Pallas kernels, finish(): pl.pallas_call(functools.partial(finish_kernel, n, m), in_specs=[hbm, hbm...  106 us
    pallas_call x1, Pallas kernels, attend_back(): pl.pallas_call(functools.partial(attend_back_kernel, keys, n), grid=(rows...  105 us
    pallas_call x1, Pallas kernels, feed(): pl.pallas_call(functools.partial(feed_kernel, n), grid=(rows, pairs), in_...  94.8 us
    pallas_call x1, Pallas kernels, project(): pl.pallas_call(functools.partial(project_kernel, n), in_specs=[hbm, vmem,...  86.8 us
    all_gather x1, waiting for transfers between devices, shards(): lax.all_gather(grad_branch.reshape(rows, span, width), 'mp', axis=1, tile...  47.9 us
    pallas_call x1, Pallas kernels, unproject(): pl.pallas_call(functools.partial(unproject_kernel, n), in_specs=[hbm] * 3...  41.8 us
    pallas_call x1, Pallas kernels, attend(): pl.pallas_call(functools.partial(attend_kernel, keys), grid_spec=spec, ou...  16.2 us
  transfers between devices with their start and end apart: 2, of which 1 were waited for; matrix products, arithmetic and copies ran while one was open for 8% of the time, Pallas kernels for 38%

profile of v5, /device:TPU:0, one launch (start us, length us, event | category | flops | bytes accessed | tf_op | source)
XLA Modules:
  0.0 704.3 jit_solution(526874057631354626)
XLA Ops:
  7.3 1.2 fusion.5
  8.5 0.9 slice_compare_fusion
  15.0 1.0 pad_maximum_fusion.w_ref
  16.0 86.8 %project.1 = (bf16[512,2048]{1,0:T(8,128)(2,1)}, f32[512,1920]{1,0:T(8,128)}, bf16[512,1280]{1,0:T(8,128)(2,1)}, bf16[512,2048]{1,0:T(8,128)(2,1)}, bf16[8,256,1...) custom-call(bf16[512,2048]{1,0:T(8,128)(2,1)} %bitcast.81, ...), custom_call_target="tpu_custom_call" | custom-call | tf_op jit(solution)/shard_map/project/pallas_call | solution.py:517
  104.9 16.2 %attend.1 = (bf16[2,256,1280]{2,1,0:T(8,128)(2,1)}, f32[2,256,1280]{2,1,0:T(8,128)}) custom-call(s32[2,3]{1,0:T(2,128)} %pad_add_fusion.info, bf16[2,256,1280]{2,1,0:T(8,128)(2,1)} %bitcast.99, bf16[2,2048,640]{2,1,0:T(8,128)(2,1)} %bitcast.90, s32[2,256,128]{2,1,0:T(8,128)} %broadcast_in_dim.61.start_ref), custom_call_target="tpu_custom_call" | custom-call | flops 21474836480 | bytes 10485760 | tf_op jit(solution)/shard_map/attend/pallas_call | solution.py:933
  121.1 8.0 %multiply_reduce_fusion.1 = (f32[512]{0:T(512)S(1)}, f32[512,2048]{1,0:T(8,128)}) fusion(bf16[512,1280]{1,0:T(8,128)(2,1)} %bitcast.101, bf16[1280,2048]{1,0:T(8,128)(2,1)} %bitcast.121, bf16[512,2048]{1,0:T(8,128)(2,1)S(1)} %bitcast.83), kind=kOutput, calls=%fused_computation.8 | convolution fusion | flops 2688548352 | bytes 12847104 | tf_op jit(solution)/shard_map/dot_general | solution.py:46
  129.1 2.8 copy.38.dt_any
  132.6 8.6 %copy.39 = bf16[6,256,2048]{2,1,0:T(8,128)(2,1)} copy(bf16[6,256,2048]{1,2,0:T(8,128)(2,1)} %bitcast.84) | data formatting | bytes 12582912 | tf_op jit(solution)/shard_map/transpose | solution.py:1660
  141.3 4.0 multiply_convert_fusion
  145.3 47.9 %all-gather.2.cloned.1.call-done = bf16[2,2048,2048]{2,1,0:T(8,128)(2,1)} async-done(((bf16[2,256,2048]{2,1,0:T(8,128)(2,1)}), bf16[2,2048,2048]{2,1,0:T(8,128)(2,1)}) %all-gather.2.cloned.1.call-update) | async-done | bytes 16777232 | tf_op jit(solution)/shard_map/all_gather | solution.py:1645
  193.2 94.8 %feed.1 = (bf16[2,4,512,2048]{3,2,1,0:T(8,128)(2,1)}, bf16[2,4,512,768]{3,2,1,0:T(8,128)(2,1)}, bf16[2,4,512,1536]{3,2,1,0:T(8,128)(2,1)}, bf16[6,128,2048]{2,1,0:T(8,128)(2,1)}) custom-call(f32[6]{0:T(128)} %convert_element_type.52.live_ref, bf16[2,256,2048]{2,1,0:T(8,128)(2,1)} %bitcast.97, bf16[2,4,512,2048]{3,2,1,0:T(8,128)(2,1)} %bitcast.119, ...), custom_call_target="tpu_custom_call" | custom-call | flops 77309411328 | bytes 59768832 | tf_op jit(solution)/shard_map/feed/pallas_call | solution.py:1290
  288.0 106.4 %spread.1 = (f32[2,256,2048]{2,1,0:T(8,128)}, bf16[6,2048,256]{2,1,0:T(8,128)(2,1)}, bf16[12,64,2048]{2,1,0:T(8,128)(2,1)}) custom-call(bf16[2,8,256,1536]{3,2,1,0:T(8,128)(2,1)} %bitcast.74, bf16[1536,2048]{1,0:T(8,128)(2,1)} %bitcast.76, bf16[4096,2048]{1,0:T(8,128)(2,1)} %bitcast.77, bf16[4096,1536]{1,0:T(8,128)(2,1)} %bitcast.75, ...), custom_call_target="tpu_custom_call" | custom-call | flops 1 | bytes 1 | tf_op jit(solution)/shard_map/spread/pallas_call | solution.py:1531
  396.5 2.1 select_convert_fusion.ka_ref
  398.6 5.8 fusion.1
  404.4 1.3 copy-done.1
  405.7 3.5 multiply_add_fusion.mid_any
  409.2 4.8 convolution_convert_fusion
  414.1 4.0 convolution_convert_fusion.1
  418.1 104.8 %attend_back.1 = (f32[2,256,1280]{2,1,0:T(8,128)}, bf16[2,2048,640]{2,1,0:T(8,128)(2,1)}, f32[2,256,2048]{2,1,0:T(8,128)}, bf16[160,2048]{1,0:T(8,128)(2,1)}) custom-call(bf16[2,256,1280]{2,1,0:T(8,128)(2,1)} %bitcast.100, bf16[2,2048,640]{2,1,0:T(8,128)(2,1)} %bitcast.91, bf16[2,256,128]{2,1,0:T(8,128)(2,1)} %select_convert_fusion.1.qa_ref, ...), custom_call_target="tpu_custom_call" | custom-call | flops 1 | bytes 1 | tf_op jit(solution)/shard_map/attend_back/pallas_call | solution.py:1090
  522.9 41.8 %unproject.1 = (bf16[512,1920]{1,0:T(8,128)(2,1)}, f32[8,128]{1,0:T(8,128)}, f32[8,128]{1,0:T(8,128)}, f32[768,2048]{1,0:T(8,128)}) custom-call(f32[512,1280]{1,0:T(8,128)} %bitcast.96, bf16[2,8,256,640]{3,2,1,0:T(8,128)(2,1)} %bitcast.89, f32[512,1920]{1,0:T(8,128)} %get-tuple-element.65.raw_any, f32[512,128]{1,0:T(8,128)} %copy.36.cos_ref, ...), custom_call_target="tpu_custom_call" | custom-call | flops 1 | bytes 1 | tf_op jit(solution)/shard_map/unproject/pallas_call | solution.py:645
  566.1 1.8 concatenate.19.sums_ref
  567.9 105.5 %finish.1 = (f32[512,2048]{1,0:T(8,128)}, f32[256,1920]{1,0:T(8,128)}, f32[160,2048]{1,0:T(8,128)}, f32[40,128]{1,0:T(8,128)}) custom-call(bf16[512,2048]{1,0:T(8,128)(2,1)} %get-tuple-element.62.normed_any, bf16[512,1920]{1,0:T(8,128)(2,1)} %get-tuple-element.67.gj_any, bf16[8,256,1920]{2,1,0:T(8,128)(2,1)} %get-tuple-element.68.w_any, ...), custom_call_target="tpu_custom_call" | custom-call | flops 1 | bytes 1 | tf_op jit(solution)/shard_map/finish/pallas_call | solution.py:830
  673.4 1.4 fusion.6
  674.8 1.3 slice_bitcast_fusion
  676.1 8.9 %convert_element_type.57 = f32[6,2048,256]{2,1,0:T(8,128)} convert(bf16[6,2048,256]{2,1,0:T(8,128)(2,1)} %all-reduce.4.cloned.1.call-done) | non-fusion elementwise | flops 3145728 | bytes 18874368 | tf_op jit(solution)/shard_map/convert_element_type | solution.py:1739
  685.0 2.1 copy.57
  687.1 1.6 copy-done.6
  688.7 2.1 copy.58
  690.8 1.2 copy-done.7
  692.0 1.3 copy.59
  693.3 1.1 copy.60
  694.3 2.7 copy.61
  (85 shorter events, 11.8 us)
Async XLA Ops:
  7.2 7.8 %slice-start.2 = ((bf16[256,1920]{1,0:T(8,128)(2,1)}), bf16[256,1280]{1,0:T(8,128)(2,1)S(1)}, s32[]{:S(2)}) async-start(bf16[256,1920]{1,0:T(8,128)(2,1)} %param.18), calls=%async_computation.4 | async-start | bytes 1310720 | tf_op jit(solution)/shard_map/slice | solution.py:1600
  7.2 6.7 copy-start.12
  7.2 7.2 %copy-start.13 = (f32[64]{0:T(128)S(1)}, f32[64]{0:T(128)}, u32[]{:S(2)}) copy-start(f32[64]{0:T(128)} %param.17) | copy-start | bytes 772
  7.2 186.0 %all-gather.2.cloned.1.call-start = ((), (), s32[]{:S(2)}) async-start(), calls=%async_computation | async-start | bytes 18874368 | tf_op jit(solution)/shard_map/all_gather | solution.py:1645
  102.8 573.3 %all-reduce.4.cloned.1.call-start = ((), (), s32[]{:S(2)}) async-start(), calls=%async_computation.1 | async-start | bytes 12582912 | tf_op jit(solution)/shard_map/psum | solution.py:1670
  104.9 16.2 %copy-start.4 = (bf16[2,256,2048]{2,1,0:T(8,128)(2,1)S(1)}, bf16[2,256,2048]{2,1,0:T(8,128)(2,1)}, u32[]{:S(2)}) copy-start(bf16[2,256,2048]{2,1,0:T(8,128)(2,1)} %param.12) | copy-start | bytes 6291460
  121.1 8.0 %copy-start.3 = (bf16[6,128,2048]{2,1,0:T(8,128)(2,1)S(1)}, bf16[6,128,2048]{2,1,0:T(8,128)(2,1)}, u32[]{:S(2)}) copy-start(bf16[6,128,2048]{2,1,0:T(8,128)(2,1)} %param.22) | copy-start | bytes 9437188
  129.1 2.8 copy-start.14
  132.6 8.6 %copy-start.11 = (f32[2048]{0:T(1024)S(1)}, f32[2048]{0:T(1024)}, u32[]{:S(2)}) copy-start(f32[2048]{0:T(1024)} %param.20) | copy-start | bytes 24580
  394.5 0.7 copy-start.10
  398.6 5.8 copy-start
  398.6 7.1 %copy-start.1 = (f32[2,256,2048]{2,1,0:T(8,128)S(1)}, f32[2,256,2048]{2,1,0:T(8,128)}, u32[]{:S(2)}) copy-start(f32[2,256,2048]{2,1,0:T(8,128)} %param.23) | copy-start | bytes 12582916
  405.6 3.6 copy-start.8
  405.6 8.5 %slice-start.3 = ((s8[5242880]{0:T(1024)(128)(4,1)}), s8[4194304]{0:T(1024)(128)(4,1)S(1)}, s32[]{:S(2)}) async-start(s8[5242880]{0:T(1024)(128)(4,1)} %bitcast.122), calls=%async_computation.5 | async-start | bytes 8388608
  409.2 4.9 copy-start.2
  409.2 4.9 slice-start.4
  676.1 8.9 %copy-start.5 = (f32[2,256,2048]{2,1,0:T(8,128)S(1)}, f32[2,256,2048]{2,1,0:T(8,128)}, u32[]{:S(2)}) copy-start(f32[2,256,2048]{2,1,0:T(8,128)} %get-tuple-element.106) | copy-start | bytes 12582916
  685.0 3.7 copy-start.6
  685.0 9.4 %slice-start = ((s8[6291456]{0:T(1024)(128)(4,1)}), s8[4194304]{0:T(1024)(128)(4,1)S(1)}, s32[]{:S(2)}) async-start(s8[6291456]{0:T(1024)(128)(4,1)} %bitcast.85), calls=%async_computation.2 | async-start | bytes 8388608
  688.7 3.3 copy-start.7
  688.7 4.6 copy-start.9
  688.7 5.7 slice-start.1
Sparse Core Ops, SparseCore 0:
  102.9 90.2 all-gather.1
  394.6 241.6 all-reduce.3

commit v6 on v5

--- a/solution.py
+++ b/solution.py
@@ -2,6 +2,7 @@
 
 import jax
 import jax.numpy as jnp
+import numpy as np
 from jax import lax
 from jax.experimental import pallas as pl
 from jax.experimental.pallas import tpu as pltpu
@@ -50,20 +51,11 @@
     return lax.dot_general(a, b, dims, preferred_element_type=F32)
 
 
-def doc_starts(docs):
-    index = jnp.arange(docs.shape[-1], dtype=jnp.int32)
-    change = jnp.concatenate(
-        [jnp.ones(docs.shape[:-1] + (1,), dtype=jnp.bool_), docs[..., 1:] != docs[..., :-1]],
-        axis=-1,
-    )
-    return lax.cummax(jnp.where(change, index, 0), axis=docs.ndim - 1)
-
-
 def rotary_tables(positions):
     half_dim = HD // 2
     freqs = 1.0 / 10000.0 ** (jnp.arange(half_dim, dtype=jnp.float32) * 2.0 / HD)
-    angles = positions.astype(jnp.float32)[..., None] * freqs
-    return jnp.tile(jnp.cos(angles), 4), jnp.tile(jnp.sin(angles), 4)
+    angles = positions.astype(jnp.float32)[..., None] * jnp.tile(freqs, 4)
+    return jnp.cos(angles), jnp.sin(angles)
 
 
 def rms_scale(values):
@@ -304,17 +296,22 @@
 
 
 def add_up(out, terms):
-    rows = out.shape[-2]
+    rows, width = out.shape[-2:]
     step = 16
+    while 2 * step * width <= 32768 and rows % (2 * step) == 0:
+        step *= 2
     lead = (slice(None),) * (len(out.shape) - 2)
 
     @pl.loop(0, rows // step)
     def _(i):
         at = lead + (pl.ds(pl.multiple_of(i * step, step), step), slice(None))
-        total = terms[0][at].astype(F32)
-        for t in terms[1:]:
-            total = total + t[at].astype(F32)
-        out[at] = total.astype(out.dtype)
+        if len(terms) == 2 and all(t.dtype == BF for t in (out, *terms)):
+            out[at] = terms[0][at] + terms[1][at]
+        else:
+            total = terms[0][at].astype(F32)
+            for t in terms[1:]:
+                total = total + t[at].astype(F32)
+            out[at] = total.astype(out.dtype)
 
 
 def scatter_scratch(n, shape, half):
@@ -550,19 +547,18 @@
 
 
 def unproject_kernel(
-    n, dq_any, dkv_any, raw_any, cos_ref, sin_ref, gq_ref, gk_ref, ones_ref, down_any,
-    gj_ref, sq_ref, sk_ref, wide_any,
-    dkv_own, dkv_ref, dq_ref, raw_ref, down_ref, wide_ref, load, *scratch,
+    n, dq_any, dkv_any, raw_any, cos_ref, sin_ref, gq_ref, gk_ref, ones_ref,
+    gj_ref, sq_ref, sk_ref,
+    dkv_own, dkv_ref, dq_ref, raw_ref, load, *scratch,
 ):
     me = lax.axis_index("mp")
     early = [
-        pltpu.make_async_copy(dkv_any.at[:, flip(me, k)], dkv_ref.at[k // 2], load.at[4 + k // 2])
+        pltpu.make_async_copy(dkv_any.at[:, flip(me, k)], dkv_ref.at[k // 2], load.at[2 + k // 2])
         for k in range(n - 2, -1, -2)
     ]
     late = [
         pltpu.make_async_copy(dq_any, dq_ref, load.at[0]),
         pltpu.make_async_copy(raw_any, raw_ref, load.at[1]),
-        pltpu.make_async_copy(down_any, down_ref, load.at[2]),
     ]
     for c in early + late:
         c.start()
@@ -622,9 +618,6 @@
             for k in left:
                 keys.even(k, dkv_term(k))
 
-    wide_ref[...] = down_ref[...].astype(F32)
-    keep = pltpu.make_async_copy(wide_ref, wide_any, load.at[3])
-    keep.start()
     keys.own(dkv_term(0), dkv_own)
 
     @pl.loop(0, tokens // chunk)
@@ -632,10 +625,9 @@
         back(i, range(QW // LANES, count), False)
 
     keys.drain(dkv_term(0))
-    keep.wait()
-
-
-def unproject(n, dq, dkv, raw, cos, sin, gq, gk, ones, down):
+
+
+def unproject(n, dq, dkv, raw, cos, sin, gq, gk, ones):
     tokens, columns = raw.shape
     rows = dkv.shape[0]
     span = tokens // rows
@@ -644,28 +636,25 @@
     hbm = pl.BlockSpec(memory_space=pl.ANY)
     return pl.pallas_call(
         functools.partial(unproject_kernel, n),
-        in_specs=[hbm] * 3 + [vmem] * 5 + [hbm],
-        out_specs=[vmem] * 3 + [hbm],
+        in_specs=[hbm] * 3 + [vmem] * 5,
+        out_specs=[vmem] * 3,
         out_shape=[
             jax.ShapeDtypeStruct((tokens, columns), BF),
             jax.ShapeDtypeStruct((8, LANES), F32),
             jax.ShapeDtypeStruct((8, LANES), F32),
-            jax.ShapeDtypeStruct(down.shape, F32),
         ],
         scratch_shapes=[
             pltpu.VMEM((rows, span, kvw), F32),
             pltpu.VMEM((n // 2, rows, span, kvw), BF),
             pltpu.VMEM(dq.shape, F32),
             pltpu.VMEM(raw.shape, F32),
-            pltpu.VMEM(down.shape, BF),
-            pltpu.VMEM(down.shape, F32),
-            pltpu.SemaphoreType.DMA((4 + n // 2,)),
+            pltpu.SemaphoreType.DMA((2 + n // 2,)),
         ]
         + scatter_scratch(n, (rows, span, kvw), (span, kvw)),
         compiler_params=params(mib=60, axes=0, key=2),
         cost_estimate=TINY,
         name="unproject",
-    )(dq, dkv, raw, cos, sin, gq, gk, ones, down)
+    )(dq, dkv, raw, cos, sin, gq, gk, ones)
 
 
 GAIN_ROWS = 40
@@ -945,7 +934,7 @@
 
 
 def attend_back_kernel(
-    keys, n, q_ref, kv_ref, qa_ref, ka_ref, do_ref, ctx_ref, rl_ref, a_ref, w_any, base_any,
+    keys, n, q_ref, kv_ref, qa_ref, ka_ref, do_ref, ctx_ref, rl_ref, a_ref, w_any,
     gout_any, dq_ref, dkv_ref, o_ref, share_ref, acc, sides, gout_ref, moves, *scratch,
 ):
     span = q_ref.shape[1]
@@ -954,7 +943,7 @@
     me = lax.axis_index("mp")
     rows = o_ref.shape[0]
     now = pl.program_id(0) * KVH + pl.program_id(1)
-    sums = TileSum(n, me, o_ref, w_any, scratch, base_any)
+    sums = TileSum(n, me, o_ref, w_any, scratch)
     half_w = share_ref.shape[1] // 2
     outs = make_scatter(
         n, me, lambda ref, h: ref.at[:, pl.ds(h * half_w, half_w)], scratch[-6:]
@@ -1075,7 +1064,7 @@
         outs.drain(out_term(0))
 
 
-def attend_back(n, q, kv, qa, ka, do, ctx, rl, a, w, base, gout):
+def attend_back(n, q, kv, qa, ka, do, ctx, rl, a, w, gout):
     rows, span, _ = q.shape
     length = kv.shape[1]
     keys = min(512, length)
@@ -1099,7 +1088,6 @@
             pl.BlockSpec((1, span, GW), own),
             pl.BlockSpec((1, span, GW), own),
             pl.BlockSpec((1, batch, span, depth), place),
-            pl.BlockSpec(memory_space=pl.ANY),
             pl.BlockSpec(memory_space=pl.ANY),
             pl.BlockSpec(memory_space=pl.ANY),
         ],
@@ -1126,7 +1114,7 @@
         compiler_params=params(mib=60, axes=2, key=4),
         cost_estimate=TINY,
         name="attend_back",
-    )(q, kv, qa, ka, do, ctx, rl, a, w, base, gout)
+    )(q, kv, qa, ka, do, ctx, rl, a, w, gout)
 
 
 def xor_of(a, b, n):
@@ -1144,7 +1132,7 @@
 ):
     me = lax.axis_index("mp")
     rows, span, width = x_own.shape
-    slots = gu_ref.shape[0]
+    slots = gu_any.shape[0]
     r, p = pl.program_id(0), pl.program_id(1)
     pairs = n // 2
     now = r * pairs + p
@@ -1167,12 +1155,15 @@
 
     def own_copy(row):
         at = pl.ds(pl.multiple_of(lax.rem(me, 2) * span, span), span)
-        return pltpu.make_async_copy(x_own.at[row], x_vm.at[row, 0, at], loads.at[2 + row])
+        return pltpu.make_async_copy(x_own.at[row], x_vm.at[row, 0, at], loads.at[1 + row])
 
     fetch = [
-        pltpu.make_async_copy(gu_any, gu_ref, loads.at[0]),
-        pltpu.make_async_copy(dt_any, dt_ref, loads.at[1]),
+        pltpu.make_async_copy(
+            gu_any.at[t], gu_ref.at[:, pl.ds(2 * t * TILE, 2 * TILE)], loads.at[3 + rows + t]
+        )
+        for t in range(slots)
     ]
+    fetch.append(pltpu.make_async_copy(dt_any, dt_ref, loads.at[0]))
 
     def events(row, upto):
         todo = gather(row).even
@@ -1185,7 +1176,7 @@
         block = lax.div(xor_of(me, 2 * lax.rem(i, pairs), n), 2)
         to = lax.rem(i, 2)
         return pltpu.make_async_copy(
-            g_any.at[lax.div(i, pairs), block], g_two.at[to], loads.at[2 + rows + to]
+            g_any.at[lax.div(i, pairs), block], g_two.at[to], loads.at[1 + rows + to]
         )
 
     @pl.when(now == 0)
@@ -1237,8 +1228,9 @@
 
     save(r, p).start()
     x = x_vm.at[r, p]
+    full = mm(x[...], gu_ref[...])
     for t in range(slots):
-        both = mm(x[...], gu_ref[t])
+        both = full[:, 2 * t * TILE : 2 * (t + 1) * TILE]
         gate, upper = both[:, :TILE], both[:, TILE:]
         live = live_ref[t]
         sig = jax.nn.sigmoid(gate)
@@ -1250,12 +1242,7 @@
         ).astype(BF)
         dgu_ref[0, 0, :, (2 * t + 1) * TILE : (2 * t + 2) * TILE] = (gh * silu).astype(BF)
 
-    cut = LANES
-
-    @pl.loop(0, slots * TILE // cut)
-    def _(i):
-        at = pl.ds(pl.multiple_of(i * cut, cut), cut)
-        d_sum[at, :] += dg(hid_ref[0, 0, :, at], g_ref[0, 0], TN)
+    d_sum[...] += dg(hid_ref[0, 0], g_ref[0, 0], TN)
 
     @pl.when(now == rows * pairs - 1)
     def _():
@@ -1312,7 +1299,7 @@
         ],
         scratch_shapes=[
             pltpu.VMEM((rows, pairs, 2 * span, width), BF),
-            pltpu.VMEM(gu.shape, BF),
+            pltpu.VMEM((width, slots * 2 * TILE), BF),
             pltpu.VMEM(dt.shape, BF),
             pltpu.VMEM((slots * TILE, width), F32),
             pltpu.VMEM((2, TILE, width), BF),
@@ -1320,7 +1307,7 @@
             pltpu.VMEM((rows * pairs, 2 * span, slots * TILE), BF),
             pltpu.SemaphoreType.DMA((rows, n, 2)),
             pltpu.SemaphoreType.DMA((rows, n, 2)),
-            pltpu.SemaphoreType.DMA((4 + rows,)),
+            pltpu.SemaphoreType.DMA((3 + rows + slots,)),
             pltpu.SemaphoreType.DMA((2,)),
             pltpu.SemaphoreType.DMA((rows, pairs)),
         ],
@@ -1349,8 +1336,8 @@
 
 
 class TileSum:
-    def __init__(self, n, me, o_ref, w_any, scratch, base=None):
-        self.n, self.me, self.o_ref, self.w_any, self.base = n, me, o_ref, w_any, base
+    def __init__(self, n, me, o_ref, w_any, scratch):
+        self.n, self.me, self.o_ref, self.w_any = n, me, o_ref, w_any
         self.w_ref, self.terms, self.core, self.link = scratch[:4]
         self.sems, self.load = scratch[4:8], scratch[8]
         self.rows, self.span, _ = o_ref.shape
@@ -1367,14 +1354,10 @@
         )
 
     def start(self, meet=greet):
-        fetch = [pltpu.make_async_copy(self.w_any, self.w_ref, self.load.at[0])]
-        if self.base is not None:
-            fetch.append(pltpu.make_async_copy(self.base, self.o_ref, self.load.at[1]))
-        for c in fetch:
-            c.start()
+        fetch = pltpu.make_async_copy(self.w_any, self.w_ref, self.load.at[0])
+        fetch.start()
         meet(self.n, self.me)
-        for c in fetch:
-            c.wait()
+        fetch.wait()
 
     def close(self, row):
         last = self.scatter(row)
@@ -1416,8 +1399,7 @@
         @pl.when(k == 0)
         def _():
             sums.core_copy(1, self.core.at[r, 0]).wait_recv()
-            here = self.o_ref.at[r]
-            add_up(here, [mine, self.core.at[r, 0]] + ([] if self.base is None else [here]))
+            add_up(self.o_ref.at[r], [mine, self.core.at[r, 0]])
 
     def end(self):
         self.close(self.rows - 1)
@@ -1439,7 +1421,7 @@
         pltpu.SemaphoreType.DMA((rows, n // 2)),
         pltpu.SemaphoreType.DMA((rows, 2, n // 2 - 1)),
         pltpu.SemaphoreType.DMA((rows, 2, n // 2 - 1)),
-        pltpu.SemaphoreType.DMA((2,)),
+        pltpu.SemaphoreType.DMA((1,)),
     ]
 
 
@@ -1599,14 +1581,14 @@
     attend_w = jnp.concatenate(
         [attend_weight[:, :QW], jnp.concatenate([keys_w, values_w], 2).reshape(-1, 2 * kw)], 1
     )
-    starts = doc_starts(doc_ids)
-    local_start = lax.dynamic_slice_in_dim(starts, offset, span, 1)
+    below = [jnp.sum((doc_ids < d).astype(jnp.int32), axis=1, keepdims=True) for d in (1, 2)]
+    local_docs = lax.dynamic_slice_in_dim(doc_ids, offset, span, 1)
+    local_start = jnp.where(local_docs == 2, below[1], jnp.where(local_docs == 1, below[0], 0))
     local_pos = offset + jnp.arange(span, dtype=jnp.int32)[None] - local_start
     cos, sin = rotary_tables(local_pos.reshape(tokens))
     gq = jnp.tile(query_gain, 2)[None]
     gk = jnp.concatenate([key_gain, jnp.ones_like(key_gain)])[None]
-    lane = jnp.arange(LANES) // HD
-    ones = (lane[:, None] == lane[None, :]).astype(BF)
+    ones = jnp.asarray(np.kron(np.eye(LANES // HD), np.ones((HD, HD))), BF)
     key_block = min(512, length)
     info = jnp.stack(
         [
@@ -1656,7 +1638,7 @@
     gate_up_slots, down_slots, middle = lax.optimization_barrier(
         (gate_up_slots, down_slots, middle)
     )
-    middle, qa, ka = lax.optimization_barrier((middle, qa, ka))
+    normed_fb, qa, ka = lax.optimization_barrier((normed_fb, qa, ka))
     gu_t = jnp.swapaxes(gate_up_slots, 1, 2).reshape(slots * 2 * TILE, width)
     d_flat = down_slots.reshape(slots * TILE, width)
     d_t = d_flat.T
@@ -1680,7 +1662,7 @@
     grad_context = dg(grad_attn_b, output_full, NT).astype(BF).reshape(rows, span, QW)
     grad_output = dg(context_b, grad_attn_b, TN).astype(BF)
 
-    dq, dkv, layer_out, output_share = attend_back(
+    dq, dkv, ffn_out, output_share = attend_back(
         n,
         q,
         kv_all,
@@ -1691,10 +1673,10 @@
         rl,
         hidden,
         d_flat,
-        middle.reshape(rows, span, width),
         grad_output.reshape(n, -1, width),
     )
-    grad_joined_b, sum_q, sum_k, down_total = unproject(
+    layer_out = middle.reshape(rows, span, width) + ffn_out
+    grad_joined_b, sum_q, sum_k = unproject(
         n,
         dq.reshape(tokens, QW),
         dkv.reshape(rows, n, span, -1),
@@ -1704,7 +1686,10 @@
         gq,
         gk,
         ones,
-        down_total.reshape(slots * TILE, width),
+    )
+    down_total = down_total.astype(F32)
+    grad_joined_b, layer_out, down_total = lax.optimization_barrier(
+        (grad_joined_b, layer_out, down_total)
     )
     sums = jnp.concatenate(
         [
@@ -1737,7 +1722,7 @@
         attend_total,
         output_total,
         gate_up_total.astype(F32),
-        down_total.reshape(slots, TILE, width),
+        down_total,
         gains[:width],
         gain_query,
         gain_key,

time: 710 us -> 693 us (0.976)
  Pallas kernels: 556 us -> 543 us
  local copies, waits for them, and re-layouts: 35.5 us -> 26.6 us
  other arithmetic: 32.3 us -> 39.9 us
    unnamed x48 -> x46, local copies, waits for them, and re-layouts: 14.3 us -> 7.23 us
where the time goes in v6:
time: 693 us; the launch traced here: 687 us
  Pallas kernels  543 us (78%)
  waiting for transfers between devices  50.1 us (7%)
  other arithmetic  39.9 us (6%)
  local copies, waits for them, and re-layouts  26.6 us (4%)
  between operations  14.6 us (2%)
  matrix products  13.1 us (2%)
    pallas_call x1, Pallas kernels, spread(): pl.pallas_call(functools.partial(spread_kernel, n, m), grid=(rows, n), in...  105 us
    pallas_call x1, Pallas kernels, attend_back(): pl.pallas_call(functools.partial(attend_back_kernel, keys, n), grid=(rows...  103 us
    pallas_call x1, Pallas kernels, finish(): pl.pallas_call(functools.partial(finish_kernel, n, m), in_specs=[hbm, hbm...  102 us
    pallas_call x1, Pallas kernels, feed(): pl.pallas_call(functools.partial(feed_kernel, n), grid=(rows, pairs), in_...  89 us
    pallas_call x1, Pallas kernels, project(): pl.pallas_call(functools.partial(project_kernel, n), in_specs=[hbm, vmem,...  86.9 us
    all_gather x1, waiting for transfers between devices, shards(): lax.all_gather(grad_branch.reshape(rows, span, width), 'mp', axis=1, tile...  50.1 us
    pallas_call x1, Pallas kernels, unproject(): pl.pallas_call(functools.partial(unproject_kernel, n), in_specs=[hbm] * 3...  39.5 us
    pallas_call x1, Pallas kernels, attend(): pl.pallas_call(functools.partial(attend_kernel, keys), grid_spec=spec, ou...  16.6 us
  transfers between devices with their start and end apart: 2, of which 1 were waited for; matrix products, arithmetic and copies ran while one was open for 8% of the time, Pallas kernels for 38%

profile of v6, /device:TPU:0, one launch (start us, length us, event | category | flops | bytes accessed | tf_op | source)
XLA Modules:
  0.0 687.3 jit_solution(9097274523736549448)
XLA Ops:
  7.3 1.2 fusion.6
  9.1 0.9 fusion.5
  11.8 1.0 pad_maximum_fusion.w_ref
  12.9 1.8 multiply_sine_fusion
  14.6 86.9 %project.1 = (bf16[512,2048]{1,0:T(8,128)(2,1)}, f32[512,1920]{1,0:T(8,128)}, bf16[512,1280]{1,0:T(8,128)(2,1)}, bf16[512,2048]{1,0:T(8,128)(2,1)}, bf16[8,256,1...) custom-call(bf16[512,2048]{1,0:T(8,128)(2,1)} %bitcast.70, f32[1,2048]{1,0:T(1,128)} %bitcast.94, ...), custom_call_target="tpu_custom_call" | custom-call | tf_op jit(solution)/shard_map/project/pallas_call | solution.py:514
  102.6 0.8 broadcast_in_dim.73.start_ref
  103.5 16.6 %attend.1 = (bf16[2,256,1280]{2,1,0:T(8,128)(2,1)}, f32[2,256,1280]{2,1,0:T(8,128)}) custom-call(s32[2,3]{1,0:T(2,128)} %pad_add_fusion.info, bf16[2,256,1280]{2,1,0:T(8,128)(2,1)} %bitcast.86, bf16[2,2048,640]{2,1,0:T(8,128)(2,1)} %bitcast.76, s32[2,256,128]{2,1,0:T(8,128)} %broadcast_in_dim.73.start_ref), custom_call_target="tpu_custom_call" | custom-call | flops 21474836480 | bytes 10485760 | tf_op jit(solution)/shard_map/attend/pallas_call | solution.py:922
  120.1 4.5 multiply_reduce_fusion.1
  126.0 2.0 select_convert_fusion.ka_ref
  128.0 1.7 multiply_convert_fusion
  130.4 2.8 copy.33.dt_any
  133.2 8.6 %copy.34 = bf16[6,256,2048]{2,1,0:T(8,128)(2,1)} copy(bf16[6,256,2048]{1,2,0:T(8,128)(2,1)} %bitcast.73) | data formatting | bytes 12582912 | tf_op jit(solution)/shard_map/transpose | solution.py:1642
  141.9 50.1 %all-gather.2.cloned.1.call-done = bf16[2,2048,2048]{2,1,0:T(8,128)(2,1)} async-done(((bf16[2,256,2048]{2,1,0:T(8,128)(2,1)}), bf16[2,2048,2048]{2,1,0:T(8,128)(2,1)}) %all-gather.2.cloned.1.call-update) | async-done | bytes 16777232 | tf_op jit(solution)/shard_map/all_gather | solution.py:1627
  191.9 89.0 %feed.1 = (bf16[2,4,512,2048]{3,2,1,0:T(8,128)(2,1)}, bf16[2,4,512,768]{3,2,1,0:T(8,128)(2,1)}, bf16[2,4,512,1536]{3,2,1,0:T(8,128)(2,1)}, bf16[6,128,2048]{2,1,0:T(8,128)(2,1)}) custom-call(f32[6]{0:T(128)} %convert_element_type.61.live_ref, bf16[2,256,2048]{2,1,0:T(8,128)(2,1)} %bitcast.83, bf16[2,4,512,2048]{3,2,1,0:T(8,128)(2,1)} %bitcast.99, ...), custom_call_target="tpu_custom_call" | custom-call | flops 77309411328 | bytes 59768832 | tf_op jit(solution)/shard_map/feed/pallas_call | solution.py:1277
  280.9 105.1 %spread.1 = (f32[2,256,2048]{2,1,0:T(8,128)}, bf16[6,2048,256]{2,1,0:T(8,128)(2,1)}, bf16[12,64,2048]{2,1,0:T(8,128)(2,1)}) custom-call(bf16[2,8,256,1536]{3,2,1,0:T(8,128)(2,1)} %bitcast.63, bf16[1536,2048]{1,0:T(8,128)(2,1)} %bitcast.65, bf16[4096,2048]{1,0:T(8,128)(2,1)} %bitcast.66, bf16[4096,1536]{1,0:T(8,128)(2,1)} %bitcast.64, ...), custom_call_target="tpu_custom_call" | custom-call | flops 1 | bytes 1 | tf_op jit(solution)/shard_map/spread/pallas_call | solution.py:1513
  386.1 4.7 fusion.1
  390.8 1.6 copy-done.2
  392.4 3.8 multiply_add_fusion.mid_any
  396.2 4.7 convolution_convert_fusion
  400.8 4.0 convolution_convert_fusion.1
  404.8 103.2 %attend_back.1 = (f32[2,256,1280]{2,1,0:T(8,128)}, bf16[2,2048,640]{2,1,0:T(8,128)(2,1)}, f32[2,256,2048]{2,1,0:T(8,128)}, bf16[160,2048]{1,0:T(8,128)(2,1)}) custom-call(bf16[2,256,1280]{2,1,0:T(8,128)(2,1)} %bitcast.87, bf16[2,2048,640]{2,1,0:T(8,128)(2,1)} %bitcast.77, bf16[2,256,128]{2,1,0:T(8,128)(2,1)} %select_convert_fusion.1.qa_ref, ...), custom_call_target="tpu_custom_call" | custom-call | flops 1 | bytes 1 | tf_op jit(solution)/shard_map/attend_back/pallas_call | solution.py:1079
  508.1 39.5 %unproject.1 = (bf16[512,1920]{1,0:T(8,128)(2,1)}, f32[8,128]{1,0:T(8,128)}, f32[8,128]{1,0:T(8,128)}) custom-call(f32[512,1280]{1,0:T(8,128)} %bitcast.82, bf16[2,8,256,640]{3,2,1,0:T(8,128)(2,1)} %bitcast.75, f32[512,1920]{1,0:T(8,128)} %get-tuple-element.65.raw_any, f32[512,128]{1,0:T(8,128)} %get-tuple-element.95.cos_ref, ...), custom_call_target="tpu_custom_call" | custom-call | flops 1 | bytes 1 | tf_op jit(solution)/shard_map/unproject/pallas_call | solution.py:637
  547.6 6.7 add.78
  554.3 3.5 bitcast_convert_fusion
  559.2 1.8 concatenate.15.sums_ref
  561.0 102.3 %finish.1 = (f32[512,2048]{1,0:T(8,128)}, f32[256,1920]{1,0:T(8,128)}, f32[160,2048]{1,0:T(8,128)}, f32[40,128]{1,0:T(8,128)}) custom-call(bf16[512,2048]{1,0:T(8,128)(2,1)} %get-tuple-element.70.normed_any, bf16[512,1920]{1,0:T(8,128)(2,1)} %get-tuple-element.71.gj_any, bf16[8,256,1920]{2,1,0:T(8,128)(2,1)} %get-tuple-element.72.w_any, ...), custom_call_target="tpu_custom_call" | custom-call | flops 1 | bytes 1 | tf_op jit(solution)/shard_map/finish/pallas_call | solution.py:819
  663.3 1.4 fusion.7
  664.7 1.3 slice_bitcast_fusion
  666.0 8.9 %convert_element_type.67 = f32[6,2048,256]{2,1,0:T(8,128)} convert(bf16[6,2048,256]{2,1,0:T(8,128)(2,1)} %all-reduce.3.cloned.1.call-done) | non-fusion elementwise | flops 3145728 | bytes 18874368 | tf_op jit(solution)/shard_map/convert_element_type | solution.py:1724
  674.9 2.1 copy.42
  677.9 1.3 copy.43
  679.1 1.1 copy.44
  (77 shorter events, 7.9 us)
Async XLA Ops:
  7.2 4.7 slice-start
  7.2 3.5 copy-start.13
  7.2 4.1 copy-start.14
  7.2 184.7 %all-gather.2.cloned.1.call-start = ((), (), s32[]{:S(2)}) async-start(), calls=%async_computation | async-start | bytes 18874368 | tf_op jit(solution)/shard_map/all_gather | solution.py:1627
  101.5 18.6 %slice-start.1 = ((s8[5242880]{0:T(1024)(128)(4,1)}), s8[1048576]{0:T(1024)(128)(4,1)S(1)}, s32[]{:S(2)}) async-start(s8[5242880]{0:T(1024)(128)(4,1)} %bitcast.101), calls=%async_computation.3 | async-start | bytes 2097152
  101.5 564.5 %all-reduce.3.cloned.1.call-start = ((), (), s32[]{:S(2)}) async-start(), calls=%async_computation.1 | async-start | bytes 12582912 | tf_op jit(solution)/shard_map/psum | solution.py:1652
  103.5 16.6 %copy-start.5 = (bf16[2,256,2048]{2,1,0:T(8,128)(2,1)S(1)}, bf16[2,256,2048]{2,1,0:T(8,128)(2,1)}, u32[]{:S(2)}) copy-start(bf16[2,256,2048]{2,1,0:T(8,128)(2,1)} %param.13) | copy-start | bytes 6291460
  103.5 16.6 %slice-start.2 = ((s8[5242880]{0:T(1024)(128)(4,1)}), s8[4194304]{0:T(1024)(128)(4,1)S(1)}, s32[]{:S(2)}) async-start(s8[5242880]{0:T(1024)(128)(4,1)} %bitcast.101), calls=%async_computation.4 | async-start | bytes 8388608
  120.1 4.5 copy-start.11
  120.1 7.9 %copy-start.12 = (f32[2048]{0:T(1024)S(1)}, f32[2048]{0:T(1024)}, u32[]{:S(2)}) copy-start(f32[2048]{0:T(1024)} %param.21) | copy-start | bytes 24580
  124.6 5.1 copy-start
  125.2 4.5 copy-start.15
  125.2 5.2 copy-start.4
  386.1 4.7 copy-start.1
  386.1 6.3 copy-start.2
  392.4 3.8 copy-start.10
  392.4 8.5 %slice-start.3 = ((s8[5242880]{0:T(1024)(128)(4,1)}), s8[4194304]{0:T(1024)(128)(4,1)S(1)}, s32[]{:S(2)}) async-start(s8[5242880]{0:T(1024)(128)(4,1)} %bitcast.104), calls=%async_computation.5 | async-start | bytes 8388608
  396.1 4.7 copy-start.3
  396.2 4.7 slice-start.4
  547.6 6.7 copy-start.7
  666.0 8.9 %copy-start.6 = (f32[512,2048]{1,0:T(8,128)S(1)}, f32[512,2048]{1,0:T(8,128)}, u32[]{:S(2)}) copy-start(f32[512,2048]{1,0:T(8,128)} %get-tuple-element.76) | copy-start | bytes 12582916
  674.9 3.0 copy-start.8
  674.9 4.2 copy-start.9
Sparse Core Ops, SparseCore 0:
  101.7 90.2 all-gather.1
  386.2 241.3 all-reduce.2

commit v7 on v6

--- a/solution.py
+++ b/solution.py
@@ -444,6 +444,9 @@
     chunk = min(128, tokens)
     lane = lax.broadcasted_iota(jnp.int32, (chunk, LANES), 1)
 
+    gain_q = jnp.concatenate([gq_ref[...], gq_ref[...]], axis=1)
+    gain_k = jnp.concatenate([gk_ref[...], jnp.ones_like(gk_ref[...])], axis=1)
+
     def finish(i, tiles):
         at = pl.ds(pl.multiple_of(i * chunk, chunk), chunk)
         cos, sin = cos_ref[at, :], sin_ref[at, :]
@@ -452,7 +455,7 @@
             x = raw_ref[at, lanes]
             query = tile < QW // LANES
             scale = lax.rsqrt(group_mean(x * x, ones_ref[...]) + EPSILON)
-            v = x * scale * (gq_ref[...] if query else gk_ref[...])
+            v = x * scale * (gain_q if query else gain_k)
             y = v * cos + half_turn(v, lane) * sin
             if query:
                 q_ref[at, lanes] = (y * (HD**-0.5 * LOG2E)).astype(BF)
@@ -770,12 +773,12 @@
         exchange(i).start()
         exchange(i).wait_recv()
         gains_ref[...] = landed[2 * i] + landed[2 * i + 1]
-    for c in range(o_pieces):
-        out_line.inward(c)
     sums.own(mine(0), attend_ref)
     for c in range(pieces):
         own_w[c] = attend_ref[c * piece : (c + 1) * piece, :].astype(BF)
         weights.launch(c)
+    for c in range(o_pieces):
+        out_line.inward(c)
     kw = KVH * HD
 
     def widen(c):
@@ -1616,8 +1619,8 @@
         output_weight,
         cos,
         sin,
-        gq,
-        gk,
+        query_gain[None],
+        key_gain[None],
         ones,
         out_grad.reshape(tokens, width),
     )
@@ -1675,7 +1678,7 @@
         d_flat,
         grad_output.reshape(n, -1, width),
     )
-    layer_out = middle.reshape(rows, span, width) + ffn_out
+    layer_out = middle + ffn_out.reshape(tokens, width)
     grad_joined_b, sum_q, sum_k = unproject(
         n,
         dq.reshape(tokens, QW),
@@ -1717,7 +1720,7 @@
     gain_key = gains[2 * width + LANES : 2 * width + LANES + HD]
     shape = (rows, span, width)
     return (
-        layer_out,
+        layer_out.reshape(shape),
         input_grad.reshape(shape),
         attend_total,
         output_total,

time: 693 us -> 691 us (level)
  no operation moved by 1% of the time
where the time goes in v7:
time: 691 us; the launch traced here: 686 us
  Pallas kernels  542 us (78%)
  waiting for transfers between devices  50.1 us (7%)
  other arithmetic  36.3 us (5%)
  local copies, waits for them, and re-layouts  29.7 us (4%)
  between operations  14.6 us (2%)
  matrix products  13.1 us (2%)
    pallas_call x1, Pallas kernels, spread(): pl.pallas_call(functools.partial(spread_kernel, n, m), grid=(rows, n), in...  105 us
    pallas_call x1, Pallas kernels, attend_back(): pl.pallas_call(functools.partial(attend_back_kernel, keys, n), grid=(rows...  103 us
    pallas_call x1, Pallas kernels, finish(): pl.pallas_call(functools.partial(finish_kernel, n, m), in_specs=[hbm, hbm...  102 us
    pallas_call x1, Pallas kernels, feed(): pl.pallas_call(functools.partial(feed_kernel, n), grid=(rows, pairs), in_...  89 us
    pallas_call x1, Pallas kernels, project(): pl.pallas_call(functools.partial(project_kernel, n), in_specs=[hbm, vmem,...  86.8 us
    all_gather x1, waiting for transfers between devices, shards(): lax.all_gather(grad_branch.reshape(rows, span, width), 'mp', axis=1, tile...  50 us
    pallas_call x1, Pallas kernels, unproject(): pl.pallas_call(functools.partial(unproject_kernel, n), in_specs=[hbm] * 3...  38.8 us
    pallas_call x1, Pallas kernels, attend(): pl.pallas_call(functools.partial(attend_kernel, keys), grid_spec=spec, ou...  16.6 us
  transfers between devices with their start and end apart: 2, of which 1 were waited for; matrix products, arithmetic and copies ran while one was open for 8% of the time, Pallas kernels for 38%

profile of v7, /device:TPU:0, one launch (start us, length us, event | category | flops | bytes accessed | tf_op | source)
XLA Modules:
  0.0 686.2 jit_solution(1029455172273698394)
XLA Ops:
  7.2 1.2 fusion.6
  9.1 0.9 fusion.5
  10.7 1.0 pad_maximum_fusion.w_ref
  11.7 1.8 multiply_sine_fusion
  13.5 86.8 %project.1 = (bf16[512,2048]{1,0:T(8,128)(2,1)}, f32[512,1920]{1,0:T(8,128)}, bf16[512,1280]{1,0:T(8,128)(2,1)}, bf16[512,2048]{1,0:T(8,128)(2,1)}, bf16[8,256,1...) custom-call(bf16[512,2048]{1,0:T(8,128)(2,1)} %bitcast.73, f32[1,2048]{1,0:T(1,128)} %bitcast.98, ...), custom_call_target="tpu_custom_call" | custom-call | tf_op jit(solution)/shard_map/project/pallas_call | solution.py:517
  102.3 16.6 %attend.1 = (bf16[2,256,1280]{2,1,0:T(8,128)(2,1)}, f32[2,256,1280]{2,1,0:T(8,128)}) custom-call(s32[2,3]{1,0:T(2,128)} %pad_add_fusion.info, bf16[2,256,1280]{2,1,0:T(8,128)(2,1)} %bitcast.90, bf16[2,2048,640]{2,1,0:T(8,128)(2,1)} %bitcast.79, s32[2,256,128]{2,1,0:T(8,128)} %broadcast_in_dim.80.start_ref), custom_call_target="tpu_custom_call" | custom-call | flops 21474836480 | bytes 10485760 | tf_op jit(solution)/shard_map/attend/pallas_call | solution.py:925
  119.0 4.5 multiply_reduce_fusion.1
  124.8 2.0 select_convert_fusion.ka_ref
  126.9 1.7 multiply_convert_fusion
  129.3 2.8 copy.33.dt_any
  132.1 8.6 %copy.34 = bf16[6,256,2048]{2,1,0:T(8,128)(2,1)} copy(bf16[6,256,2048]{1,2,0:T(8,128)(2,1)} %bitcast.76) | data formatting | bytes 12582912 | tf_op jit(solution)/shard_map/transpose | solution.py:1645
  140.7 50.0 %all-gather.2.cloned.1.call-done = bf16[2,2048,2048]{2,1,0:T(8,128)(2,1)} async-done(((bf16[2,256,2048]{2,1,0:T(8,128)(2,1)}), bf16[2,2048,2048]{2,1,0:T(8,128)(2,1)}) %all-gather.2.cloned.1.call-update) | async-done | bytes 16777232 | tf_op jit(solution)/shard_map/all_gather | solution.py:1630
  190.8 89.0 %feed.1 = (bf16[2,4,512,2048]{3,2,1,0:T(8,128)(2,1)}, bf16[2,4,512,768]{3,2,1,0:T(8,128)(2,1)}, bf16[2,4,512,1536]{3,2,1,0:T(8,128)(2,1)}, bf16[6,128,2048]{2,1,0:T(8,128)(2,1)}) custom-call(f32[6]{0:T(128)} %convert_element_type.61.live_ref, bf16[2,256,2048]{2,1,0:T(8,128)(2,1)} %bitcast.87, bf16[2,4,512,2048]{3,2,1,0:T(8,128)(2,1)} %bitcast.105, ...), custom_call_target="tpu_custom_call" | custom-call | flops 77309411328 | bytes 59768832 | tf_op jit(solution)/shard_map/feed/pallas_call | solution.py:1280
  279.8 105.1 %spread.1 = (f32[2,256,2048]{2,1,0:T(8,128)}, bf16[6,2048,256]{2,1,0:T(8,128)(2,1)}, bf16[12,64,2048]{2,1,0:T(8,128)(2,1)}) custom-call(bf16[2,8,256,1536]{3,2,1,0:T(8,128)(2,1)} %bitcast.66, bf16[1536,2048]{1,0:T(8,128)(2,1)} %bitcast.68, bf16[4096,2048]{1,0:T(8,128)(2,1)} %bitcast.69, bf16[4096,1536]{1,0:T(8,128)(2,1)} %bitcast.67, ...), custom_call_target="tpu_custom_call" | custom-call | flops 1 | bytes 1 | tf_op jit(solution)/shard_map/spread/pallas_call | solution.py:1516
  386.7 4.6 fusion.1
  392.2 1.6 copy-done.3
  393.8 3.5 multiply_add_fusion.mid_any
  397.4 4.7 convolution_convert_fusion
  402.1 4.0 convolution_convert_fusion.1
  406.1 103.2 %attend_back.1 = (f32[2,256,1280]{2,1,0:T(8,128)}, bf16[2,2048,640]{2,1,0:T(8,128)(2,1)}, f32[2,256,2048]{2,1,0:T(8,128)}, bf16[160,2048]{1,0:T(8,128)(2,1)}) custom-call(bf16[2,256,1280]{2,1,0:T(8,128)(2,1)} %bitcast.91, bf16[2,2048,640]{2,1,0:T(8,128)(2,1)} %bitcast.80, bf16[2,256,128]{2,1,0:T(8,128)(2,1)} %select_convert_fusion.1.qa_ref, ...), custom_call_target="tpu_custom_call" | custom-call | flops 1 | bytes 1 | tf_op jit(solution)/shard_map/attend_back/pallas_call | solution.py:1082
  509.3 38.8 %unproject.1 = (bf16[512,1920]{1,0:T(8,128)(2,1)}, f32[8,128]{1,0:T(8,128)}, f32[8,128]{1,0:T(8,128)}) custom-call(f32[512,1280]{1,0:T(8,128)} %bitcast.86, bf16[2,8,256,640]{3,2,1,0:T(8,128)(2,1)} %bitcast.78, f32[512,1920]{1,0:T(8,128)} %get-tuple-element.65.raw_any, f32[512,128]{1,0:T(8,128)} %get-tuple-element.95.cos_ref, ...), custom_call_target="tpu_custom_call" | custom-call | flops 1 | bytes 1 | tf_op jit(solution)/shard_map/unproject/pallas_call | solution.py:640
  548.1 4.0 bitcast_convert_fusion
  552.2 1.7 copy-done.7
  553.8 2.8 bitcast_add_fusion
  558.0 1.8 concatenate.15.sums_ref
  559.8 102.4 %finish.1 = (f32[512,2048]{1,0:T(8,128)}, f32[256,1920]{1,0:T(8,128)}, f32[160,2048]{1,0:T(8,128)}, f32[40,128]{1,0:T(8,128)}) custom-call(bf16[512,2048]{1,0:T(8,128)(2,1)} %get-tuple-element.70.normed_any, bf16[512,1920]{1,0:T(8,128)(2,1)} %get-tuple-element.71.gj_any, bf16[8,256,1920]{2,1,0:T(8,128)(2,1)} %get-tuple-element.72.w_any, ...), custom_call_target="tpu_custom_call" | custom-call | flops 1 | bytes 1 | tf_op jit(solution)/shard_map/finish/pallas_call | solution.py:822
  662.2 1.4 fusion.7
  663.6 1.3 slice_bitcast_fusion
  664.9 8.9 %convert_element_type.67 = f32[6,2048,256]{2,1,0:T(8,128)} convert(bf16[6,2048,256]{2,1,0:T(8,128)(2,1)} %all-reduce.3.cloned.1.call-done) | non-fusion elementwise | flops 3145728 | bytes 18874368 | tf_op jit(solution)/shard_map/convert_element_type | solution.py:1727
  673.8 2.1 copy.42
  676.8 1.3 copy.43
  678.0 1.1 copy.44
  (81 shorter events, 10.2 us)
Async XLA Ops:
  7.2 3.5 slice-start
  7.2 183.6 %all-gather.2.cloned.1.call-start = ((), (), s32[]{:S(2)}) async-start(), calls=%async_computation | async-start | bytes 18874368 | tf_op jit(solution)/shard_map/all_gather | solution.py:1630
  100.4 18.6 %slice-start.1 = ((s8[5242880]{0:T(1024)(128)(4,1)}), s8[1048576]{0:T(1024)(128)(4,1)S(1)}, s32[]{:S(2)}) async-start(s8[5242880]{0:T(1024)(128)(4,1)} %bitcast.107), calls=%async_computation.3 | async-start | bytes 2097152
  100.4 564.5 %all-reduce.3.cloned.1.call-start = ((), (), s32[]{:S(2)}) async-start(), calls=%async_computation.1 | async-start | bytes 12582912 | tf_op jit(solution)/shard_map/psum | solution.py:1655
  102.3 16.6 %copy-start.6 = (bf16[2,256,2048]{2,1,0:T(8,128)(2,1)S(1)}, bf16[2,256,2048]{2,1,0:T(8,128)(2,1)}, u32[]{:S(2)}) copy-start(bf16[2,256,2048]{2,1,0:T(8,128)(2,1)} %param.13) | copy-start | bytes 6291460
  102.3 16.6 %slice-start.2 = ((s8[5242880]{0:T(1024)(128)(4,1)}), s8[4194304]{0:T(1024)(128)(4,1)S(1)}, s32[]{:S(2)}) async-start(s8[5242880]{0:T(1024)(128)(4,1)} %bitcast.107), calls=%async_computation.4 | async-start | bytes 8388608
  119.0 4.5 copy-start.13
  119.0 7.9 %copy-start.14 = (f32[2048]{0:T(1024)S(1)}, f32[2048]{0:T(1024)}, u32[]{:S(2)}) copy-start(f32[2048]{0:T(1024)} %param.21) | copy-start | bytes 24580
  123.5 5.1 copy-start
  124.1 4.5 copy-start.17
  124.1 5.2 copy-start.5
  384.9 0.7 copy-start.15
  384.9 1.2 copy-start.16
  386.7 5.5 copy-start.1
  386.7 7.1 %copy-start.3 = (f32[2,256,2048]{2,1,0:T(8,128)S(1)}, f32[2,256,2048]{2,1,0:T(8,128)}, u32[]{:S(2)}) copy-start(f32[2,256,2048]{2,1,0:T(8,128)} %param.24) | copy-start | bytes 12582916
  393.8 3.6 copy-start.12
  393.8 8.2 %slice-start.3 = ((s8[5242880]{0:T(1024)(128)(4,1)}), s8[4194304]{0:T(1024)(128)(4,1)S(1)}, s32[]{:S(2)}) async-start(s8[5242880]{0:T(1024)(128)(4,1)} %bitcast.110), calls=%async_computation.5 | async-start | bytes 8388608
  397.4 4.7 copy-start.4
  397.4 4.7 slice-start.4
  509.2 38.8 %copy-start.9 = (bf16[12,64,2048]{2,1,0:T(8,128)(2,1)S(1)}, bf16[12,64,2048]{2,1,0:T(8,128)(2,1)}, u32[]{:S(2)}) copy-start(bf16[12,64,2048]{2,1,0:T(8,128)(2,1)} %get-tuple-element.68) | copy-start | bytes 9437188
  548.1 4.1 copy-start.2
  548.1 5.7 copy-start.7
  664.9 8.9 %copy-start.8 = (f32[512,2048]{1,0:T(8,128)S(1)}, f32[512,2048]{1,0:T(8,128)}, u32[]{:S(2)}) copy-start(f32[512,2048]{1,0:T(8,128)} %get-tuple-element.76) | copy-start | bytes 12582916
  673.8 3.0 copy-start.10
  673.8 4.2 copy-start.11
Sparse Core Ops, SparseCore 0:
  100.5 90.2 all-gather.1
  385.1 241.2 all-reduce.2

commit v8 on v7

--- a/solution.py
+++ b/solution.py
@@ -664,7 +664,7 @@
 
 
 def finish_kernel(
-    n, m, normed_any, gj_any, w_any, x_any, mid_any, gain_ref, share_any, sums_ref,
+    n, m, normed_any, gj_any, w_any, x_any, mid_any, gain_ref, share_any, feed_ref, sq_ref, sk_ref,
     grad_any, attend_ref, out_ref, gains_ref,
     normed_ref, gj_ref, x_ref, grad_ref,
     w_ref, term, error, mid_ref, own_w, up_w, across_w, own_o, up_o, across_o, landed,
@@ -700,7 +700,11 @@
     at = lambda ref: lambda c: ref.at[c]
     weights = Line(m, line, at(own_w), at(up_w), at(across_w), at(up_w), sem_w)
     out_line = Line(m, line, at(own_o), at(up_o), at(across_o), at(up_o), sem_o)
-    gains_ref[...] = sums_ref[...]
+    tiles = width // LANES
+    gains_ref[...] = jnp.zeros_like(gains_ref)
+    gains_ref[tiles : 2 * tiles, :] = feed_ref[...]
+    gains_ref[2 * tiles : 2 * tiles + 1, :] = sq_ref[:1, :]
+    gains_ref[2 * tiles + 1 : 2 * tiles + 2, :] = sk_ref[:1, :]
 
     def tokens_part(i):
         here = pl.ds(pl.multiple_of(i * chunk, chunk), chunk)
@@ -809,7 +813,7 @@
     sums.drain(mine(0))
 
 
-def finish(n, m, normed, gj, w, x, middle, gain, share, sums):
+def finish(n, m, normed, gj, w, x, middle, gain, share, gain_feed, sum_q, sum_k):
     tokens, width = x.shape
     columns = gj.shape[1]
     depth = width // n
@@ -821,7 +825,7 @@
     steps = n.bit_length() + m.bit_length() - 2
     return pl.pallas_call(
         functools.partial(finish_kernel, n, m),
-        in_specs=[hbm, hbm, hbm, hbm, hbm, vmem, hbm, vmem],
+        in_specs=[hbm, hbm, hbm, hbm, hbm, vmem, hbm, vmem, vmem, vmem],
         out_specs=[hbm, vmem, vmem, vmem],
         out_shape=[
             jax.ShapeDtypeStruct((tokens, width), F32),
@@ -852,7 +856,7 @@
         compiler_params=params(mib=60, axes=0, key=5),
         cost_estimate=TINY,
         name="finish",
-    )(normed, gj, w, x, middle, gain, share.reshape(split), sums)
+    )(normed, gj, w, x, middle, gain, share.reshape(split), gain_feed, sum_q, sum_k)
 
 
 def key_positions(shape, axis, group, per, span):
@@ -1447,10 +1451,14 @@
     @pl.when(now == 0)
     def _():
         bring.start()
-        sums.start(lambda n, me: greet_all(n, me, m, line))
-        bring.wait()
-        for c in range(chunks):
-            down.launch(c)
+
+        def meet(n, me):
+            greet_all(n, me, m, line)
+            bring.wait()
+            for c in range(chunks):
+                down.launch(c)
+
+        sums.start(meet)
 
     sums.step(now, a_ref.at[0, 0])
     for c in range(chunks):
@@ -1694,15 +1702,6 @@
     grad_joined_b, layer_out, down_total = lax.optimization_barrier(
         (grad_joined_b, layer_out, down_total)
     )
-    sums = jnp.concatenate(
-        [
-            jnp.zeros((width // LANES, LANES), F32),
-            gain_feed.reshape(-1, LANES),
-            sum_q[:1],
-            sum_k[:1],
-            jnp.zeros((GAIN_ROWS - 2 * (width // LANES) - 2, LANES), F32),
-        ]
-    )
     input_grad, attend_total, output_total, gains = finish(
         n,
         m,
@@ -1713,7 +1712,9 @@
         grad_middle,
         attention_gain[None],
         output_share,
-        sums,
+        gain_feed.reshape(-1, LANES),
+        sum_q,
+        sum_k,
     )
     gains = gains.reshape(-1)
     gain_query = gains[2 * width : 2 * width + HD] + gains[2 * width + HD : 2 * width + 2 * HD]

time: 691 us -> 690 us (level)
  transfers between devices with their start and end apart: 2 -> 2, of which waited for: 1 -> 1; matrix products, arithmetic and copies ran while one was open for 8% -> 8% of each run, Pallas kernels for 38% -> 39%
where the time goes in v8:
time: 690 us; the launch traced here: 685 us
  Pallas kernels  544 us (79%)
  waiting for transfers between devices  50.1 us (7%)
  other arithmetic  37.4 us (5%)
  local copies, waits for them, and re-layouts  25.5 us (4%)
  between operations  14.6 us (2%)
  matrix products  13.1 us (2%)
    pallas_call x1, Pallas kernels, finish(): pl.pallas_call(functools.partial(finish_kernel, n, m), in_specs=[hbm, hbm...  105 us
    pallas_call x1, Pallas kernels, spread(): pl.pallas_call(functools.partial(spread_kernel, n, m), grid=(rows, n), in...  104 us
    pallas_call x1, Pallas kernels, attend_back(): pl.pallas_call(functools.partial(attend_back_kernel, keys, n), grid=(rows...  103 us
    pallas_call x1, Pallas kernels, feed(): pl.pallas_call(functools.partial(feed_kernel, n), grid=(rows, pairs), in_...  89 us
    pallas_call x1, Pallas kernels, project(): pl.pallas_call(functools.partial(project_kernel, n), in_specs=[hbm, vmem,...  86.8 us
    all_gather x1, waiting for transfers between devices, shards(): lax.all_gather(grad_branch.reshape(rows, span, width), 'mp', axis=1, tile...  50.1 us
    pallas_call x1, Pallas kernels, unproject(): pl.pallas_call(functools.partial(unproject_kernel, n), in_specs=[hbm] * 3...  39 us
    pallas_call x1, Pallas kernels, attend(): pl.pallas_call(functools.partial(attend_kernel, keys), grid_spec=spec, ou...  16.6 us
  transfers between devices with their start and end apart: 2, of which 1 were waited for; matrix products, arithmetic and copies ran while one was open for 8% of the time, Pallas kernels for 39%

profile of v8, /device:TPU:0, one launch (start us, length us, event | category | flops | bytes accessed | tf_op | source)
XLA Modules:
  0.0 684.8 jit_solution(18182794598906635394)
XLA Ops:
  7.2 1.2 fusion.6
  9.1 0.9 fusion.5
  10.7 1.0 pad_maximum_fusion.w_ref
  11.7 1.8 multiply_sine_fusion
  13.5 86.8 %project.1 = (bf16[512,2048]{1,0:T(8,128)(2,1)}, f32[512,1920]{1,0:T(8,128)}, bf16[512,1280]{1,0:T(8,128)(2,1)}, bf16[512,2048]{1,0:T(8,128)(2,1)}, bf16[8,256,1...) custom-call(bf16[512,2048]{1,0:T(8,128)(2,1)} %bitcast.73, f32[1,2048]{1,0:T(1,128)} %bitcast.98, ...), custom_call_target="tpu_custom_call" | custom-call | tf_op jit(solution)/shard_map/project/pallas_call | solution.py:517
  101.5 0.8 broadcast_in_dim.74.start_ref
  102.3 16.6 %attend.1 = (bf16[2,256,1280]{2,1,0:T(8,128)(2,1)}, f32[2,256,1280]{2,1,0:T(8,128)}) custom-call(s32[2,3]{1,0:T(2,128)} %pad_add_fusion.info, bf16[2,256,1280]{2,1,0:T(8,128)(2,1)} %bitcast.90, bf16[2,2048,640]{2,1,0:T(8,128)(2,1)} %bitcast.79, s32[2,256,128]{2,1,0:T(8,128)} %broadcast_in_dim.74.start_ref), custom_call_target="tpu_custom_call" | custom-call | flops 21474836480 | bytes 10485760 | tf_op jit(solution)/shard_map/attend/pallas_call | solution.py:929
  119.0 4.5 multiply_reduce_fusion.1
  124.8 2.0 select_convert_fusion.ka_ref
  126.9 1.7 multiply_convert_fusion
  129.3 2.8 copy.33.dt_any
  132.1 8.6 %copy.34 = bf16[6,256,2048]{2,1,0:T(8,128)(2,1)} copy(bf16[6,256,2048]{1,2,0:T(8,128)(2,1)} %bitcast.76) | data formatting | bytes 12582912 | tf_op jit(solution)/shard_map/transpose | solution.py:1653
  140.7 50.1 %all-gather.2.cloned.1.call-done = bf16[2,2048,2048]{2,1,0:T(8,128)(2,1)} async-done(((bf16[2,256,2048]{2,1,0:T(8,128)(2,1)}), bf16[2,2048,2048]{2,1,0:T(8,128)(2,1)}) %all-gather.2.cloned.1.call-update) | async-done | bytes 16777232 | tf_op jit(solution)/shard_map/all_gather | solution.py:1638
  190.8 89.0 %feed.1 = (bf16[2,4,512,2048]{3,2,1,0:T(8,128)(2,1)}, bf16[2,4,512,768]{3,2,1,0:T(8,128)(2,1)}, bf16[2,4,512,1536]{3,2,1,0:T(8,128)(2,1)}, bf16[6,128,2048]{2,1,0:T(8,128)(2,1)}) custom-call(f32[6]{0:T(128)} %convert_element_type.61.live_ref, bf16[2,256,2048]{2,1,0:T(8,128)(2,1)} %bitcast.87, bf16[2,4,512,2048]{3,2,1,0:T(8,128)(2,1)} %bitcast.105, ...), custom_call_target="tpu_custom_call" | custom-call | flops 77309411328 | bytes 59768832 | tf_op jit(solution)/shard_map/feed/pallas_call | solution.py:1284
  279.8 104.1 %spread.1 = (f32[2,256,2048]{2,1,0:T(8,128)}, bf16[6,2048,256]{2,1,0:T(8,128)(2,1)}, bf16[12,64,2048]{2,1,0:T(8,128)(2,1)}) custom-call(bf16[2,8,256,1536]{3,2,1,0:T(8,128)(2,1)} %bitcast.66, bf16[1536,2048]{1,0:T(8,128)(2,1)} %bitcast.68, bf16[4096,2048]{1,0:T(8,128)(2,1)} %bitcast.69, bf16[4096,1536]{1,0:T(8,128)(2,1)} %bitcast.67, ...), custom_call_target="tpu_custom_call" | custom-call | flops 1 | bytes 1 | tf_op jit(solution)/shard_map/spread/pallas_call | solution.py:1524
  385.6 5.7 fusion.1
  391.5 1.3 copy-done.4
  392.7 3.5 multiply_add_fusion.mid_any
  396.3 4.7 convolution_convert_fusion
  401.0 4.0 convolution_convert_fusion.1
  405.0 103.2 %attend_back.1 = (f32[2,256,1280]{2,1,0:T(8,128)}, bf16[2,2048,640]{2,1,0:T(8,128)(2,1)}, f32[2,256,2048]{2,1,0:T(8,128)}, bf16[160,2048]{1,0:T(8,128)(2,1)}) custom-call(bf16[2,256,1280]{2,1,0:T(8,128)(2,1)} %bitcast.91, bf16[2,2048,640]{2,1,0:T(8,128)(2,1)} %bitcast.80, bf16[2,256,128]{2,1,0:T(8,128)(2,1)} %select_convert_fusion.1.qa_ref, ...), custom_call_target="tpu_custom_call" | custom-call | flops 1 | bytes 1 | tf_op jit(solution)/shard_map/attend_back/pallas_call | solution.py:1086
  508.2 39.0 %unproject.1 = (bf16[512,1920]{1,0:T(8,128)(2,1)}, f32[8,128]{1,0:T(8,128)}, f32[8,128]{1,0:T(8,128)}) custom-call(f32[512,1280]{1,0:T(8,128)} %bitcast.86, bf16[2,8,256,640]{3,2,1,0:T(8,128)(2,1)} %bitcast.78, f32[512,1920]{1,0:T(8,128)} %get-tuple-element.65.raw_any, f32[512,128]{1,0:T(8,128)} %get-tuple-element.95.cos_ref, ...), custom_call_target="tpu_custom_call" | custom-call | flops 1 | bytes 1 | tf_op jit(solution)/shard_map/unproject/pallas_call | solution.py:640
  547.2 4.0 bitcast_convert_fusion
  551.3 1.7 copy-done.7
  553.0 2.8 bitcast_add_fusion
  555.8 105.0 %finish.1 = (f32[512,2048]{1,0:T(8,128)}, f32[256,1920]{1,0:T(8,128)}, f32[160,2048]{1,0:T(8,128)}, f32[40,128]{1,0:T(8,128)}) custom-call(bf16[512,2048]{1,0:T(8,128)(2,1)} %get-tuple-element.70.normed_any, bf16[512,1920]{1,0:T(8,128)(2,1)} %get-tuple-element.71.gj_any, bf16[8,256,1920]{2,1,0:T(8,128)(2,1)} %get-tuple-element.72.w_any, ...), custom_call_target="tpu_custom_call" | custom-call | flops 1 | bytes 1 | tf_op jit(solution)/shard_map/finish/pallas_call | solution.py:826
  660.8 1.4 fusion.7
  662.2 1.3 slice_bitcast_fusion
  663.5 8.9 %convert_element_type.67 = f32[6,2048,256]{2,1,0:T(8,128)} convert(bf16[6,2048,256]{2,1,0:T(8,128)(2,1)} %all-reduce.3.cloned.1.call-done) | non-fusion elementwise | flops 3145728 | bytes 18874368 | tf_op jit(solution)/shard_map/convert_element_type | solution.py:1728
  672.4 2.1 copy.42
  675.4 1.3 copy.43
  676.6 1.1 copy.44
  (76 shorter events, 7.2 us)
Async XLA Ops:
  7.2 3.5 slice-start
  7.2 183.6 %all-gather.2.cloned.1.call-start = ((), (), s32[]{:S(2)}) async-start(), calls=%async_computation | async-start | bytes 18874368 | tf_op jit(solution)/shard_map/all_gather | solution.py:1638
  100.4 18.6 %slice-start.1 = ((s8[5242880]{0:T(1024)(128)(4,1)}), s8[1048576]{0:T(1024)(128)(4,1)S(1)}, s32[]{:S(2)}) async-start(s8[5242880]{0:T(1024)(128)(4,1)} %bitcast.107), calls=%async_computation.3 | async-start | bytes 2097152
  100.4 563.1 %all-reduce.3.cloned.1.call-start = ((), (), s32[]{:S(2)}) async-start(), calls=%async_computation.1 | async-start | bytes 12582912 | tf_op jit(solution)/shard_map/psum | solution.py:1663
  102.3 16.6 %copy-start.6 = (bf16[2,256,2048]{2,1,0:T(8,128)(2,1)S(1)}, bf16[2,256,2048]{2,1,0:T(8,128)(2,1)}, u32[]{:S(2)}) copy-start(bf16[2,256,2048]{2,1,0:T(8,128)(2,1)} %param.13) | copy-start | bytes 6291460
  102.3 16.6 %slice-start.2 = ((s8[5242880]{0:T(1024)(128)(4,1)}), s8[4194304]{0:T(1024)(128)(4,1)S(1)}, s32[]{:S(2)}) async-start(s8[5242880]{0:T(1024)(128)(4,1)} %bitcast.107), calls=%async_computation.4 | async-start | bytes 8388608
  119.0 4.5 copy-start.13
  119.0 7.9 %copy-start.14 = (f32[2048]{0:T(1024)S(1)}, f32[2048]{0:T(1024)}, u32[]{:S(2)}) copy-start(f32[2048]{0:T(1024)} %param.21) | copy-start | bytes 24580
  123.5 5.1 copy-start
  124.1 4.5 copy-start.17
  124.1 5.2 copy-start.5
  383.9 0.7 copy-start.15
  383.9 1.2 copy-start.16
  385.6 5.8 copy-start.1
  385.6 7.1 %copy-start.4 = (f32[2,256,2048]{2,1,0:T(8,128)S(1)}, f32[2,256,2048]{2,1,0:T(8,128)}, u32[]{:S(2)}) copy-start(f32[2,256,2048]{2,1,0:T(8,128)} %param.24) | copy-start | bytes 12582916
  392.7 3.6 copy-start.12
  392.7 8.2 %slice-start.3 = ((s8[5242880]{0:T(1024)(128)(4,1)}), s8[4194304]{0:T(1024)(128)(4,1)S(1)}, s32[]{:S(2)}) async-start(s8[5242880]{0:T(1024)(128)(4,1)} %bitcast.110), calls=%async_computation.5 | async-start | bytes 8388608
  396.3 4.7 copy-start.3
  396.3 4.7 slice-start.4
  508.2 39.0 %copy-start.9 = (bf16[12,64,2048]{2,1,0:T(8,128)(2,1)S(1)}, bf16[12,64,2048]{2,1,0:T(8,128)(2,1)}, u32[]{:S(2)}) copy-start(bf16[12,64,2048]{2,1,0:T(8,128)(2,1)} %get-tuple-element.68) | copy-start | bytes 9437188
  547.2 4.1 copy-start.2
  547.2 5.8 copy-start.7
  663.5 8.9 %copy-start.8 = (f32[512,2048]{1,0:T(8,128)S(1)}, f32[512,2048]{1,0:T(8,128)}, u32[]{:S(2)}) copy-start(f32[512,2048]{1,0:T(8,128)} %get-tuple-element.76) | copy-start | bytes 12582916
  672.4 3.0 copy-start.10
  672.4 4.2 copy-start.11
Sparse Core Ops, SparseCore 0:
  100.5 90.2 all-gather.1
  384.0 240.5 all-reduce.2
